TPU v7x, 32 devices: a whole 2x2x4 slice. The times are simulated.
32 devices in a mesh: row: 4 (over z), col: 8 (over y, x, core).
Axes of the slice: x: 2, y: 2, z: 4, core: 2. Of those that a mesh axis runs over, the one named last changes fastest.
Arguments:
- tokens: bfloat16 [10240, 2048], P('row', 'col'), may hold values from -6 to 6
- attn_norm: float32 [2048], replicated, may hold values from 0.5 to 1.5
- w_query: bfloat16 [2048, 2048], P('row', 'col'), may hold values from -0.125 to 0.125
- w_key: bfloat16 [2048, 2048], P('row', 'col'), may hold values from -0.125 to 0.125
- w_value: bfloat16 [2048, 2048], P('row', 'col'), may hold values from -0.125 to 0.125
- q_norm: float32 [2048], replicated, may hold values from 0.5 to 1.5
- k_norm: float32 [2048], replicated, may hold values from 0.5 to 1.5
- w_out: bfloat16 [2048, 2048], P('row', 'col'), may hold values from -1 to 1
- moe_norm: float32 [2048], replicated, may hold values from 0.5 to 1.5
- w_gate: bfloat16 [2048, 65536], P('row', 'col'), may hold values from -0.125 to 0.125
- w_up: bfloat16 [2048, 65536], P('row', 'col'), may hold values from -0.125 to 0.125
- w_down: bfloat16 [2048, 65536], P('row', 'col'), may hold values from -0.1875 to 0.1875
- routes: int32 [10240, 8], P('row'), may hold values from 0 to 63, all different within a row; in each aligned block of 2560 rows (0 to 2559, 2560 to 5119, ...) at most 426 rows name the same one
- gates: float32 [10240, 8], P('row'), may hold values from 0.2 to 0.6
- parents: int32 [4, 20], P('row'), may hold values from -1 to 7, as said below
- cotangent: bfloat16 [10240, 2048], P('row', 'col'), may hold values from -6 to 6
Outputs:
- output: bfloat16 [10240, 2048], P('row', 'col')
- tokens_grad: float32 [10240, 2048], P('row', 'col')
- attn_norm_grad: float32 [2048], P('col')
- w_query_grad: float32 [2048, 2048], P('row', 'col')
- w_key_grad: float32 [2048, 2048], P('row', 'col')
- w_value_grad: float32 [2048, 2048], P('row', 'col')
- q_norm_grad: float32 [2048], P('col')
- k_norm_grad: float32 [2048], P('col')
- w_out_grad: float32 [2048, 2048], P('row', 'col')
- moe_norm_grad: float32 [2048], P('col')
- w_gate_grad: float32 [2048, 65536], P('row', 'col')
- w_up_grad: float32 [2048, 65536], P('row', 'col')
- w_down_grad: float32 [2048, 65536], P('row', 'col')
Inputs may be any that keep to these rules, and one draw needn't show every extreme that they name: `routes`: each row names 8 different experts; within each aligned block of 2560 rows no expert is named by more than 426 rows, a bound that some block reaches. `parents`: in every tree, segments 0 to 3 form a chain (segment 0 has parent -1, each next one the one before); the next 4 segments have the trunk's last segment as parent; the next 8 segments each have one of those branch segments as parent, 2 leaves to every branch; the last 4 segments have parent -1.
All inputs are finite; a program needn't handle non-finite values.
Results may differ from a plain program's by a relative error of at most 0.018.
Values may be sent and summed in bfloat16 or wider, within the bound.
No kernel may reach another device: no remote copies, remote signals or barrier semaphores. Data moves between devices by JAX's collectives and lax.ppermute only.
A program may use at most 512 MiB of HBM per device.

v0:
```python
import math

import jax
import jax.numpy as jnp
from jax import lax
from jax.sharding import PartitionSpec as P

HD = 128
FF = 1024
SEG = 128
TREE = 2560
NSEG = 20
CAP = 426
QB = 512


EPS = 1e-05
NEGATIVE = -1e30


def ancestry(parent_ids):
    segment_ids = jnp.arange(NSEG, dtype=jnp.int32)

    def advance(turn_index, loop_state):
        current, reached = loop_state
        matches = current[:, None] == segment_ids[None, :]
        reached = reached + matches.astype(jnp.int32)
        parent_of = jnp.sum(jnp.where(matches, parent_ids[None, :], 0), 1)
        current = jnp.where(current >= 0, parent_of, -1)
        return (current, reached)

    start_state = (segment_ids, jnp.zeros((NSEG, NSEG), jnp.int32))
    return lax.fori_loop(0, NSEG, advance, start_state)[1]


def block_mask(ancestors, begin):
    segment_ids = jnp.arange(NSEG, dtype=jnp.int32)
    query_pos = begin + jnp.arange(QB, dtype=jnp.int32)
    key_pos = jnp.arange(TREE, dtype=jnp.int32)
    picks = (query_pos[:, None] // SEG == segment_ids[None, :]).astype(jnp.float32)
    visible = jnp.dot(picks, ancestors.astype(jnp.float32))
    visible = jnp.repeat(visible, SEG, axis=1) > 0.5
    same_seg = query_pos[:, None] // SEG == key_pos[None, :] // SEG
    return visible & (jnp.logical_not(same_seg) | (key_pos[None, :] <= query_pos[:, None]))


def rope_tables(ancestors):
    depths = jnp.sum(ancestors, 1) - 1
    position = jnp.arange(TREE, dtype=jnp.int32)
    places = (jnp.repeat(depths, SEG) * SEG + position % SEG).astype(jnp.float32)
    frequency = jnp.exp(jnp.arange(HD // 2, dtype=jnp.float32) * (-2.0 * math.log(10000.0) / HD))
    angles = places[:, None] * frequency[None, :]
    return (jnp.cos(angles), jnp.sin(angles))


def rotate(field, cos_table, sin_table):
    half_width = field.shape[-1] // 2
    first_half = field[..., :half_width]
    second_half = field[..., half_width:]
    cosine = cos_table[:, None, :]
    sine_part = sin_table[:, None, :]
    return jnp.concatenate(
        [
            first_half * cosine - second_half * sine_part,
            second_half * cosine + first_half * sine_part,
        ],
        -1,
    )


def unrotate(field, cos_table, sin_table):
    half_width = field.shape[-1] // 2
    first_half = field[..., :half_width]
    second_half = field[..., half_width:]
    cosine = cos_table[:, None, :]
    sine_part = sin_table[:, None, :]
    return jnp.concatenate(
        [
            first_half * cosine + second_half * sine_part,
            second_half * cosine - first_half * sine_part,
        ],
        -1,
    )


def dispatch(route_rows, gate_rows, first_expert, expert_count):
    pair_count = route_rows.shape[0] * route_rows.shape[1]
    local_ids = route_rows.reshape(-1) - first_expert
    expert_ids = jnp.arange(expert_count, dtype=jnp.int32)
    onehot = (local_ids[:, None] == expert_ids[None, :]).astype(jnp.int32)
    rank_in = jnp.cumsum(onehot, 0) - 1
    slot_index = jnp.sum(onehot * (rank_in + expert_ids[None, :] * CAP), 1)
    is_local = jnp.sum(onehot, 1) > 0
    slot_index = jnp.where(is_local, slot_index, expert_count * CAP)
    token_index = jnp.arange(pair_count, dtype=jnp.int32) // route_rows.shape[1]
    slot_token = (
        jnp.full((expert_count * CAP + 1,), route_rows.shape[0], jnp.int32)
        .at[slot_index]
        .set(token_index)[: expert_count * CAP]
    )
    slot_gate = (
        jnp.zeros((expert_count * CAP + 1,), jnp.float32)
        .at[slot_index]
        .set(gate_rows.reshape(-1))[: expert_count * CAP]
    )
    return (slot_token, slot_gate)


def gather_features(part_rows):
    return lax.all_gather(part_rows, "col", axis=1, tiled=True)


def head_total(partial_value):
    return lax.psum_scatter(partial_value, "col", scatter_dimension=1, tiled=True)


def across_heads(stacked):
    return lax.psum(stacked, "col")


def expert_total(slot_terms, slot_token, tok_rows):
    flat = slot_terms.reshape(-1, slot_terms.shape[-1])
    summed = jnp.zeros((tok_rows + 1, flat.shape[1]), jnp.float32).at[slot_token].add(flat)
    return head_total(summed[:tok_rows])


def contract_rows(left, right):
    return lax.dot_general(
        left, right, (((0,), (0,)), ((), ())), preferred_element_type=jnp.float32
    )


def contract_cols(left, right):
    return lax.dot_general(
        left, right, (((1,), (1,)), ((), ())), preferred_element_type=jnp.float32
    )


def attend_tree(parts):
    query_t, key_t, value_t, ancestors = parts
    scale_factor = 1.0 / math.sqrt(HD)

    def attend_one_block(begin):
        query_block = lax.dynamic_slice_in_dim(query_t, begin, QB, 0)
        scores = (
            jnp.einsum("qhd,khd->hqk", query_block, key_t, preferred_element_type=jnp.float32)
            * scale_factor
        )
        scores = jnp.where(block_mask(ancestors, begin)[None], scores, NEGATIVE)
        highest = jnp.max(scores, -1, keepdims=True)
        raised = jnp.exp(scores - highest)
        summed = jnp.sum(raised, -1, keepdims=True)
        weights = (raised / summed).astype(jnp.bfloat16)
        mixed = jnp.einsum("hqk,khd->qhd", weights, value_t, preferred_element_type=jnp.float32)
        return (mixed.astype(jnp.bfloat16), (highest + jnp.log(summed))[..., 0])

    return lax.map(attend_one_block, jnp.arange(TREE // QB, dtype=jnp.int32) * QB)


def tree_grads(parts):
    query_t, key_t, value_t, grad_t, log_totals, ancestors = parts
    scale_factor = 1.0 / math.sqrt(HD)

    def tree_one_block(running, inputs):
        key_acc, value_acc = running
        begin, log_block = inputs
        query_block = lax.dynamic_slice_in_dim(query_t, begin, QB, 0)
        grad_block = lax.dynamic_slice_in_dim(grad_t, begin, QB, 0)
        scores = (
            jnp.einsum("qhd,khd->hqk", query_block, key_t, preferred_element_type=jnp.float32)
            * scale_factor
        )
        scores = jnp.where(block_mask(ancestors, begin)[None], scores, NEGATIVE)
        weights = jnp.exp(scores - log_block[..., None])
        weights_low = weights.astype(jnp.bfloat16)
        d_weights = jnp.einsum(
            "qhd,khd->hqk", grad_block, value_t, preferred_element_type=jnp.float32
        )
        row_dot = jnp.sum(weights * d_weights, -1, keepdims=True)
        d_scores = (weights * (d_weights - row_dot)).astype(jnp.bfloat16)
        d_query = (
            jnp.einsum("hqk,khd->qhd", d_scores, key_t, preferred_element_type=jnp.float32)
            * scale_factor
        )
        key_acc = (
            key_acc
            + jnp.einsum("hqk,qhd->khd", d_scores, query_block, preferred_element_type=jnp.float32)
            * scale_factor
        )
        value_acc = value_acc + jnp.einsum(
            "hqk,qhd->khd", weights_low, grad_block, preferred_element_type=jnp.float32
        )
        return ((key_acc, value_acc), d_query)

    empty_acc = jnp.zeros(key_t.shape, jnp.float32)
    begins = jnp.arange(TREE // QB, dtype=jnp.int32) * QB
    (d_key, d_value), d_query = lax.scan(
        tree_one_block, (empty_acc, empty_acc), (begins, log_totals)
    )
    return (d_query.reshape(key_t.shape), d_key, d_value)


def body(
    tokens,
    attn_norm,
    w_query,
    w_key,
    w_value,
    q_norm,
    k_norm,
    w_out,
    moe_norm,
    w_gate,
    w_up,
    w_down,
    routes,
    gates,
    parents,
    cotangent,
):
    tok_rows, own_width = tokens.shape
    width = own_width * lax.axis_size("col")
    col_start = lax.axis_index("col") * own_width
    tree_count = parents.shape[0]
    heads_here = own_width // HD
    experts_here = w_gate.shape[1] // FF
    first_expert = lax.axis_index("col") * experts_here
    tree_shape = (tree_count, TREE, heads_here, HD)
    ancestors = jax.vmap(ancestry)(parents)
    cos_table, sin_table = jax.vmap(rope_tables)(ancestors)
    whole = gather_features(tokens)
    wide = whole.astype(jnp.float32)
    scale_one = lax.rsqrt(jnp.mean(wide * wide, 1, keepdims=True) + EPS)
    normed_one = (wide * scale_one * attn_norm[None, :]).astype(jnp.bfloat16)
    query_cols, key_cols, value_cols, out_cols = (
        lax.all_gather(w_query, "row", axis=0, tiled=True),
        lax.all_gather(w_key, "row", axis=0, tiled=True),
        lax.all_gather(w_value, "row", axis=0, tiled=True),
        lax.all_gather(w_out, "row", axis=0, tiled=True),
    )
    query = jnp.dot(normed_one, query_cols, preferred_element_type=jnp.float32)
    keyed = jnp.dot(normed_one, key_cols, preferred_element_type=jnp.float32)
    values_low = jnp.dot(normed_one, value_cols, preferred_element_type=jnp.float32).astype(
        jnp.bfloat16
    )
    squares = across_heads(jnp.stack([jnp.sum(query * query, 1), jnp.sum(keyed * keyed, 1)]))
    q_scale = lax.rsqrt(squares[0] / width + EPS)[:, None]
    k_scale = lax.rsqrt(squares[1] / width + EPS)[:, None]
    q_gain = lax.dynamic_slice_in_dim(q_norm, col_start, own_width)
    k_gain = lax.dynamic_slice_in_dim(k_norm, col_start, own_width)
    q_rot = jax.vmap(rotate)(
        (query * q_scale * q_gain).reshape(tree_shape), cos_table, sin_table
    ).astype(jnp.bfloat16)
    k_rot = jax.vmap(rotate)(
        (keyed * k_scale * k_gain).reshape(tree_shape), cos_table, sin_table
    ).astype(jnp.bfloat16)
    value_trees = values_low.reshape(tree_shape)
    attended, log_totals = lax.map(attend_tree, (q_rot, k_rot, value_trees, ancestors))
    attended = attended.reshape(tok_rows, own_width)
    attn_sum = head_total(contract_cols(attended, out_cols))
    residual = tokens.astype(jnp.float32) + attn_sum
    mid_low = residual.astype(jnp.bfloat16)
    mid_wide = gather_features(mid_low).astype(jnp.float32)
    scale_two = lax.rsqrt(jnp.mean(mid_wide * mid_wide, 1, keepdims=True) + EPS)
    normed_two = (mid_wide * scale_two * moe_norm[None, :]).astype(jnp.bfloat16)
    gate_cols, up_cols, down_cols = (
        lax.all_gather(w_gate, "row", axis=0, tiled=True),
        lax.all_gather(w_up, "row", axis=0, tiled=True),
        lax.all_gather(w_down, "row", axis=0, tiled=True),
    )
    expert_shape = (width, experts_here, FF)
    slot_token, slot_gate = dispatch(routes, gates, first_expert, experts_here)
    padded = jnp.concatenate([normed_two, jnp.zeros((1, width), jnp.bfloat16)], 0)
    expert_in = padded[slot_token].reshape(experts_here, CAP, width)
    gate_act = jnp.einsum(
        "ecd,def->ecf",
        expert_in,
        gate_cols.reshape(expert_shape),
        preferred_element_type=jnp.float32,
    )
    up_act = jnp.einsum(
        "ecd,def->ecf", expert_in, up_cols.reshape(expert_shape), preferred_element_type=jnp.float32
    )
    sigmoid_gate = jax.nn.sigmoid(gate_act)
    silu_gate = gate_act * sigmoid_gate
    hidden_low = (silu_gate * up_act).astype(jnp.bfloat16)
    expert_out = jnp.einsum(
        "ecf,def->ecd",
        hidden_low,
        down_cols.reshape(expert_shape),
        preferred_element_type=jnp.float32,
    )
    gated_out = slot_gate[:, None] * expert_out.reshape(-1, width)
    moe_sum = expert_total(gated_out, slot_token, tok_rows)
    output = (residual + moe_sum).astype(jnp.bfloat16)
    grad_whole = gather_features(cotangent)
    grad_pad = jnp.concatenate([grad_whole, jnp.zeros((1, width), jnp.bfloat16)], 0)
    d_out_low = (
        (slot_gate[:, None] * grad_pad[slot_token].astype(jnp.float32))
        .astype(jnp.bfloat16)
        .reshape(experts_here, CAP, width)
    )
    d_hidden = jnp.einsum(
        "ecd,def->ecf",
        d_out_low,
        down_cols.reshape(expert_shape),
        preferred_element_type=jnp.float32,
    )
    d_gate_low = (
        d_hidden * up_act * sigmoid_gate * (1.0 + gate_act * (1.0 - sigmoid_gate))
    ).astype(jnp.bfloat16)
    d_up_low = (d_hidden * silu_gate).astype(jnp.bfloat16)
    d_expert_in = jnp.einsum(
        "ecf,def->ecd",
        d_gate_low,
        gate_cols.reshape(expert_shape),
        preferred_element_type=jnp.float32,
    )
    d_expert_in = d_expert_in + jnp.einsum(
        "ecf,def->ecd", d_up_low, up_cols.reshape(expert_shape), preferred_element_type=jnp.float32
    )
    d_normed_two = expert_total(d_expert_in, slot_token, tok_rows)
    moved_in, moved_out = (
        lax.all_to_all(expert_in, "row", split_axis=2, concat_axis=1, tiled=True),
        lax.all_to_all(d_out_low, "row", split_axis=2, concat_axis=1, tiled=True),
    )
    slice_rows = moved_in.shape[2]
    gate_piece = lax.all_gather(d_gate_low, "row", axis=1, tiled=True)
    up_piece = lax.all_gather(d_up_low, "row", axis=1, tiled=True)
    hidden_piece = lax.all_gather(hidden_low, "row", axis=1, tiled=True)
    grad_part = moved_out
    gate_total = jnp.einsum(
        "ecd,ecf->def", moved_in, gate_piece, preferred_element_type=jnp.float32
    )
    up_total = jnp.einsum("ecd,ecf->def", moved_in, up_piece, preferred_element_type=jnp.float32)
    down_total = jnp.einsum(
        "ecd,ecf->def", grad_part, hidden_piece, preferred_element_type=jnp.float32
    )
    gate_total, up_total, down_total = (gate_total, up_total, down_total)
    w_gate_grad = gate_total.reshape(slice_rows, -1)
    w_up_grad = up_total.reshape(slice_rows, -1)
    w_down_grad = down_total.reshape(slice_rows, -1)
    mid_own = mid_low.astype(jnp.float32)
    gain_two = lax.dynamic_slice_in_dim(moe_norm, col_start, own_width)
    moe_dot = across_heads(jnp.sum(d_normed_two * gain_two * mid_own, 1)[None, :])[0]
    d_residual = (
        cotangent.astype(jnp.float32)
        + scale_two * gain_two * d_normed_two
        - mid_own * scale_two**3 * (moe_dot / width)[:, None]
    )
    moe_gain_grad = jnp.sum(d_normed_two * mid_own * scale_two, 0)
    d_attn_whole = gather_features(d_residual.astype(jnp.bfloat16))
    d_attended = jnp.dot(d_attn_whole, out_cols, preferred_element_type=jnp.float32).astype(
        jnp.bfloat16
    )
    d_qrot, d_krot, d_values = lax.map(
        tree_grads,
        (q_rot, k_rot, value_trees, d_attended.reshape(tree_shape), log_totals, ancestors),
    )
    d_values_low = d_values.reshape(tok_rows, own_width).astype(jnp.bfloat16)
    d_qn = jax.vmap(unrotate)(d_qrot, cos_table, sin_table).reshape(tok_rows, own_width)
    d_kn = jax.vmap(unrotate)(d_krot, cos_table, sin_table).reshape(tok_rows, own_width)
    qk_dots = across_heads(
        jnp.stack([jnp.sum(query * q_gain * d_qn, 1), jnp.sum(keyed * k_gain * d_kn, 1)])
    )
    d_query_low = (
        q_scale * q_gain * d_qn - query * q_scale**3 * (qk_dots[0] / width)[:, None]
    ).astype(jnp.bfloat16)
    d_keyed_low = (
        k_scale * k_gain * d_kn - keyed * k_scale**3 * (qk_dots[1] / width)[:, None]
    ).astype(jnp.bfloat16)
    q_gain_grad = jnp.sum(d_qn * query * q_scale, 0)
    k_gain_grad = jnp.sum(d_kn * keyed * k_scale, 0)
    d_one_part = (
        contract_cols(d_query_low, query_cols)
        + contract_cols(d_keyed_low, key_cols)
        + contract_cols(d_values_low, value_cols)
    )
    d_normed_one = head_total(d_one_part)
    grad_part = d_attn_whole
    attn_grads = lax.psum_scatter(
        jnp.concatenate(
            [
                contract_rows(normed_one, d_query_low),
                contract_rows(normed_one, d_keyed_low),
                contract_rows(normed_one, d_values_low),
                contract_rows(grad_part, attended),
            ],
            1,
        ).astype(jnp.bfloat16),
        "row",
        scatter_dimension=0,
        tiled=True,
    ).astype(jnp.float32)
    w_query_grad = attn_grads[:, :own_width]
    w_key_grad = attn_grads[:, own_width : 2 * own_width]
    w_value_grad = attn_grads[:, 2 * own_width : 3 * own_width]
    w_out_grad = attn_grads[:, 3 * own_width :]
    tokens_own = tokens.astype(jnp.float32)
    gain_one = lax.dynamic_slice_in_dim(attn_norm, col_start, own_width)
    attn_dot = across_heads(jnp.sum(d_normed_one * gain_one * tokens_own, 1)[None, :])[0]
    tokens_grad = (
        d_residual
        + scale_one * gain_one * d_normed_one
        - tokens_own * scale_one**3 * (attn_dot / width)[:, None]
    )
    attn_gain_grad = jnp.sum(d_normed_one * tokens_own * scale_one, 0)
    gain_grads = lax.psum(
        jnp.stack([attn_gain_grad, q_gain_grad, k_gain_grad, moe_gain_grad]), "row"
    )
    return (
        output,
        tokens_grad,
        gain_grads[0],
        w_query_grad,
        w_key_grad,
        w_value_grad,
        gain_grads[1],
        gain_grads[2],
        w_out_grad,
        gain_grads[3],
        w_gate_grad,
        w_up_grad,
        w_down_grad,
    )


def solution(mesh):
    in_specs = (
        P("row", "col"),
        P(),
        P("row", "col"),
        P("row", "col"),
        P("row", "col"),
        P(),
        P(),
        P("row", "col"),
        P(),
        P("row", "col"),
        P("row", "col"),
        P("row", "col"),
        P("row", None),
        P("row", None),
        P("row", None),
        P("row", "col"),
    )
    out_specs = (
        P("row", "col"),
        P("row", "col"),
        P("col"),
        P("row", "col"),
        P("row", "col"),
        P("row", "col"),
        P("col"),
        P("col"),
        P("row", "col"),
        P("col"),
        P("row", "col"),
        P("row", "col"),
        P("row", "col"),
    )
    return jax.shard_map(body, mesh=mesh, in_specs=in_specs, out_specs=out_specs, check_vma=False)
```

profile of v0, /device:TPU:0, one launch (start us, length us, event | category | flops | bytes accessed | tf_op | source)
XLA Modules:
  0.0 5166.4 jit_solution(12366382255845700313)
XLA Ops:
  10.6 24.1 while.67
  43.1 34.8 all-gather.15.cloned.1.call-done
  91.3 16.1 all-gather.17.cloned.1.call-done
  113.4 23.0 all-gather.19.cloned.1.call-done
  145.1 25.5 psum.35
  200.3 112.0 %while.66 = (s32[]{:T(128)}, bf16[5,512,2,128]{3,2,1,0:T(2,128)(2,1)}, f32[5,2,512]{2,1,0:T(2,128)}, s32[5]{0:T(128)S(1)}, bf16[20,20]{1,0:T(8,128)(2,1)S(1)}, /...) while((s32[]{:T(128)}, ...), condition=%wide.region_11.12_spmd, body=%wide.region_8.11_spmd.sunk | while | flops 1380776960 | bytes 48320480 | solution.py:157
  325.2 133.3 %reduce-scatter.6.cloned.1.call-done = f32[2560,256]{1,0:T(8,128)} async-done(((f32[2560,2048]{1,0:T(8,128)}), f32[2560,256]{1,0:T(8,128)}) %reduce-scatter.6.cloned.1.call-update) | async-done | bytes 2621456 | tf_op jit(solution)/shard_map/reduce_scatter | solution.py:114
  504.4 75.2 %scatter_custom_fusion = s32[3409]{0:T(1024)S(1)} fusion(s32[20480]{0:T(1024)S(1)} %bitcast.250, s32[20480]{0:T(1024)S(1)} %add_select_fusion.4, s32[]{:T(128)} %constant.326.clone.1), kind=kCustom, calls=%fused_computation.258 | custom fusion | bytes 13640 | tf_op jit(solution)/shard_map/scatter | solution.py:99
  579.7 75.5 %scatter_custom_fusion.1 = f32[3409]{0:T(1024)S(1)} fusion(s32[20480]{0:T(1024)S(1)} %bitcast.251, f32[20480]{0:T(1024)S(1)} %reshape.899, f32[]{:T(128)} %constant.315.clone.1), kind=kCustom, calls=%fused_computation.253 | custom fusion | bytes 13640 | tf_op jit(solution)/shard_map/scatter | solution.py:104
  665.4 32.8 gather_fusion.1
  698.2 19.2 reshape.870
  748.5 33.1 gather_fusion
  797.2 358.6 %all-gather.27.cloned.1.call-done = bf16[2048,8192]{0,1:T(8,128)(2,1)} async-done(((bf16[512,8192]{0,1:T(8,128)(2,1)}), bf16[2048,8192]{0,1:T(8,128)(2,1)}) %all-gather.27.cloned.1.call-update) | async-done | bytes 33554448 | tf_op jit(solution)/shard_map/all_gather | solution.py:267
  1155.8 29.1 fusion.137
  1185.0 531.9 %all-gather.29.cloned.1.call-done = bf16[2048,8192]{0,1:T(8,128)(2,1)} async-done(((bf16[512,8192]{0,1:T(8,128)(2,1)}), bf16[2048,8192]{0,1:T(8,128)(2,1)}) %all-gather.29.cloned.1.call-update) | async-done | bytes 33554448 | tf_op jit(solution)/shard_map/all_gather | solution.py:268
  1716.9 29.2 fusion.138
  1746.1 532.0 %all-gather.31.cloned.1.call-done = bf16[2048,8192]{0,1:T(8,128)(2,1)} async-done(((bf16[512,8192]{0,1:T(8,128)(2,1)}), bf16[2048,8192]{0,1:T(8,128)(2,1)}) %all-gather.31.cloned.1.call-update) | async-done | bytes 33554448 | tf_op jit(solution)/shard_map/all_gather | solution.py:269
  2278.1 35.6 multiply_convert_fusion.2
  2313.7 33.7 fusion.140
  2347.4 33.0 convolution_add_fusion
  2380.4 23.3 reshape.915
  2403.7 54.3 %scatter_custom_fusion.3 = f32[2561,2048]{1,0:T(8,128)} fusion(s32[3408]{0:T(1024)} %copy-done.46, f32[3408,2048]{1,0:T(8,128)} %reshape.915, f32[]{:T(128)} %constant.315.clone.1), kind=kCustom, calls=%fused_computation.125 | custom fusion | flops 6979584 | bytes 20980224 | tf_op jit(solution)/shard_map/scatter-add | solution.py:123
  2458.0 16.1 slice.132
  2475.2 133.3 %reduce-scatter.10.cloned.1.call-done = f32[2560,256]{1,0:T(8,128)} async-done(((f32[2560,2048]{1,0:T(8,128)}), f32[2560,256]{1,0:T(8,128)}) %reduce-scatter.10.cloned.1.call-update) | async-done | bytes 2621456 | tf_op jit(solution)/shard_map/reduce_scatter | solution.py:114
  2611.9 23.6 psum.36
  2671.8 33.4 all-gather.35.cloned.1.call-done
  2713.5 234.5 %while.68 = (s32[]{:T(128)}, f32[2560,2,128]{0,2,1:T(8,128)S(1)}, f32[2560,2,128]{0,2,1:T(8,128)}, f32[5,512,2,128]{3,1,0,2:T(8,128)}, s32[5]{0:T(128)S(1)}, /*i...) while((s32[]{:T(128)}, f32[2560,2,128]{0,2,1:T(8,128)S(1)}, ...), condition=%wide.region_29.30_spmd.clone, body=%wide.region_27.29_spmd.clone.sunk | while | flops 3389455360 | bytes 241508032 | solution.py:197
  2979.1 25.4 psum.37
  3050.9 22.4 add_add_fusion
  3073.3 24.6 copy.136
  3105.0 24.6 copy.127
  3129.6 696.4 %all-to-all-done.1 = bf16[8,426,2048]{1,0,2:T(8,128)(2,1)} async-done(((bf16[8,426,2048]{1,0,2:T(8,128)(2,1)}), bf16[8,426,2048]{1,0,2:T(8,128)(2,1)}, u32[]{:S(2)}, u32[]{:S(2)}) %all-to-all-start.1) | async-done | bytes 13959200 | tf_op jit(solution)/shard_map/all_to_all | solution.py:325
  3833.0 28.4 fusion.139
  3861.4 23.2 reshape.863
  3884.7 57.5 %scatter_custom_fusion.2 = f32[2561,2048]{1,0:T(8,128)} fusion(s32[3408]{0:T(1024)} %copy-done.46, f32[3408,2048]{1,0:T(8,128)} %reshape.863, f32[3408]{0:T(1024)S(1)} %bitcast.249, f32[]{:T(128)} %constant.315.clone.1), kind=kCustom, calls=%fused_computation.102 | custom fusion | flops 13959168 | bytes 48912192 | tf_op jit(solution)/shard_map/scatter-add | solution.py:123
  3959.5 30.9 copy.157
  4005.2 475.5 %all-to-all-done = bf16[8,426,2048]{1,0,2:T(8,128)(2,1)} async-done(((bf16[8,426,2048]{1,0,2:T(8,128)(2,1)}), bf16[8,426,2048]{1,0,2:T(8,128)(2,1)}, u32[]{:S(2)}, u32[]{:S(2)}) %all-to-all-start) | async-done | bytes 13959200 | tf_op jit(solution)/shard_map/all_to_all | solution.py:324
  4480.6 30.9 copy.156
  4526.3 80.8 %fusion.57 = f32[8,1024,512]{2,1,0:T(8,128)} fusion(bf16[8,1704,1024]{2,0,1:T(8,128)(2,1)} %all-gather.37.cloned.1.call-done, bf16[8,1704,512]{2,0,1:T(8,128)(2,1)} %bitcast.235), kind=kOutput, calls=%fused_computation.100 | convolution fusion | flops 14294188032 | bytes 58654720 | tf_op jit(solution)/shard_map/ecd,ecf->def/dot_general | solution.py:332
  4607.1 17.4 copy.145
  4624.6 93.1 %fusion.55 = f32[8,1024,512]{2,1,0:T(8,128)} fusion(bf16[8,1704,1024]{2,0,1:T(8,128)(2,1)} %all-gather.39.cloned.1.call-done, bf16[8,1704,512]{2,0,1:T(8,128)(2,1)} %bitcast.236), kind=kOutput, calls=%fused_computation.98 | convolution fusion | flops 14294188032 | bytes 58654720 | tf_op jit(solution)/shard_map/ecd,ecf->def/dot_general | solution.py:335
  4717.6 17.4 copy.146
  4735.1 58.6 %all-gather.41.cloned.1.call-done = bf16[8,1704,1024]{2,0,1:T(8,128)(2,1)} async-done(((bf16[8,426,1024]{2,0,1:T(8,128)(2,1)}), bf16[8,1704,1024]{2,0,1:T(8,128)(2,1)}) %all-gather.41.cloned.1.call-update) | async-done | bytes 27918352 | tf_op jit(solution)/shard_map/all_gather | solution.py:330
  4793.7 80.7 %fusion.53 = f32[8,1024,512]{2,1,0:T(8,128)} fusion(bf16[8,1704,1024]{2,0,1:T(8,128)(2,1)} %all-gather.41.cloned.1.call-done, bf16[8,1704,512]{2,0,1:T(8,128)(2,1)} %bitcast.234), kind=kOutput, calls=%fused_computation.96 | convolution fusion | flops 14294188032 | bytes 58654720 | tf_op jit(solution)/shard_map/ecd,ecf->def/dot_general | solution.py:336
  4874.4 18.5 copy.147
  4900.8 110.4 %reduce-scatter.12.cloned.1.call-done = f32[2560,256]{1,0:T(8,128)} async-done(((f32[2560,2048]{1,0:T(8,128)}), f32[2560,256]{1,0:T(8,128)}) %reduce-scatter.12.cloned.1.call-update) | async-done | bytes 2621456 | tf_op jit(solution)/shard_map/reduce_scatter | solution.py:114
  5025.8 22.3 psum.38
  5048.7 102.4 %reduce-scatter.8.cloned.1.call-done = f32[2560,256]{1,0:T(8,128)} async-done(((f32[2560,2048]{1,0:T(8,128)}), f32[2560,256]{1,0:T(8,128)}) %reduce-scatter.8.cloned.1.call-update) | async-done | bytes 2621456 | tf_op jit(solution)/shard_map/reduce_scatter | solution.py:114
  (552 shorter events, 752.9 us)
Async XLA Ops:
  7.2 70.7 %all-gather.15.cloned.1.call-start = ((), (), s32[]{:S(2)}) async-start(), calls=%async_computation.7 | async-start | bytes 11796480 | tf_op jit(solution)/shard_map/all_gather | solution.py:110
  7.9 99.5 %all-gather.17.cloned.1.call-start = ((), (), s32[]{:S(2)}) async-start(), calls=%async_computation.8 | async-start | bytes 1310720 | tf_op jit(solution)/shard_map/all_gather | solution.py:236
  8.7 127.8 %all-gather.19.cloned.1.call-start = ((), (), s32[]{:S(2)}) async-start(), calls=%async_computation.9 | async-start | bytes 1310720 | tf_op jit(solution)/shard_map/all_gather | solution.py:237
  9.4 172.7 %all-gather.21.cloned.1.call-start = ((), (), s32[]{:S(2)}) async-start(), calls=%async_computation.10 | async-start | bytes 1310720 | tf_op jit(solution)/shard_map/all_gather | solution.py:238
  10.0 302.4 %all-gather.23.cloned.1.call-start = ((), (), s32[]{:S(2)}) async-start(), calls=%async_computation.11 | async-start | bytes 1310720 | tf_op jit(solution)/shard_map/all_gather | solution.py:239
  10.6 447.9 %reduce-scatter.6.cloned.1.call-start = ((), (), s32[]{:S(2)}) async-start(), calls=%async_computation.12 | async-start | bytes 23592960 | tf_op jit(solution)/shard_map/reduce_scatter | solution.py:114
  36.0 134.6 %copy-start.50 = (f32[256]{0:T(256)}, f32[256]{0:T(256)S(1)}, u32[]{:S(2)}) copy-start(f32[256]{0:T(256)S(1)} %dynamic_slice.79) | copy-start | bytes 3076
  36.8 140.8 %copy-start.52 = (f32[256]{0:T(256)}, f32[256]{0:T(256)S(1)}, u32[]{:S(2)}) copy-start(f32[256]{0:T(256)S(1)} %dynamic_slice.80) | copy-start | bytes 3076
  43.1 42.3 copy-start.57
  113.4 57.3 %copy-start.10 = (f32[2560,256]{0,1:T(8,128)}, f32[2560,256]{0,1:T(8,128)S(1)}, u32[]{:S(2)}) copy-start(f32[2560,256]{0,1:T(8,128)S(1)} %get-tuple-element.659) | copy-start | bytes 7864324
  324.3 134.1 %copy-start.13 = (bf16[2560,256]{1,0:T(8,128)(2,1)S(1)}, bf16[2560,256]{1,0:T(8,128)(2,1)}, u32[]{:S(2)}) copy-start(bf16[2560,256]{1,0:T(8,128)(2,1)} %param.22) | copy-start | bytes 3932164
  324.4 330.9 %all-gather.33.cloned.1.call-start = ((), (), s32[]{:S(2)}) async-start(), calls=%async_computation.18 | async-start | bytes 11796480 | tf_op jit(solution)/shard_map/all_gather | solution.py:110
  325.1 408.3 %all-gather.25.cloned.1.call-start = ((), (), s32[]{:S(2)}) async-start(), calls=%async_computation.13 | async-start | bytes 11796480 | tf_op jit(solution)/shard_map/all_gather | solution.py:110
  461.6 694.2 %all-gather.27.cloned.1.call-start = ((), (), s32[]{:S(2)}) async-start(), calls=%async_computation.14 | async-start | bytes 41943040 | tf_op jit(solution)/shard_map/all_gather | solution.py:267
  473.8 1243.1 %all-gather.29.cloned.1.call-start = ((), (), s32[]{:S(2)}) async-start(), calls=%async_computation.15 | async-start | bytes 41943040 | tf_op jit(solution)/shard_map/all_gather | solution.py:268
  485.8 1792.2 %all-gather.31.cloned.1.call-start = ((), (), s32[]{:S(2)}) async-start(), calls=%async_computation.16 | async-start | bytes 41943040 | tf_op jit(solution)/shard_map/all_gather | solution.py:269
  498.0 2110.5 %reduce-scatter.10.cloned.1.call-start = ((), (), s32[]{:S(2)}) async-start(), calls=%async_computation.19 | async-start | bytes 23592960 | tf_op jit(solution)/shard_map/reduce_scatter | solution.py:114
  2313.7 33.7 copy-start.21
  2474.2 134.3 %copy-start.8 = (bf16[2560,256]{1,0:T(8,128)(2,1)S(1)}, bf16[2560,256]{1,0:T(8,128)(2,1)}, u32[]{:S(2)}) copy-start(bf16[2560,256]{1,0:T(8,128)(2,1)} %fusion.95) | copy-start | bytes 3932164
  2474.2 134.3 %copy-start.28 = (f32[2560]{0:T(1024)S(1)}, f32[2560]{0:T(1024)}, u32[]{:S(2)}) copy-start(f32[2560]{0:T(1024)} %copy-done.27) | copy-start | bytes 30724
  2474.2 162.0 %copy-start.17 = (bf16[2560,256]{1,0:T(8,128)(2,1)S(1)}, bf16[2560,256]{1,0:T(8,128)(2,1)}, u32[]{:S(2)}) copy-start(bf16[2560,256]{1,0:T(8,128)(2,1)} %param.37) | copy-start | bytes 3932164
  2474.2 162.0 %copy-start.40 = (f32[2560]{0:T(1024)S(1)}, f32[2560]{0:T(1024)}, u32[]{:S(2)}) copy-start(f32[2560]{0:T(1024)} %get-tuple-element.650) | copy-start | bytes 30724
  2474.2 231.0 %all-gather.35.cloned.1.call-start = ((), (), s32[]{:S(2)}) async-start(), calls=%async_computation.20 | async-start | bytes 11796480 | tf_op jit(solution)/shard_map/all_gather | solution.py:110
  2475.2 164.8 %copy-start.54 = (f32[256]{0:T(256)}, f32[256]{0:T(256)S(1)}, u32[]{:S(2)}) copy-start(f32[256]{0:T(256)S(1)} %dynamic_slice.81) | copy-start | bytes 3076
  2640.0 1886.4 %all-gather.37.cloned.1.call-start = ((), (), s32[]{:S(2)}) async-start(), calls=%async_computation.23 | async-start | bytes 34897920 | tf_op jit(solution)/shard_map/all_gather | solution.py:328
  2649.9 1974.7 %all-gather.39.cloned.1.call-start = ((), (), s32[]{:S(2)}) async-start(), calls=%async_computation.24 | async-start | bytes 34897920 | tf_op jit(solution)/shard_map/all_gather | solution.py:329
  2659.9 2133.8 %all-gather.41.cloned.1.call-start = ((), (), s32[]{:S(2)}) async-start(), calls=%async_computation.25 | async-start | bytes 34897920 | tf_op jit(solution)/shard_map/all_gather | solution.py:330
  2669.9 2223.0 %reduce-scatter.14.cloned.1.call-start = ((), (), s32[]{:S(2)}) async-start(), calls=%async_computation.22 | async-start | bytes 5242880 | tf_op jit(solution)/shard_map/reduce_scatter | solution.py:381
  2671.8 41.6 copy-start.60
  2671.8 41.6 copy-start.65
  2976.1 28.5 copy-start.47
  2976.1 28.5 copy-start.48
  3030.3 1980.9 %reduce-scatter.12.cloned.1.call-start = ((), (), s32[]{:S(2)}) async-start(), calls=%async_computation.21 | async-start | bytes 23592960 | tf_op jit(solution)/shard_map/reduce_scatter | solution.py:114
  3098.0 728.0 %all-to-all-start.1 = ((bf16[8,426,2048]{1,0,2:T(8,128)(2,1)}), bf16[8,426,2048]{1,0,2:T(8,128)(2,1)}, u32[]{:S(2)}, u32[]{:S(2)}) async-start(bf16[8,426,2048]{1,0,2:T(8,128)(2,1)} %copy.136), calls=%async_computation.6 | async-start | bytes 33554432 | tf_op jit(solution)/shard_map/all_to_all | solution.py:325
  3826.0 654.7 %all-to-all-start = ((bf16[8,426,2048]{1,0,2:T(8,128)(2,1)}), bf16[8,426,2048]{1,0,2:T(8,128)(2,1)}, u32[]{:S(2)}, u32[]{:S(2)}) async-start(bf16[8,426,2048]{1,0,2:T(8,128)(2,1)} %copy.127), calls=%async_computation.5 | async-start | bytes 33554432 | tf_op jit(solution)/shard_map/all_to_all | solution.py:324
  3833.0 1318.2 %reduce-scatter.8.cloned.1.call-start = ((), (), s32[]{:S(2)}) async-start(), calls=%async_computation.17 | async-start | bytes 23592960 | tf_op jit(solution)/shard_map/reduce_scatter | solution.py:114
  4895.4 115.7 %copy-start.14 = (bf16[2560,256]{1,0:T(8,128)(2,1)S(1)}, bf16[2560,256]{1,0:T(8,128)(2,1)}, u32[]{:S(2)}) copy-start(bf16[2560,256]{1,0:T(8,128)(2,1)} %param.22) | copy-start | bytes 3932164
  4895.4 115.7 %copy-start.37 = (f32[2560]{0:T(1024)S(1)}, f32[2560]{0:T(1024)}, u32[]{:S(2)}) copy-start(f32[2560]{0:T(1024)} %copy-done.36) | copy-start | bytes 30724
  4895.4 115.7 %copy-start.58 = (f32[256]{0:T(256)S(1)}, f32[256]{0:T(256)}, u32[]{:S(2)}) copy-start(f32[256]{0:T(256)} %dynamic_slice.82) | copy-start | bytes 3076
  4899.7 114.4 %copy-start.61 = (f32[256]{0:T(256)S(1)}, f32[256]{0:T(256)}, u32[]{:S(2)}) copy-start(f32[256]{0:T(256)} %get-tuple-element.557) | copy-start | bytes 3076
  4899.7 114.4 %copy-start.62 = (f32[256]{0:T(256)S(1)}, f32[256]{0:T(256)}, u32[]{:S(2)}) copy-start(f32[256]{0:T(256)} %get-tuple-element.551) | copy-start | bytes 3076
  4899.7 114.4 %copy-start.63 = (f32[256]{0:T(256)S(1)}, f32[256]{0:T(256)}, u32[]{:S(2)}) copy-start(f32[256]{0:T(256)} %get-tuple-element.553) | copy-start | bytes 3076
  4899.7 251.5 %copy-start.9 = (bf16[2560,256]{1,0:T(8,128)(2,1)S(1)}, bf16[2560,256]{1,0:T(8,128)(2,1)}, u32[]{:S(2)}) copy-start(bf16[2560,256]{1,0:T(8,128)(2,1)} %fusion.95) | copy-start | bytes 3932164
  4899.7 251.5 %copy-start.29 = (f32[2560]{0:T(1024)S(1)}, f32[2560]{0:T(1024)}, u32[]{:S(2)}) copy-start(f32[2560]{0:T(1024)} %copy-done.27) | copy-start | bytes 30724
  4899.7 251.5 %copy-start.41 = (f32[2560]{0:T(1024)S(1)}, f32[2560]{0:T(1024)}, u32[]{:S(2)}) copy-start(f32[2560]{0:T(1024)} %get-tuple-element.650) | copy-start | bytes 30724
  4899.7 251.5 %copy-start.43 = (f32[2560]{0:T(1024)S(1)}, f32[2560]{0:T(1024)}, u32[]{:S(2)}) copy-start(f32[2560]{0:T(1024)} %copy-done.42) | copy-start | bytes 30724
  4899.7 251.5 %copy-start.49 = (f32[2560]{0:T(1024)S(1)}, f32[2560]{0:T(1024)}, u32[]{:S(2)}) copy-start(f32[2560]{0:T(1024)} %get-tuple-element.648) | copy-start | bytes 30724
  4899.7 251.5 %copy-start.55 = (f32[256]{0:T(256)S(1)}, f32[256]{0:T(256)}, u32[]{:S(2)}) copy-start(f32[256]{0:T(256)} %copy-done.54) | copy-start | bytes 3076
  (80 other events, 562.0 us)
Sparse Core Ops, SparseCore 0:
  9.9 67.9 all-gather.14
  79.4 27.9 all-gather.16
  109.0 27.4 all-gather.18
  137.9 27.4 all-gather.20
  166.7 27.4 all-gather.22
  324.5 133.9 reduce-scatter.5
  460.4 65.2 all-gather.32
  527.5 65.2 all-gather.24
  594.4 561.3 all-gather.26
  1157.2 559.5 all-gather.28
  1718.5 559.5 all-gather.30
  2474.3 134.1 reduce-scatter.9
  2640.1 65.1 all-gather.34
  2706.7 596.9 all-gather.36
  3305.1 951.5 all-gather.38
  4258.1 535.5 all-gather.40
  4795.8 74.9 reduce-scatter.13
  4874.7 136.4 reduce-scatter.11
  5015.2 135.9 reduce-scatter.7
where the time goes:
time: 5180 us; the launch traced here: 5170 us
  waiting for transfers between devices  3240 us (63%)
  matrix products  726 us (14%)
  local copies, waits for them, and re-layouts  723 us (14%)
  other arithmetic  313 us (6%)
  blocking collectives  108 us (2%)
    all_to_all x1, waiting for transfers between devices, body(): lax.all_to_all(d_out_low, 'row', split_axis=2, concat_axis=1, tiled=True)  696 us
    all_gather x1, waiting for transfers between devices, body(): lax.all_gather(w_down, 'row', axis=0, tiled=True)  532 us
    all_gather x1, waiting for transfers between devices, body(): lax.all_gather(w_up, 'row', axis=0, tiled=True)  532 us
    reduce_scatter x4, waiting for transfers between devices, head_total(): lax.psum_scatter(partial_value, 'col', scatter_dimension=1, tiled=True)  479 us
    all_to_all x1, waiting for transfers between devices, body(): lax.all_to_all(expert_in, 'row', split_axis=2, concat_axis=1, tiled=True)  475 us
    all_gather x1, waiting for transfers between devices, body(): lax.all_gather(w_gate, 'row', axis=0, tiled=True)  359 us
    scatter-add x2, other arithmetic, expert_total(): jnp.zeros((tok_rows + 1, flat.shape[1]), jnp.float32).at[slot_token]  112 us
    unnamed x149, local copies, waits for them, and re-layouts  108 us
  transfers between devices with their start and end apart: 21, of which 14 were waited for; matrix products, arithmetic and copies ran while one was open for 29% of the time, Pallas kernels for 0%

commit v1 on v0

v1 whole, which is shorter than its diff:
```python
import math

import jax
import jax.numpy as jnp
from jax import lax
from jax.experimental import pallas as pl
from jax.experimental.pallas import tpu as pltpu
from jax.sharding import PartitionSpec as P

HD = 128
FF = 1024
SEG = 128
TREE = 2560
NSEG = 20
TRUNK = 512
BRANCH_END = 1024
LEAF_END = 2048
CAP = 426
CAPP = 432


EPS = 1e-05
NEGATIVE = -1e30
MIB = 1024 * 1024


def depths_of(parent_ids):
    segment_ids = jnp.arange(NSEG, dtype=jnp.int32)

    def advance(turn_index, loop_state):
        current, depth = loop_state
        matches = current[:, None] == segment_ids[None, :]
        parent_of = jnp.sum(jnp.where(matches, parent_ids[None, :], 0), 1)
        current = jnp.where(current >= 0, parent_of, -1)
        return (current, depth + (current >= 0).astype(jnp.int32))

    start = (segment_ids, jnp.zeros((NSEG,), jnp.int32))
    state = start
    for turn in range(6):
        state = advance(turn, state)
    return state[1]


def rope_tables(parent_ids):
    depths = depths_of(parent_ids)
    position = jnp.arange(TREE, dtype=jnp.int32)
    places = (jnp.repeat(depths, SEG) * SEG + position % SEG).astype(jnp.float32)
    frequency = jnp.exp(jnp.arange(HD // 2, dtype=jnp.float32) * (-2.0 * math.log(10000.0) / HD))
    angles = places[:, None] * frequency[None, :]
    cosine, sine = jnp.cos(angles), jnp.sin(angles)
    return (
        jnp.concatenate([cosine, cosine], -1),
        jnp.concatenate([-sine, sine], -1),
    )


def dot_f32(left, right, left_dim, right_dim):
    return lax.dot_general(
        left, right, (((left_dim,), (right_dim,)), ((), ())), preferred_element_type=jnp.float32
    )


def contract_rows(left, right):
    return dot_f32(left, right, 0, 0)


def contract_cols(left, right):
    return dot_f32(left, right, 1, 1)


def over_col(partial_value):
    return jnp.sum(lax.all_gather(partial_value, "col", axis=0), 0)


def causal(count):
    rows = lax.broadcasted_iota(jnp.int32, (count, count), 0)
    cols = lax.broadcasted_iota(jnp.int32, (count, count), 1)
    return cols <= rows


def key_starts(chunk, parent_of):
    first = chunk * 4
    blocks = [[(first + s) * SEG for s in range(4)]]
    if TRUNK * chunk >= BRANCH_END and TRUNK * chunk < LEAF_END:
        blocks.append([parent_of[first + s] * SEG for s in range(4)])
    return blocks


def seg_dot(rows, keys_ref, starts):
    return jnp.concatenate(
        [
            contract_cols(rows[s * SEG : (s + 1) * SEG], keys_ref[pl.ds(starts[s], SEG), :])
            for s in range(4)
        ],
        0,
    )


def chunk_weights(chunk, query, k_ref, blocks, scale):
    pieces = []
    if chunk == 0:
        score = contract_cols(query, k_ref[0:TRUNK, :]) * scale
        pieces.append(jnp.where(causal(TRUNK), score, NEGATIVE))
    else:
        if TRUNK * chunk < LEAF_END:
            pieces.append(contract_cols(query, k_ref[0:TRUNK, :]) * scale)
        mask = jnp.concatenate([causal(SEG)] * 4, 0)
        pieces.append(jnp.where(mask, seg_dot(query, k_ref, blocks[0]) * scale, NEGATIVE))
        for starts in blocks[1:]:
            pieces.append(seg_dot(query, k_ref, starts) * scale)
    highest = jnp.max(pieces[0], -1, keepdims=True)
    for piece in pieces[1:]:
        highest = jnp.maximum(highest, jnp.max(piece, -1, keepdims=True))
    raised = [jnp.exp(piece - highest) for piece in pieces]
    total = jnp.sum(raised[0], -1, keepdims=True)
    for piece in raised[1:]:
        total = total + jnp.sum(piece, -1, keepdims=True)
    inverse = 1.0 / total
    return [piece * inverse for piece in raised]


def chunk_parts(chunk, pieces, blocks):
    places = []
    if chunk == 0:
        places = [None]
    else:
        if TRUNK * chunk < LEAF_END:
            places.append(None)
        places = places + blocks
    return list(zip(pieces, places))


def forward_kernel(
    parents_ref,
    q_ref,
    k_ref,
    v_ref,
    qs_ref,
    ks_ref,
    qg_ref,
    kg_ref,
    cos_ref,
    sin_ref,
    att_ref,
    qr_ref,
    kr_ref,
    vl_ref,
):
    tree = pl.program_id(0)
    scale = 1.0 / math.sqrt(HD)
    parent_of = [parents_ref[tree, s] for s in range(NSEG)]

    def turned(field):
        return field * cos_ref[...] + pltpu.roll(field, HD // 2, 1) * sin_ref[...]

    qr_ref[...] = turned(q_ref[...] * qs_ref[...] * qg_ref[...]).astype(jnp.bfloat16)
    kr_ref[...] = turned(k_ref[...] * ks_ref[...] * kg_ref[...]).astype(jnp.bfloat16)
    vl_ref[...] = v_ref[...].astype(jnp.bfloat16)
    for chunk in range(TREE // TRUNK):
        rows = slice(chunk * TRUNK, (chunk + 1) * TRUNK)
        blocks = key_starts(chunk, parent_of)
        weights = chunk_weights(chunk, qr_ref[rows, :], kr_ref, blocks, scale)
        total = jnp.zeros((TRUNK, HD), jnp.float32)
        for weight, starts in chunk_parts(chunk, weights, blocks):
            low = weight.astype(jnp.bfloat16)
            if starts is None:
                total = total + dot_f32(low, vl_ref[0:TRUNK, :], 1, 0)
            else:
                total = total + jnp.concatenate(
                    [
                        dot_f32(
                            low[s * SEG : (s + 1) * SEG], vl_ref[pl.ds(starts[s], SEG), :], 1, 0
                        )
                        for s in range(4)
                    ],
                    0,
                )
        att_ref[rows, :] = total.astype(jnp.bfloat16)


def backward_kernel(
    parents_ref,
    qr_ref,
    kr_ref,
    vl_ref,
    do_ref,
    cos_ref,
    sin_ref,
    dq_ref,
    dk_ref,
    dv_ref,
    dv_acc,
):
    tree = pl.program_id(0)
    scale = 1.0 / math.sqrt(HD)
    parent_of = [parents_ref[tree, s] for s in range(NSEG)]
    dk_ref[...] = jnp.zeros_like(dk_ref)
    dv_acc[...] = jnp.zeros_like(dv_acc)
    for chunk in range(TREE // TRUNK):
        rows = slice(chunk * TRUNK, (chunk + 1) * TRUNK)
        blocks = key_starts(chunk, parent_of)
        query = qr_ref[rows, :]
        grad = do_ref[rows, :]
        weights = chunk_weights(chunk, query, kr_ref, blocks, scale)
        parts = chunk_parts(chunk, weights, blocks)
        d_weights = []
        row_dot = jnp.zeros((TRUNK, 1), jnp.float32)
        for weight, starts in parts:
            if starts is None:
                d_weight = contract_cols(grad, vl_ref[0:TRUNK, :])
            else:
                d_weight = seg_dot(grad, vl_ref, starts)
            d_weights.append(d_weight)
            row_dot = row_dot + jnp.sum(weight * d_weight, -1, keepdims=True)
        d_query = jnp.zeros((TRUNK, HD), jnp.float32)
        for (weight, starts), d_weight in zip(parts, d_weights):
            low = weight.astype(jnp.bfloat16)
            d_score = (weight * (d_weight - row_dot)).astype(jnp.bfloat16)
            if starts is None:
                d_query = d_query + dot_f32(d_score, kr_ref[0:TRUNK, :], 1, 0)
                dk_ref[0:TRUNK, :] += contract_rows(d_score, query)
                dv_acc[0:TRUNK, :] += contract_rows(low, grad)
            else:
                turns = []
                for s in range(4):
                    own = slice(s * SEG, (s + 1) * SEG)
                    keys = pl.ds(starts[s], SEG)
                    turns.append(dot_f32(d_score[own], kr_ref[keys, :], 1, 0))
                    dk_ref[keys, :] += contract_rows(d_score[own], query[own])
                    dv_acc[keys, :] += contract_rows(low[own], grad[own])
                d_query = d_query + jnp.concatenate(turns, 0)
        dq_ref[rows, :] = d_query

    def unturned(field):
        return (field * cos_ref[...] - pltpu.roll(field, HD // 2, 1) * sin_ref[...]) * scale

    dq_ref[...] = unturned(dq_ref[...])
    dk_ref[...] = unturned(dk_ref[...])
    dv_ref[...] = dv_acc[...].astype(jnp.bfloat16)


def attend(parents, qkv, q_scale, k_scale, q_gain, k_gain, cos_table, sin_table, heads):
    trees = parents.shape[0]
    rows = qkv.shape[0]

    def field(shift):
        return pl.BlockSpec((TREE, HD), lambda t, h, p: (t, h + shift))

    scale_spec = pl.BlockSpec((TREE, 1), lambda t, h, p: (t, 0))
    gain_spec = pl.BlockSpec((1, HD), lambda t, h, p: (0, h))
    table = pl.BlockSpec((TREE, HD), lambda t, h, p: (t, 0))
    return pl.pallas_call(
        forward_kernel,
        grid_spec=pltpu.PrefetchScalarGridSpec(
            num_scalar_prefetch=1,
            grid=(trees, heads),
            in_specs=[
                field(0),
                field(heads),
                field(2 * heads),
                scale_spec,
                scale_spec,
                gain_spec,
                gain_spec,
                table,
                table,
            ],
            out_specs=[field(0)] * 4,
        ),
        out_shape=[jax.ShapeDtypeStruct((rows, heads * HD), jnp.bfloat16)] * 4,
        compiler_params=pltpu.CompilerParams(vmem_limit_bytes=50 * MIB),
        name="tree_forward",
    )(
        parents,
        qkv,
        qkv,
        qkv,
        q_scale,
        k_scale,
        q_gain[None, :],
        k_gain[None, :],
        cos_table,
        sin_table,
    )


def attend_back(parents, q_rot, k_rot, values, d_attended, cos_table, sin_table, heads):
    trees = parents.shape[0]
    rows = q_rot.shape[0]
    field = pl.BlockSpec((TREE, HD), lambda t, h, p: (t, h))
    table = pl.BlockSpec((TREE, HD), lambda t, h, p: (t, 0))
    return pl.pallas_call(
        backward_kernel,
        grid_spec=pltpu.PrefetchScalarGridSpec(
            num_scalar_prefetch=1,
            grid=(trees, heads),
            in_specs=[field, field, field, field, table, table],
            out_specs=[field] * 3,
            scratch_shapes=[pltpu.VMEM((TREE, HD), jnp.float32)],
        ),
        out_shape=[
            jax.ShapeDtypeStruct((rows, heads * HD), jnp.float32),
            jax.ShapeDtypeStruct((rows, heads * HD), jnp.float32),
            jax.ShapeDtypeStruct((rows, heads * HD), jnp.bfloat16),
        ],
        compiler_params=pltpu.CompilerParams(vmem_limit_bytes=50 * MIB),
        name="tree_backward",
    )(parents, q_rot, k_rot, values, d_attended, cos_table, sin_table)


def combine_kernel(slot_ref, y_ref, out_ref):
    units = y_ref.shape[0]
    total = None
    for e in range(units):
        slots = lax.broadcasted_iota(jnp.int32, (slot_ref.shape[0], CAPP), 1)
        picks = (slot_ref[:, e : e + 1] == slots).astype(jnp.bfloat16)
        term = dot_f32(picks, y_ref[e, 0], 1, 0)
        total = term if total is None else total + term
    out_ref[...] = total.astype(out_ref.dtype)


def combine(slot_of, slot_rows, tok_rows):
    units, groups, _, width = slot_rows.shape
    block = 512
    steps = tok_rows // block
    return pl.pallas_call(
        combine_kernel,
        grid=(groups, steps),
        in_specs=[
            pl.BlockSpec((block, units), lambda g, t: (g * steps + t, 0)),
            pl.BlockSpec((units, 1, CAPP, width), lambda g, t: (0, g, 0, 0)),
        ],
        out_specs=pl.BlockSpec((block, width), lambda g, t: (g * steps + t, 0)),
        out_shape=jax.ShapeDtypeStruct((groups * tok_rows, width), jnp.bfloat16),
        compiler_params=pltpu.CompilerParams(vmem_limit_bytes=50 * MIB),
        cost_estimate=pl.CostEstimate(
            flops=2 * groups * tok_rows * units * CAPP * width,
            bytes_accessed=2 * groups * tok_rows * width,
            transcendentals=0,
        ),
        name="combine",
    )(slot_of, slot_rows)


def rows_home(weight):
    groups = lax.axis_size("row")
    here = lax.axis_index("row")
    depth, columns = weight.shape
    share = columns // groups
    whole = jnp.zeros((depth * groups, share), weight.dtype)
    for k in range(groups):
        to = (here + k) % groups
        block = lax.dynamic_slice_in_dim(weight, to * share, share, 1)
        if k > 0:
            block = lax.ppermute(block, "row", [(i, (i + k) % groups) for i in range(groups)])
        whole = lax.dynamic_update_slice_in_dim(
            whole, block, ((here - k) % groups) * depth, 0
        )
    return whole


def rows_back(grad):
    groups = lax.axis_size("row")
    here = lax.axis_index("row")
    depth, share = grad.shape[0] // groups, grad.shape[1]
    whole = jnp.zeros((depth, share * groups), jnp.float32)
    for k in range(groups):
        to = (here + k) % groups
        block = lax.dynamic_slice_in_dim(grad, to * depth, depth, 0)
        if k > 0:
            block = lax.ppermute(block, "row", [(i, (i + k) % groups) for i in range(groups)])
        whole = lax.dynamic_update_slice_in_dim(
            whole, block.astype(jnp.float32), ((here - k) % groups) * share, 1
        )
    return whole


def total_home(partial_rows):
    groups = lax.axis_size("row")
    here = lax.axis_index("row")
    part = lax.psum_scatter(partial_rows, "col", scatter_dimension=1, tiled=True)
    rows = part.shape[0] // groups
    total = None
    for k in range(groups):
        to = (here + k) % groups
        block = lax.dynamic_slice_in_dim(part, to * rows, rows, 0)
        if k > 0:
            block = lax.ppermute(block, "row", [(i, (i + k) % groups) for i in range(groups)])
        block = block.astype(jnp.float32)
        total = block if total is None else total + block
    return total


def gather_all(part_rows):
    return lax.all_gather(
        lax.all_gather(part_rows, "row", axis=0, tiled=True), "col", axis=1, tiled=True
    )


def body(
    tokens,
    attn_norm,
    w_query,
    w_key,
    w_value,
    q_norm,
    k_norm,
    w_out,
    moe_norm,
    w_gate,
    w_up,
    w_down,
    routes,
    gates,
    parents,
    cotangent,
):
    tok_rows, own_width = tokens.shape
    groups = lax.axis_size("row")
    cols = lax.axis_size("col")
    width = own_width * cols
    here, col = lax.axis_index("row"), lax.axis_index("col")
    col_start = col * own_width
    heads = own_width // HD
    trees = parents.shape[0]

    whole = lax.all_gather(tokens, "col", axis=1, tiled=True)
    qkv_cols = lax.all_gather(
        jnp.concatenate([w_query, w_key, w_value], 1), "row", axis=0, tiled=True
    )
    out_cols = lax.all_gather(w_out, "row", axis=0, tiled=True)
    cos_table, sin_table = jax.vmap(rope_tables)(parents)
    cos_table, sin_table = cos_table.reshape(-1, HD), sin_table.reshape(-1, HD)
    wide = whole.astype(jnp.float32)
    scale_one = lax.rsqrt(jnp.mean(wide * wide, 1, keepdims=True) + EPS)
    normed_one = (wide * scale_one * attn_norm[None, :]).astype(jnp.bfloat16)
    qkv = jnp.dot(normed_one, qkv_cols, preferred_element_type=jnp.float32)
    query, keyed = qkv[:, :own_width], qkv[:, own_width : 2 * own_width]
    squares = over_col(jnp.stack([jnp.sum(query * query, 1), jnp.sum(keyed * keyed, 1)]))
    q_scale = lax.rsqrt(squares[0] / width + EPS)[:, None]
    k_scale = lax.rsqrt(squares[1] / width + EPS)[:, None]
    q_gain = lax.dynamic_slice_in_dim(q_norm, col_start, own_width)
    k_gain = lax.dynamic_slice_in_dim(k_norm, col_start, own_width)
    attended, q_rot, k_rot, value_low = attend(
        parents, qkv, q_scale, k_scale, q_gain, k_gain, cos_table, sin_table, heads
    )
    attn_sum = lax.psum_scatter(
        contract_cols(attended, out_cols).astype(jnp.bfloat16),
        "col",
        scatter_dimension=1,
        tiled=True,
    )
    residual = tokens.astype(jnp.float32) + attn_sum.astype(jnp.float32)
    mid_low = residual.astype(jnp.bfloat16)
    mid_own = mid_low.astype(jnp.float32)
    mid_all = gather_all(mid_low)
    scale_two = lax.rsqrt(over_col(jnp.sum(mid_own * mid_own, 1)) / width + EPS)[:, None]

    share = w_gate.shape[1] // groups
    units, hidden_units = max(1, share // FF), min(share, FF)
    first_unit = col * (w_gate.shape[1] // FF) + (here * share) // FF
    route_all = lax.all_gather(routes, "row", axis=0)
    gate_all = lax.all_gather(gates, "row", axis=0)
    unit_ids = first_unit + jnp.arange(units, dtype=jnp.int32)
    match = route_all[None] == unit_ids[:, None, None, None]
    named = jnp.any(match, -1)
    token_gate = jnp.sum(jnp.where(match, gate_all[None], 0.0), -1)
    rank = jnp.cumsum(named.astype(jnp.int32), 2) - 1
    slot_of = jnp.where(named, rank, -1)
    in_slot = slot_of[:, :, None, :] == jnp.arange(CAPP, dtype=jnp.int32)[None, None, :, None]
    slot_token = jnp.sum(
        jnp.where(in_slot, jnp.arange(tok_rows, dtype=jnp.int32)[None, None, None, :], 0), -1
    )
    slot_gate = jnp.sum(jnp.where(in_slot, token_gate[:, :, None, :], 0.0), -1)
    slot_row = slot_token + (jnp.arange(groups, dtype=jnp.int32) * tok_rows)[None, :, None]
    slot_row = slot_row.reshape(-1)
    slot_gate = slot_gate.reshape(units, -1)[:, :, None]
    slot_of = slot_of.transpose(1, 2, 0).reshape(groups * tok_rows, units)

    gate_home, up_home, down_home = rows_home(w_gate), rows_home(w_up), rows_home(w_down)
    grad_all = gather_all(cotangent)
    slots = groups * CAPP
    slot_mid = mid_all[slot_row].astype(jnp.float32)
    slot_scale = lax.rsqrt(jnp.mean(slot_mid * slot_mid, 1, keepdims=True) + EPS)
    expert_in = (slot_mid * slot_scale * moe_norm[None, :]).astype(jnp.bfloat16)
    expert_in = expert_in.reshape(units, slots, width)
    slot_grad = grad_all[slot_row].astype(jnp.float32).reshape(units, slots, width)
    d_out = (slot_gate * slot_grad).astype(jnp.bfloat16)

    gated, d_in, gate_grads, up_grads, down_grads = [], [], [], [], []
    for e in range(units):
        unit = slice(e * hidden_units, (e + 1) * hidden_units)
        x_e, d_e = expert_in[e], d_out[e]
        gate_w, up_w, down_w = gate_home[:, unit], up_home[:, unit], down_home[:, unit]
        gate_act = dot_f32(x_e, gate_w, 1, 0)
        up_act = dot_f32(x_e, up_w, 1, 0)
        sigmoid_gate = jax.nn.sigmoid(gate_act)
        silu_gate = gate_act * sigmoid_gate
        hidden = (silu_gate * up_act).astype(jnp.bfloat16)
        down_grads.append(contract_rows(d_e, hidden).astype(jnp.bfloat16))
        d_hidden = dot_f32(d_e, down_w, 1, 0)
        d_gate = (
            d_hidden * up_act * sigmoid_gate * (1.0 + gate_act * (1.0 - sigmoid_gate))
        ).astype(jnp.bfloat16)
        d_up = (d_hidden * silu_gate).astype(jnp.bfloat16)
        d_in.append(
            (contract_cols(d_gate, gate_w) + contract_cols(d_up, up_w)).astype(jnp.bfloat16)
        )
        gate_grads.append(contract_rows(x_e, d_gate).astype(jnp.bfloat16))
        up_grads.append(contract_rows(x_e, d_up).astype(jnp.bfloat16))
        gated.append((slot_gate[e] * contract_cols(hidden, down_w)).astype(jnp.bfloat16))
    slot_shape = (units, groups, CAPP, width)
    d_normed_two = total_home(combine(slot_of, jnp.stack(d_in).reshape(slot_shape), tok_rows))
    moe_sum = total_home(combine(slot_of, jnp.stack(gated).reshape(slot_shape), tok_rows))
    output = (residual + moe_sum).astype(jnp.bfloat16)
    w_down_grad = rows_back(jnp.concatenate(down_grads, 1))
    w_gate_grad = rows_back(jnp.concatenate(gate_grads, 1))
    w_up_grad = rows_back(jnp.concatenate(up_grads, 1))

    gain_two = lax.dynamic_slice_in_dim(moe_norm, col_start, own_width)
    moe_dot = over_col(jnp.sum(d_normed_two * gain_two * mid_own, 1))
    d_residual = (
        cotangent.astype(jnp.float32)
        + scale_two * gain_two * d_normed_two
        - mid_own * scale_two**3 * (moe_dot / width)[:, None]
    )
    moe_gain_grad = jnp.sum(d_normed_two * mid_own * scale_two, 0)
    d_attn_whole = lax.all_gather(d_residual.astype(jnp.bfloat16), "col", axis=1, tiled=True)
    d_attended = jnp.dot(d_attn_whole, out_cols, preferred_element_type=jnp.float32).astype(
        jnp.bfloat16
    )
    d_qn, d_kn, d_values = attend_back(
        parents, q_rot, k_rot, value_low, d_attended, cos_table, sin_table, heads
    )
    qk_dots = over_col(
        jnp.stack([jnp.sum(query * q_gain * d_qn, 1), jnp.sum(keyed * k_gain * d_kn, 1)])
    )
    d_query = (
        q_scale * q_gain * d_qn - query * q_scale**3 * (qk_dots[0] / width)[:, None]
    ).astype(jnp.bfloat16)
    d_keyed = (
        k_scale * k_gain * d_kn - keyed * k_scale**3 * (qk_dots[1] / width)[:, None]
    ).astype(jnp.bfloat16)
    q_gain_grad = jnp.sum(d_qn * query * q_scale, 0)
    k_gain_grad = jnp.sum(d_kn * keyed * k_scale, 0)
    d_qkv = jnp.concatenate([d_query, d_keyed, d_values], 1)
    d_normed_one = lax.psum_scatter(
        contract_cols(d_qkv, qkv_cols).astype(jnp.bfloat16),
        "col",
        scatter_dimension=1,
        tiled=True,
    ).astype(jnp.float32)
    attn_grads = lax.psum_scatter(
        jnp.concatenate(
            [contract_rows(normed_one, d_qkv), contract_rows(d_attn_whole, attended)], 1
        ).astype(jnp.bfloat16),
        "row",
        scatter_dimension=0,
        tiled=True,
    ).astype(jnp.float32)
    w_query_grad = attn_grads[:, :own_width]
    w_key_grad = attn_grads[:, own_width : 2 * own_width]
    w_value_grad = attn_grads[:, 2 * own_width : 3 * own_width]
    w_out_grad = attn_grads[:, 3 * own_width :]
    tokens_own = tokens.astype(jnp.float32)
    gain_one = lax.dynamic_slice_in_dim(attn_norm, col_start, own_width)
    attn_dot = over_col(jnp.sum(d_normed_one * gain_one * tokens_own, 1))
    tokens_grad = (
        d_residual
        + scale_one * gain_one * d_normed_one
        - tokens_own * scale_one**3 * (attn_dot / width)[:, None]
    )
    attn_gain_grad = jnp.sum(d_normed_one * tokens_own * scale_one, 0)
    gain_grads = jnp.sum(
        lax.all_gather(
            jnp.stack([attn_gain_grad, q_gain_grad, k_gain_grad, moe_gain_grad]), "row", axis=0
        ),
        0,
    )
    return (
        output,
        tokens_grad,
        gain_grads[0],
        w_query_grad,
        w_key_grad,
        w_value_grad,
        gain_grads[1],
        gain_grads[2],
        w_out_grad,
        gain_grads[3],
        w_gate_grad,
        w_up_grad,
        w_down_grad,
    )


def solution(mesh):
    grid = P("row", "col")
    rows = P("row", None)
    in_specs = (
        grid,
        P(),
        grid,
        grid,
        grid,
        P(),
        P(),
        grid,
        P(),
        grid,
        grid,
        grid,
        rows,
        rows,
        rows,
        grid,
    )
    out_specs = (
        grid,
        grid,
        P("col"),
        grid,
        grid,
        grid,
        P("col"),
        P("col"),
        grid,
        P("col"),
        grid,
        grid,
        grid,
    )
    return jax.shard_map(body, mesh=mesh, in_specs=in_specs, out_specs=out_specs, check_vma=False)
```

time: 5180 us -> 2890 us (0.56)
  waiting for transfers between devices: 3240 us -> 1250 us
  matrix products: 726 us -> 281 us
  local copies, waits for them, and re-layouts: 723 us -> 321 us
  blocking collectives: 108 us -> 463 us
  starting transfers between devices: 15.3 us -> 248 us
  other arithmetic: 313 us -> 150 us
  Pallas kernels: 0 us -> 146 us
    all_gather x14 -> x8, waiting for transfers between devices: 1590 us -> 304 us  [the longest x2 194 us: gather_all(): lax.all_gather(part_rows, 'row', axis=0, tiled=True)]
    all_to_all x2 -> x0, waiting for transfers between devices: 1170 us -> none  [the longest x1 696 us: body(): lax.all_to_all(d_out_low, 'row', split_axis=2, concat_axis=1, tiled=True)]
    ppermute x0 -> x24, waiting for transfers between devices: none -> 495 us  [the longest x9 252 us: rows_back(): lax.ppermute(block, 'row', [(i, (i + k) % groups) for i in range(groups)])]
    all_gather x0 -> x8, blocking collectives: none -> 463 us  [the longest x1 308 us: body(): route_all = lax.all_gather(routes, 'row', axis=0)]
    dot_general x65 -> x23, matrix products: 718 us -> 273 us  [the longest x22 260 us: dot_f32(): lax.dot_general(left, right, (((left_dim,), (right_dim,)), ((), ())), pre...]
    ppermute x0 -> x24, starting transfers between devices: none -> 247 us  [the longest x9 182 us: rows_back(): lax.ppermute(block, 'row', [(i, (i + k) % groups) for i in range(groups)])]
    scatter x2 -> x0, local copies, waits for them, and re-layouts: 151 us -> none  [the longest x1 75.5 us: dispatch(): slot_gate = jnp.zeros((expert_count * CAP + 1,), jnp.float32).at[slot_ind...]
    pallas_call x0 -> x4, Pallas kernels: none -> 146 us  [the longest x2 106 us: combine(): pl.pallas_call(combine_kernel, grid=(groups, steps), in_specs=[pl.BlockSp...]
  transfers between devices with their start and end apart: 21 -> 37, of which waited for: 14 -> 13; matrix products, arithmetic and copies ran while one was open for 29% -> 18% of each run, Pallas kernels for 0% -> 3%
where the time goes in v1:
time: 2890 us; the launch traced here: 2870 us
  waiting for transfers between devices  1250 us (43%)
  blocking collectives  463 us (16%)
  local copies, waits for them, and re-layouts  321 us (11%)
  matrix products  281 us (10%)
  starting transfers between devices  248 us (9%)
  other arithmetic  150 us (5%)
  Pallas kernels  146 us (5%)
    reduce_scatter x2, waiting for transfers between devices, total_home(): lax.psum_scatter(partial_rows, 'col', scatter_dimension=1, tiled=True)  369 us
    all_gather x1, blocking collectives, body(): route_all = lax.all_gather(routes, 'row', axis=0)  308 us
    dot_general x22, matrix products, dot_f32(): lax.dot_general(left, right, (((left_dim,), (right_dim,)), ((), ())), pre...  260 us
    ppermute x9, waiting for transfers between devices, rows_back(): lax.ppermute(block, 'row', [(i, (i + k) % groups) for i in range(groups)])  252 us
    all_gather x2, waiting for transfers between devices, gather_all(): lax.all_gather(part_rows, 'row', axis=0, tiled=True)  194 us
    ppermute x9, starting transfers between devices, rows_back(): lax.ppermute(block, 'row', [(i, (i + k) % groups) for i in range(groups)])  182 us
    ppermute x9, waiting for transfers between devices, rows_home(): lax.ppermute(block, 'row', [(i, (i + k) % groups) for i in range(groups)])  141 us
    pallas_call x2, Pallas kernels, combine(): pl.pallas_call(combine_kernel, grid=(groups, steps), in_specs=[pl.BlockSp...  106 us
  transfers between devices with their start and end apart: 37, of which 13 were waited for; matrix products, arithmetic and copies ran while one was open for 18% of the time, Pallas kernels for 3%

profile of v1, /device:TPU:0, one launch (start us, length us, event | category | flops | bytes accessed | tf_op | source)
XLA Modules:
  0.0 2873.2 jit_solution(10003666502051839818)
XLA Ops:
  26.3 51.6 %all-gather.23.cloned.1.call-done = bf16[2560,2048]{1,0:T(8,128)(2,1)} async-done(((bf16[2560,256]{1,0:T(8,128)(2,1)}), bf16[2560,2048]{1,0:T(8,128)(2,1)}) %all-gather.23.cloned.1.call-update) | async-done | bytes 10485776 | tf_op jit(solution)/shard_map/all_gather | solution.py:427
  84.6 59.0 %all-gather.25.cloned.1.call-done = bf16[2048,768]{1,0:T(8,128)(2,1)} async-done(((bf16[512,768]{1,0:T(8,128)(2,1)}), bf16[2048,768]{1,0:T(8,128)(2,1)}) %all-gather.25.cloned.1.call-update) | async-done | bytes 3145744 | tf_op jit(solution)/shard_map/all_gather | solution.py:428
  143.6 12.7 fusion.58.q_ref.k_ref.v_ref
  173.2 17.8 tree_forward.1
  200.0 78.8 %reduce-scatter.6.cloned.1.call-done = bf16[2560,256]{1,0:T(8,128)(2,1)} async-done(((bf16[2560,2048]{1,0:T(8,128)(2,1)}), bf16[2560,256]{1,0:T(8,128)(2,1)}) %reduce-scatter.6.cloned.1.call-update) | async-done | bytes 1310736 | tf_op jit(solution)/shard_map/reduce_scatter | solution.py:447
  282.4 96.0 %all-gather.33.cloned.1.call-done = bf16[10240,256]{1,0:T(8,128)(2,1)} async-done(((bf16[2560,256]{1,0:T(8,128)(2,1)}), bf16[10240,256]{1,0:T(8,128)(2,1)}) %all-gather.33.cloned.1.call-update) | async-done | bytes 5242896 | tf_op jit(solution)/shard_map/all_gather | solution.py:396
  378.4 97.8 %all-gather.29.cloned.1.call-done = bf16[10240,256]{1,0:T(8,128)(2,1)} async-done(((bf16[2560,256]{1,0:T(8,128)(2,1)}), bf16[10240,256]{1,0:T(8,128)(2,1)}) %all-gather.29.cloned.1.call-update) | async-done | bytes 5242896 | tf_op jit(solution)/shard_map/all_gather | solution.py:396
  502.2 307.7 %all-gather.1 = s32[10240,8]{0,1:T(8,128)S(1)} all-gather(s32[2560,8]{0,1:T(8,128)S(1)} %copy-done.44), channel_id=3, replica_groups=mesh['row'=4,'col'=8] {'row'}, dimensions={0}, use_global_device_ids=true | all-gather | bytes 409600 | tf_op jit(solution)/shard_map/all_gather | solution.py:462
  810.2 11.0 reduce-window.6
  827.0 15.1 all-gather.2
  886.2 57.6 %collective-permute-done.5 = bf16[512,2048]{1,0:T(8,128)(2,1)S(1)} collective-permute-done((bf16[512,2048]{1,0:T(8,128)(2,1)}, bf16[512,2048]{1,0:T(8,128)(2,1)S(1)}, u32[]{:S(2)}, u32[]{:S(2)}) %collective-permute-start.5) | collective-permute-done | bytes 2097184 | tf_op jit(solution)/shard_map/ppermute | solution.py:355
  948.4 82.9 %collective-permute-done.1 = bf16[512,2048]{1,0:T(8,128)(2,1)} collective-permute-done((bf16[512,2048]{1,0:T(8,128)(2,1)}, bf16[512,2048]{1,0:T(8,128)(2,1)}, u32[]{:S(2)}, u32[]{:S(2)}) %collective-permute-start.1) | collective-permute-done | bytes 2097184 | tf_op jit(solution)/shard_map/ppermute | solution.py:355
  1035.9 56.8 %gather_fusion.1 = bf16[3456,2048]{1,0:T(8,128)(2,1)} fusion(bf16[10240,2048]{1,0:T(8,128)(2,1)} %all-gather.35.cloned.1.call-done, s32[4096]{0:T(1024)S(1)} %pad_clamp_fusion), kind=kCustom, calls=%fused_computation.1 | custom fusion | bytes 28325376 | tf_op jit(solution)/shard_map/gather | solution.py:487
  1101.2 12.9 fusion.12
  1114.1 9.5 fusion.10
  1123.6 57.1 %gather_fusion = bf16[3456,2048]{1,0:T(8,128)(2,1)} fusion(bf16[10240,2048]{1,0:T(8,128)(2,1)} %all-gather.31.cloned.1.call-done, s32[4096]{0:T(1024)S(1)} %pad_clamp_fusion), kind=kCustom, calls=%fused_computation | custom fusion | bytes 28325376 | tf_op jit(solution)/shard_map/gather | solution.py:483
  1197.7 12.9 fusion.17
  1210.6 9.5 fusion.25
  1220.1 19.4 multiply_convert_fusion.3
  1239.5 12.8 fusion.45
  1252.4 19.1 multiply_convert_fusion.5
  1271.5 13.2 fusion.52
  1284.7 12.5 add_convert_fusion
  1297.2 12.5 add_convert_fusion.1
  1315.7 53.2 %combine.3 = bf16[10240,2048]{1,0:T(8,128)(2,1)} custom-call(s32[10240,2]{1,0:T(8,128)} %bitcast.95, bf16[2,4,432,2048]{3,2,1,0:T(8,128)(2,1)} %pad_maximum_fusion.1.y_ref), custom_call_target="tpu_custom_call" | custom-call | flops 36238786560 | bytes 41943040 | tf_op jit(solution)/shard_map/combine/pallas_call | solution.py:326
  1369.1 369.0 %reduce-scatter.10.cloned.1.call-done = bf16[10240,256]{1,0:T(8,128)(2,1)} async-done(((bf16[10240,2048]{1,0:T(8,128)(2,1)}), bf16[10240,256]{1,0:T(8,128)(2,1)}) %reduce-scatter.10.cloned.1.call-update) | async-done | bytes 5242896 | tf_op jit(solution)/shard_map/reduce_scatter | solution.py:381
  1756.7 18.4 collective-permute-done.14
  1775.1 83.1 %collective-permute-done.13 = bf16[2560,256]{1,0:T(8,128)(2,1)} collective-permute-done((bf16[2560,256]{1,0:T(8,128)(2,1)}, bf16[2560,256]{1,0:T(8,128)(2,1)}, u32[]{:S(2)}, u32[]{:S(2)}) %collective-permute-start.13) | collective-permute-done | bytes 1310752 | tf_op jit(solution)/shard_map/ppermute | solution.py:388
  1877.0 10.8 multiply_convert_fusion
  1887.8 10.2 multiply_convert_fusion.1
  1904.1 53.2 %combine.2 = bf16[10240,2048]{1,0:T(8,128)(2,1)} custom-call(s32[10240,2]{1,0:T(8,128)} %bitcast.96, bf16[2,4,432,2048]{3,2,1,0:T(8,128)(2,1)} %pad_maximum_fusion.y_ref), custom_call_target="tpu_custom_call" | custom-call | flops 36238786560 | bytes 41943040 | tf_op jit(solution)/shard_map/combine/pallas_call | solution.py:326
  1966.5 21.6 tree_backward.1
  2005.5 9.8 subtract_convert_fusion.1
  2024.3 9.5 convolution_convert_fusion.3
  2038.0 13.2 fusion.29
  2051.3 9.9 fusion.35
  2061.2 12.8 convolution_convert_fusion
  2087.9 12.4 fusion.32
  2100.3 11.6 fusion.38
  2130.7 10.0 fusion.41
  2147.3 107.0 %collective-permute-done.16 = bf16[512,2048]{0,1:T(8,128)(2,1)} collective-permute-done((bf16[512,2048]{0,1:T(8,128)(2,1)}, bf16[512,2048]{0,1:T(8,128)(2,1)}, u32[]{:S(2)}, u32[]{:S(2)}) %collective-permute-start.16) | collective-permute-done | bytes 2097184 | tf_op jit(solution)/shard_map/ppermute | solution.py:371
  2254.3 73.9 %collective-permute-start.21 = (bf16[512,2048]{0,1:T(8,128)(2,1)}, bf16[512,2048]{0,1:T(8,128)(2,1)}, u32[]{:S(2)}, u32[]{:S(2)}) collective-permute-start(bf16[512,2048]{0,1:T(8,128)(2,1)} %get-tuple-element.106), channel_id=1, source_target_pairs={{0,8},{8,16},{16,24},{24,0},{1,9},{9,17},{17,25},{25,1},{2,10},{10... | collective-permute-start | bytes 6291464 | tf_op jit(solution)/shard_map/ppermute | solution.py:371
  2328.2 96.1 %collective-permute-start.22 = (bf16[512,2048]{0,1:T(8,128)(2,1)}, bf16[512,2048]{0,1:T(8,128)(2,1)}, u32[]{:S(2)}, u32[]{:S(2)}) collective-permute-start(bf16[512,2048]{0,1:T(8,128)(2,1)} %get-tuple-element.107), channel_id=1, source_target_pairs={{0,16},{8,24},{16,0},{24,8},{1,17},{9,25},{17,1},{25,9},{2,18},{10... | collective-permute-start | bytes 6291464 | tf_op jit(solution)/shard_map/ppermute | solution.py:371
  2447.7 10.0 broadcast.763.clone.1
  2491.0 68.0 %collective-permute-done.19 = bf16[512,2048]{0,1:T(8,128)(2,1)} collective-permute-done((bf16[512,2048]{0,1:T(8,128)(2,1)}, bf16[512,2048]{0,1:T(8,128)(2,1)}, u32[]{:S(2)}, u32[]{:S(2)}) %collective-permute-start.19) | collective-permute-done | bytes 2097184 | tf_op jit(solution)/shard_map/ppermute | solution.py:371
  2571.6 77.3 %collective-permute-done.22 = bf16[512,2048]{0,1:T(8,128)(2,1)} collective-permute-done((bf16[512,2048]{0,1:T(8,128)(2,1)}, bf16[512,2048]{0,1:T(8,128)(2,1)}, u32[]{:S(2)}, u32[]{:S(2)}) %collective-permute-start.22) | collective-permute-done | bytes 2097184 | tf_op jit(solution)/shard_map/ppermute | solution.py:371
  2691.0 46.5 %collective-permute-start.11 = (bf16[2560,256]{1,0:T(8,128)(2,1)}, bf16[2560,256]{1,0:T(8,128)(2,1)}, u32[]{:S(2)}, u32[]{:S(2)}) collective-permute-start(bf16[2560,256]{1,0:T(8,128)(2,1)} %get-tuple-element.134), channel_id=1, source_target_pairs={{0,24},{8,0},{16,8},{24,16},{1,25},{9,1},{17,9},{25,17},{2,26},{10... | collective-permute-start | bytes 3932168 | tf_op jit(solution)/shard_map/ppermute | solution.py:388
  2762.5 94.3 %all-gather.13 = f32[4,4,256]{2,1,0:T(4,128)S(1)} all-gather(f32[1,4,256]{2,1,0:T(4,128)S(1)} %maximum_bitcast_fusion.4), channel_id=9, replica_groups=mesh['row'=4,'col'=8] {'row'}, dimensions={0}, use_global_device_ids=true | all-gather | bytes 20480 | tf_op jit(solution)/shard_map/all_gather | solution.py:575
  (378 shorter events, 439.4 us)
Async XLA Ops:
  7.2 70.7 %all-gather.23.cloned.1.call-start = ((), (), s32[]{:S(2)}) async-start(), calls=%async_computation.5 | async-start | bytes 11796480 | tf_op jit(solution)/shard_map/all_gather | solution.py:427
  7.9 135.6 %all-gather.25.cloned.1.call-start = ((), (), s32[]{:S(2)}) async-start(), calls=%async_computation.6 | async-start | bytes 3932160 | tf_op jit(solution)/shard_map/all_gather | solution.py:428
  10.0 182.0 %all-gather.27.cloned.1.call-start = ((), (), s32[]{:S(2)}) async-start(), calls=%async_computation.7 | async-start | bytes 1310720 | tf_op jit(solution)/shard_map/all_gather | solution.py:431
  10.8 268.1 %reduce-scatter.6.cloned.1.call-start = ((), (), s32[]{:S(2)}) async-start(), calls=%async_computation.8 | async-start | bytes 11796480 | tf_op jit(solution)/shard_map/reduce_scatter | solution.py:447
  26.3 117.2 %copy-start.54 = (f32[2048]{0:T(1024)S(1)}, f32[2048]{0:T(1024)}, u32[]{:S(2)}) copy-start(f32[2048]{0:T(1024)} %param.17) | copy-start | bytes 24580
  199.4 179.0 %all-gather.33.cloned.1.call-start = ((), (), s32[]{:S(2)}) async-start(), calls=%async_computation.12 | async-start | bytes 6553600 | tf_op jit(solution)/shard_map/all_gather | solution.py:396
  200.0 276.3 %all-gather.29.cloned.1.call-start = ((), (), s32[]{:S(2)}) async-start(), calls=%async_computation.9 | async-start | bytes 6553600 | tf_op jit(solution)/shard_map/all_gather | solution.py:396
  282.4 753.6 %all-gather.35.cloned.1.call-start = ((), (), s32[]{:S(2)}) async-start(), calls=%async_computation.13 | async-start | bytes 47185920 | tf_op jit(solution)/shard_map/all_gather | solution.py:395
  378.4 745.2 %all-gather.31.cloned.1.call-start = ((), (), s32[]{:S(2)}) async-start(), calls=%async_computation.10 | async-start | bytes 47185920 | tf_op jit(solution)/shard_map/all_gather | solution.py:395
  476.3 1261.8 %reduce-scatter.10.cloned.1.call-start = ((), (), s32[]{:S(2)}) async-start(), calls=%async_computation.14 | async-start | bytes 47185920 | tf_op jit(solution)/shard_map/reduce_scatter | solution.py:381
  484.6 362.3 %collective-permute-start.6 = (bf16[512,2048]{1,0:T(8,128)(2,1)}, bf16[512,2048]{1,0:T(8,128)(2,1)}, u32[]{:S(2)}, u32[]{:S(2)}) collective-permute-start(bf16[512,2048]{1,0:T(8,128)(2,1)} %get-tuple-element.117), channel_id=1, source_target_pairs={{0,8},{8,16},{16,24},{24,0},{1,9},{9,17},{17,25},{25,1},{2,10},{10... | collective-permute-start | bytes 6291464 | tf_op jit(solution)/shard_map/ppermute | solution.py:355
  484.6 377.3 %collective-permute-start.7 = (bf16[512,2048]{1,0:T(8,128)(2,1)}, bf16[512,2048]{1,0:T(8,128)(2,1)}, u32[]{:S(2)}, u32[]{:S(2)}) collective-permute-start(bf16[512,2048]{1,0:T(8,128)(2,1)} %get-tuple-element.119), channel_id=1, source_target_pairs={{0,16},{8,24},{16,0},{24,8},{1,17},{9,25},{17,1},{25,9},{2,18},{10... | collective-permute-start | bytes 6291464 | tf_op jit(solution)/shard_map/ppermute | solution.py:355
  485.1 397.9 %collective-permute-start.8 = (bf16[512,2048]{1,0:T(8,128)(2,1)}, bf16[512,2048]{1,0:T(8,128)(2,1)}, u32[]{:S(2)}, u32[]{:S(2)}) collective-permute-start(bf16[512,2048]{1,0:T(8,128)(2,1)} %get-tuple-element.116), channel_id=1, source_target_pairs={{0,24},{8,0},{16,8},{24,16},{1,25},{9,1},{17,9},{25,17},{2,26},{10... | collective-permute-start | bytes 6291464 | tf_op jit(solution)/shard_map/ppermute | solution.py:355
  489.6 337.4 %copy-start.45 = (f32[2560,8]{0,1:T(8,128)S(1)}, f32[2560,8]{0,1:T(8,128)}, u32[]{:S(2)}) copy-start(f32[2560,8]{0,1:T(8,128)} %param.29) | copy-start | bytes 245764
  500.0 362.4 %collective-permute-start.3 = (bf16[512,2048]{1,0:T(8,128)(2,1)}, bf16[512,2048]{1,0:T(8,128)(2,1)}, u32[]{:S(2)}, u32[]{:S(2)}) collective-permute-start(bf16[512,2048]{1,0:T(8,128)(2,1)} %get-tuple-element.125), channel_id=1, source_target_pairs={{0,8},{8,16},{16,24},{24,0},{1,9},{9,17},{17,25},{25,1},{2,10},{10... | collective-permute-start | bytes 6291464 | tf_op jit(solution)/shard_map/ppermute | solution.py:355
  500.9 365.4 %collective-permute-start.4 = (bf16[512,2048]{1,0:T(8,128)(2,1)}, bf16[512,2048]{1,0:T(8,128)(2,1)}, u32[]{:S(2)}, u32[]{:S(2)}) collective-permute-start(bf16[512,2048]{1,0:T(8,128)(2,1)} %get-tuple-element.127), channel_id=1, source_target_pairs={{0,16},{8,24},{16,0},{24,8},{1,17},{9,25},{17,1},{25,9},{2,18},{10... | collective-permute-start | bytes 6291464 | tf_op jit(solution)/shard_map/ppermute | solution.py:355
  846.9 96.9 %collective-permute-start.5 = (bf16[512,2048]{1,0:T(8,128)(2,1)}, bf16[512,2048]{1,0:T(8,128)(2,1)S(1)}, u32[]{:S(2)}, u32[]{:S(2)}) collective-permute-start(bf16[512,2048]{1,0:T(8,128)(2,1)} %get-tuple-element.124), channel_id=1, source_target_pairs={{0,24},{8,0},{16,8},{24,16},{1,25},{9,1},{17,9},{25,17},{2,26},{10... | collective-permute-start | bytes 6291464 | tf_op jit(solution)/shard_map/ppermute | solution.py:355
  861.9 83.3 %collective-permute-start = (bf16[512,2048]{1,0:T(8,128)(2,1)}, bf16[512,2048]{1,0:T(8,128)(2,1)}, u32[]{:S(2)}, u32[]{:S(2)}) collective-permute-start(bf16[512,2048]{1,0:T(8,128)(2,1)} %get-tuple-element.121), channel_id=1, source_target_pairs={{0,8},{8,16},{16,24},{24,0},{1,9},{9,17},{17,25},{25,1},{2,10},{10... | collective-permute-start | bytes 6291464 | tf_op jit(solution)/shard_map/ppermute | solution.py:355
  862.4 168.9 %collective-permute-start.1 = (bf16[512,2048]{1,0:T(8,128)(2,1)}, bf16[512,2048]{1,0:T(8,128)(2,1)}, u32[]{:S(2)}, u32[]{:S(2)}) collective-permute-start(bf16[512,2048]{1,0:T(8,128)(2,1)} %get-tuple-element.123), channel_id=1, source_target_pairs={{0,16},{8,24},{16,0},{24,8},{1,17},{9,25},{17,1},{25,9},{2,18},{10... | collective-permute-start | bytes 6291464 | tf_op jit(solution)/shard_map/ppermute | solution.py:355
  866.4 168.1 %collective-permute-start.2 = (bf16[512,2048]{1,0:T(8,128)(2,1)}, bf16[512,2048]{1,0:T(8,128)(2,1)S(1)}, u32[]{:S(2)}, u32[]{:S(2)}) collective-permute-start(bf16[512,2048]{1,0:T(8,128)(2,1)} %get-tuple-element.120), channel_id=1, source_target_pairs={{0,24},{8,0},{16,8},{24,16},{1,25},{9,1},{17,9},{25,17},{2,26},{10... | collective-permute-start | bytes 6291464 | tf_op jit(solution)/shard_map/ppermute | solution.py:355
  1369.0 378.4 %copy-start.46 = (f32[2560]{0:T(1024)S(1)}, f32[2560]{0:T(1024)}, u32[]{:S(2)}) copy-start(f32[2560]{0:T(1024)} %get-tuple-element.96) | copy-start | bytes 30724
  1369.0 489.2 %copy-start.8 = (bf16[2560,256]{1,0:T(8,128)(2,1)S(1)}, bf16[2560,256]{1,0:T(8,128)(2,1)}, u32[]{:S(2)}) copy-start(bf16[2560,256]{1,0:T(8,128)(2,1)} %get-tuple-element.97) | copy-start | bytes 3932164
  1369.0 589.1 %all-gather.37.cloned.1.call-start = ((), (), s32[]{:S(2)}) async-start(), calls=%async_computation.15 | async-start | bytes 11796480 | tf_op jit(solution)/shard_map/all_gather | solution.py:528
  1742.2 32.9 %collective-permute-start.14 = (bf16[2560,256]{1,0:T(8,128)(2,1)}, bf16[2560,256]{1,0:T(8,128)(2,1)}, u32[]{:S(2)}, u32[]{:S(2)}) collective-permute-start(bf16[2560,256]{1,0:T(8,128)(2,1)} %get-tuple-element.131), channel_id=1, source_target_pairs={{0,24},{8,0},{16,8},{24,16},{1,25},{9,1},{17,9},{25,17},{2,26},{10... | collective-permute-start | bytes 3932168 | tf_op jit(solution)/shard_map/ppermute | solution.py:388
  1745.5 112.7 %collective-permute-start.13 = (bf16[2560,256]{1,0:T(8,128)(2,1)}, bf16[2560,256]{1,0:T(8,128)(2,1)}, u32[]{:S(2)}, u32[]{:S(2)}) collective-permute-start(bf16[2560,256]{1,0:T(8,128)(2,1)} %get-tuple-element.132), channel_id=1, source_target_pairs={{0,16},{8,24},{16,0},{24,8},{1,17},{9,25},{17,1},{25,9},{2,18},{10... | collective-permute-start | bytes 3932168 | tf_op jit(solution)/shard_map/ppermute | solution.py:388
  1745.5 112.7 %collective-permute-start.12 = (bf16[2560,256]{1,0:T(8,128)(2,1)}, bf16[2560,256]{1,0:T(8,128)(2,1)}, u32[]{:S(2)}, u32[]{:S(2)}) collective-permute-start(bf16[2560,256]{1,0:T(8,128)(2,1)} %get-tuple-element.130), channel_id=1, source_target_pairs={{0,8},{8,16},{16,24},{24,0},{1,9},{9,17},{17,25},{25,1},{2,10},{10... | collective-permute-start | bytes 3932168 | tf_op jit(solution)/shard_map/ppermute | solution.py:388
  1747.4 125.4 %copy-start.48 = (f32[256]{0:T(256)}, f32[256]{0:T(256)S(1)}, u32[]{:S(2)}) copy-start(f32[256]{0:T(256)S(1)} %dynamic_slice.126) | copy-start | bytes 3076
  1756.6 116.1 %copy-start.33 = (f32[2560]{0:T(1024)}, f32[2560]{0:T(1024)S(1)}, u32[]{:S(2)}) copy-start(f32[2560]{0:T(1024)S(1)} %get-tuple-element.152) | copy-start | bytes 30724
  1756.6 116.1 %copy-start.40 = (f32[2560]{0:T(1024)}, f32[2560]{0:T(1024)S(1)}, u32[]{:S(2)}) copy-start(f32[2560]{0:T(1024)S(1)} %get-tuple-element.151) | copy-start | bytes 30724
  1876.8 809.9 %reduce-scatter.8.cloned.1.call-start = ((), (), s32[]{:S(2)}) async-start(), calls=%async_computation.11 | async-start | bytes 47185920 | tf_op jit(solution)/shard_map/reduce_scatter | solution.py:381
  1957.3 783.4 %reduce-scatter.14.cloned.1.call-start = ((), (), s32[]{:S(2)}) async-start(), calls=%async_computation.17 | async-start | bytes 5242880 | tf_op jit(solution)/shard_map/reduce_scatter | solution.py:553
  2037.8 712.7 %reduce-scatter.12.cloned.1.call-start = ((), (), s32[]{:S(2)}) async-start(), calls=%async_computation.16 | async-start | bytes 11796480 | tf_op jit(solution)/shard_map/reduce_scatter | solution.py:547
  2082.1 63.1 %collective-permute-start.15 = (bf16[512,2048]{0,1:T(8,128)(2,1)}, bf16[512,2048]{0,1:T(8,128)(2,1)}, u32[]{:S(2)}, u32[]{:S(2)}) collective-permute-start(bf16[512,2048]{0,1:T(8,128)(2,1)} %get-tuple-element.114), channel_id=1, source_target_pairs={{0,8},{8,16},{16,24},{24,0},{1,9},{9,17},{17,25},{25,1},{2,10},{10... | collective-permute-start | bytes 6291464 | tf_op jit(solution)/shard_map/ppermute | solution.py:371
  2083.0 171.4 %collective-permute-start.16 = (bf16[512,2048]{0,1:T(8,128)(2,1)}, bf16[512,2048]{0,1:T(8,128)(2,1)}, u32[]{:S(2)}, u32[]{:S(2)}) collective-permute-start(bf16[512,2048]{0,1:T(8,128)(2,1)} %get-tuple-element.115), channel_id=1, source_target_pairs={{0,16},{8,24},{16,0},{24,8},{1,17},{9,25},{17,1},{25,9},{2,18},{10... | collective-permute-start | bytes 6291464 | tf_op jit(solution)/shard_map/ppermute | solution.py:371
  2084.9 243.3 %collective-permute-start.17 = (bf16[512,2048]{0,1:T(8,128)(2,1)}, bf16[512,2048]{0,1:T(8,128)(2,1)}, u32[]{:S(2)}, u32[]{:S(2)}) collective-permute-start(bf16[512,2048]{0,1:T(8,128)(2,1)} %get-tuple-element.112), channel_id=1, source_target_pairs={{0,24},{8,0},{16,8},{24,16},{1,25},{9,1},{17,9},{25,17},{2,26},{10... | collective-permute-start | bytes 6291464 | tf_op jit(solution)/shard_map/ppermute | solution.py:371
  2119.8 304.5 %collective-permute-start.18 = (bf16[512,2048]{0,1:T(8,128)(2,1)}, bf16[512,2048]{0,1:T(8,128)(2,1)}, u32[]{:S(2)}, u32[]{:S(2)}) collective-permute-start(bf16[512,2048]{0,1:T(8,128)(2,1)} %get-tuple-element.110), channel_id=1, source_target_pairs={{0,8},{8,16},{16,24},{24,0},{1,9},{9,17},{17,25},{25,1},{2,10},{10... | collective-permute-start | bytes 6291464 | tf_op jit(solution)/shard_map/ppermute | solution.py:371
  2119.8 439.2 %collective-permute-start.19 = (bf16[512,2048]{0,1:T(8,128)(2,1)}, bf16[512,2048]{0,1:T(8,128)(2,1)}, u32[]{:S(2)}, u32[]{:S(2)}) collective-permute-start(bf16[512,2048]{0,1:T(8,128)(2,1)} %get-tuple-element.111), channel_id=1, source_target_pairs={{0,16},{8,24},{16,0},{24,8},{1,17},{9,25},{17,1},{25,9},{2,18},{10... | collective-permute-start | bytes 6291464 | tf_op jit(solution)/shard_map/ppermute | solution.py:371
  2145.1 418.1 %collective-permute-start.20 = (bf16[512,2048]{0,1:T(8,128)(2,1)}, bf16[512,2048]{0,1:T(8,128)(2,1)}, u32[]{:S(2)}, u32[]{:S(2)}) collective-permute-start(bf16[512,2048]{0,1:T(8,128)(2,1)} %get-tuple-element.108), channel_id=1, source_target_pairs={{0,24},{8,0},{16,8},{24,16},{1,25},{9,1},{17,9},{25,17},{2,26},{10... | collective-permute-start | bytes 6291464 | tf_op jit(solution)/shard_map/ppermute | solution.py:371
  2254.3 313.1 %collective-permute-start.21 = (bf16[512,2048]{0,1:T(8,128)(2,1)}, bf16[512,2048]{0,1:T(8,128)(2,1)}, u32[]{:S(2)}, u32[]{:S(2)}) collective-permute-start(bf16[512,2048]{0,1:T(8,128)(2,1)} %get-tuple-element.106), channel_id=1, source_target_pairs={{0,8},{8,16},{16,24},{24,0},{1,9},{9,17},{17,25},{25,1},{2,10},{10... | collective-permute-start | bytes 6291464 | tf_op jit(solution)/shard_map/ppermute | solution.py:371
  2328.2 320.7 %collective-permute-start.22 = (bf16[512,2048]{0,1:T(8,128)(2,1)}, bf16[512,2048]{0,1:T(8,128)(2,1)}, u32[]{:S(2)}, u32[]{:S(2)}) collective-permute-start(bf16[512,2048]{0,1:T(8,128)(2,1)} %get-tuple-element.107), channel_id=1, source_target_pairs={{0,16},{8,24},{16,0},{24,8},{1,17},{9,25},{17,1},{25,9},{2,18},{10... | collective-permute-start | bytes 6291464 | tf_op jit(solution)/shard_map/ppermute | solution.py:371
  2424.3 228.8 %collective-permute-start.23 = (bf16[512,2048]{0,1:T(8,128)(2,1)}, bf16[512,2048]{0,1:T(8,128)(2,1)}, u32[]{:S(2)}, u32[]{:S(2)}) collective-permute-start(bf16[512,2048]{0,1:T(8,128)(2,1)} %get-tuple-element.104), channel_id=1, source_target_pairs={{0,24},{8,0},{16,8},{24,16},{1,25},{9,1},{17,9},{25,17},{2,26},{10... | collective-permute-start | bytes 6291464 | tf_op jit(solution)/shard_map/ppermute | solution.py:371
  2691.0 166.4 %collective-permute-start.11 = (bf16[2560,256]{1,0:T(8,128)(2,1)}, bf16[2560,256]{1,0:T(8,128)(2,1)}, u32[]{:S(2)}, u32[]{:S(2)}) collective-permute-start(bf16[2560,256]{1,0:T(8,128)(2,1)} %get-tuple-element.134), channel_id=1, source_target_pairs={{0,24},{8,0},{16,8},{24,16},{1,25},{9,1},{17,9},{25,17},{2,26},{10... | collective-permute-start | bytes 3932168 | tf_op jit(solution)/shard_map/ppermute | solution.py:388
  2737.5 119.9 %collective-permute-start.10 = (bf16[2560,256]{1,0:T(8,128)(2,1)}, bf16[2560,256]{1,0:T(8,128)(2,1)}, u32[]{:S(2)}, u32[]{:S(2)}) collective-permute-start(bf16[2560,256]{1,0:T(8,128)(2,1)} %get-tuple-element.135), channel_id=1, source_target_pairs={{0,16},{8,24},{16,0},{24,8},{1,17},{9,25},{17,1},{25,9},{2,18},{10... | collective-permute-start | bytes 3932168 | tf_op jit(solution)/shard_map/ppermute | solution.py:388
  2737.5 119.9 %collective-permute-start.9 = (bf16[2560,256]{1,0:T(8,128)(2,1)}, bf16[2560,256]{1,0:T(8,128)(2,1)}, u32[]{:S(2)}, u32[]{:S(2)}) collective-permute-start(bf16[2560,256]{1,0:T(8,128)(2,1)} %get-tuple-element.133), channel_id=1, source_target_pairs={{0,8},{8,16},{16,24},{24,0},{1,9},{9,17},{17,25},{25,1},{2,10},{10... | collective-permute-start | bytes 3932168 | tf_op jit(solution)/shard_map/ppermute | solution.py:388
  2743.3 114.1 %copy-start.9 = (bf16[2560,256]{1,0:T(8,128)(2,1)S(1)}, bf16[2560,256]{1,0:T(8,128)(2,1)}, u32[]{:S(2)}) copy-start(bf16[2560,256]{1,0:T(8,128)(2,1)} %get-tuple-element.97) | copy-start | bytes 3932164
  2743.3 114.1 %copy-start.34 = (f32[2560]{0:T(1024)S(1)}, f32[2560]{0:T(1024)}, u32[]{:S(2)}) copy-start(f32[2560]{0:T(1024)} %copy-done.33) | copy-start | bytes 30724
  2743.3 114.1 %copy-start.41 = (f32[2560]{0:T(1024)S(1)}, f32[2560]{0:T(1024)}, u32[]{:S(2)}) copy-start(f32[2560]{0:T(1024)} %copy-done.40) | copy-start | bytes 30724
  2743.3 114.1 %copy-start.43 = (f32[2560]{0:T(1024)S(1)}, f32[2560]{0:T(1024)}, u32[]{:S(2)}) copy-start(f32[2560]{0:T(1024)} %copy-done.42) | copy-start | bytes 30724
  (68 other events, 1122.0 us)
Sparse Core Ops, SparseCore 0:
  9.9 67.9 all-gather.22
  80.0 63.4 all-gather.24
  145.1 26.5 all-gather.26
  199.5 79.2 reduce-scatter.5
  280.3 98.0 all-gather.32
  379.8 96.4 all-gather.28
  478.2 203.8 all-gather.34
  683.9 205.4 all-gather.30
  1369.1 368.9 reduce-scatter.9
  1876.9 64.6 all-gather.36
  1957.5 244.2 reduce-scatter.7
  2203.9 183.6 reduce-scatter.13
  2391.4 127.9 reduce-scatter.11

commit v2 on v1

--- a/solution.py
+++ b/solution.py
@@ -1,3 +1,4 @@
+import functools
 import math
 
 import jax
@@ -70,6 +71,46 @@
 
 def over_col(partial_value):
     return jnp.sum(lax.all_gather(partial_value, "col", axis=0), 0)
+
+
+def after(value, *earlier):
+    return lax.optimization_barrier((value,) + earlier)[0]
+
+
+def gather_blocks(part):
+    count = lax.axis_size("col")
+
+    def swap(block, bits):
+        return lax.ppermute(block, "col", [(i, i ^ bits) for i in range(count)])
+
+    if count == 8:
+        half = part.shape[0] // 2
+        side, far, twin = swap(part, 2), swap(part, 4), swap(part, 1)
+        corner = jnp.concatenate([swap(far[:half], 2), swap(side[half:], 4)], 0)
+        return [
+            part,
+            twin,
+            side,
+            swap(side, 1),
+            far,
+            swap(far, 1),
+            corner,
+            swap(corner, 1),
+        ]
+    blocks = [part]
+    bits = 1
+    while bits < count:
+        blocks = blocks + [swap(block, bits) for block in blocks]
+        bits = bits * 2
+    return blocks
+
+
+def block_order(rows, depth):
+    own = lax.axis_index("col")
+    count = rows.shape[0] // depth
+    return jnp.concatenate(
+        [lax.dynamic_slice_in_dim(rows, (own ^ k) * depth, depth, 0) for k in range(count)], 0
+    )
 
 
 def causal(count):
@@ -308,77 +349,219 @@
     )(parents, q_rot, k_rot, values, d_attended, cos_table, sin_table)
 
 
-def combine_kernel(slot_ref, y_ref, out_ref):
-    units = y_ref.shape[0]
-    total = None
+def slots_kernel(slot_ref, gate_ref, gain_ref, x_ref, *refs, normed):
+    units = slot_ref.shape[1]
+    outs, gate_out, acc, gate_acc = refs[:units], refs[units], refs[units + 1], refs[units + 2]
+    step = pl.program_id(1)
+
+    @pl.when(step == 0)
+    def _():
+        acc[...] = jnp.zeros_like(acc)
+        gate_acc[...] = jnp.zeros_like(gate_acc)
+
     for e in range(units):
-        slots = lax.broadcasted_iota(jnp.int32, (slot_ref.shape[0], CAPP), 1)
-        picks = (slot_ref[:, e : e + 1] == slots).astype(jnp.bfloat16)
-        term = dot_f32(picks, y_ref[e, 0], 1, 0)
-        total = term if total is None else total + term
-    out_ref[...] = total.astype(out_ref.dtype)
-
-
-def combine(slot_of, slot_rows, tok_rows):
-    units, groups, _, width = slot_rows.shape
-    block = 512
+        slots = lax.broadcasted_iota(jnp.int32, (CAPP, x_ref.shape[0]), 0)
+        picks = slot_ref[0, e : e + 1, :] == slots
+        acc[e] += dot_f32(picks.astype(jnp.bfloat16), x_ref[...], 1, 0)
+        gate_acc[e] += jnp.sum(jnp.where(picks, gate_ref[0, e : e + 1, :], 0.0), 1, keepdims=True)
+
+    @pl.when(step == pl.num_programs(1) - 1)
+    def _():
+        for e in range(units):
+            rows = acc[e]
+            if normed:
+                scale = lax.rsqrt(jnp.mean(rows * rows, 1, keepdims=True) + EPS)
+                outs[e][...] = (rows * scale * gain_ref[...]).astype(jnp.bfloat16)
+            else:
+                outs[e][...] = (gate_acc[e] * rows).astype(jnp.bfloat16)
+            gate_out[e] = gate_acc[e]
+
+
+def to_slots(slot_of, token_gate, gain, rows, normed):
+    groups, units, tok_rows = slot_of.shape
+    width = rows.shape[1]
+    block = tok_rows // 2
     steps = tok_rows // block
-    return pl.pallas_call(
-        combine_kernel,
+    table = pl.BlockSpec((1, units, block), lambda g, t: (g, 0, t))
+    out = pl.pallas_call(
+        functools.partial(slots_kernel, normed=normed),
         grid=(groups, steps),
         in_specs=[
-            pl.BlockSpec((block, units), lambda g, t: (g * steps + t, 0)),
-            pl.BlockSpec((units, 1, CAPP, width), lambda g, t: (0, g, 0, 0)),
+            table,
+            table,
+            pl.BlockSpec((1, width), lambda g, t: (0, 0)),
+            pl.BlockSpec((block, width), lambda g, t: (g * steps + t, 0)),
         ],
-        out_specs=pl.BlockSpec((block, width), lambda g, t: (g * steps + t, 0)),
-        out_shape=jax.ShapeDtypeStruct((groups * tok_rows, width), jnp.bfloat16),
-        compiler_params=pltpu.CompilerParams(vmem_limit_bytes=50 * MIB),
+        out_specs=[pl.BlockSpec((CAPP, width), lambda g, t: (g, 0))] * units
+        + [pl.BlockSpec((units, CAPP, 1), lambda g, t: (0, g, 0))],
+        out_shape=[jax.ShapeDtypeStruct((groups * CAPP, width), jnp.bfloat16)] * units
+        + [jax.ShapeDtypeStruct((units, groups * CAPP, 1), jnp.float32)],
+        scratch_shapes=[
+            pltpu.VMEM((units, CAPP, width), jnp.float32),
+            pltpu.VMEM((units, CAPP, 1), jnp.float32),
+        ],
+        compiler_params=pltpu.CompilerParams(vmem_limit_bytes=56 * MIB),
         cost_estimate=pl.CostEstimate(
             flops=2 * groups * tok_rows * units * CAPP * width,
             bytes_accessed=2 * groups * tok_rows * width,
             transcendentals=0,
         ),
+        name="slots",
+    )(slot_of, token_gate, gain[None, :], rows)
+    return out[:units], out[units]
+
+
+def combine_kernel(slot_ref, *refs):
+    out_ref = refs[-1]
+    total = None
+    for e, y_ref in enumerate(refs[:-1]):
+        slots = lax.broadcasted_iota(jnp.int32, (slot_ref.shape[0], CAPP), 1)
+        picks = (slot_ref[:, e : e + 1] == slots).astype(jnp.bfloat16)
+        term = dot_f32(picks, y_ref[0], 1, 0)
+        total = term if total is None else total + term
+    out_ref[...] = total.astype(out_ref.dtype)
+
+
+def combine(slot_of, slot_rows, tok_rows, half=None):
+    units, width = len(slot_rows), slot_rows[0].shape[1]
+    groups = slot_rows[0].shape[0] // CAPP
+    block = tok_rows // 4
+    steps = 4 if half is None else 2
+    first = 0 if half is None else 2 * half
+    rows_spec = pl.BlockSpec((1, CAPP, width), lambda g, t: (g, 0, 0))
+    return pl.pallas_call(
+        combine_kernel,
+        grid=(groups, steps),
+        in_specs=[pl.BlockSpec((block, units), lambda g, t: (g * 4 + first + t, 0))]
+        + [rows_spec] * units,
+        out_specs=pl.BlockSpec((block, width), lambda g, t: (g * steps + t, 0)),
+        out_shape=jax.ShapeDtypeStruct((groups * steps * block, width), jnp.bfloat16),
+        compiler_params=pltpu.CompilerParams(vmem_limit_bytes=50 * MIB),
+        cost_estimate=pl.CostEstimate(
+            flops=2 * groups * steps * block * units * CAPP * width,
+            bytes_accessed=2 * groups * steps * block * width,
+            transcendentals=0,
+        ),
         name="combine",
-    )(slot_of, slot_rows)
-
-
-def rows_home(weight):
+    )(slot_of, *[rows.reshape(groups, CAPP, width) for rows in slot_rows])
+
+
+def shift_row(block, k):
+    count = lax.axis_size("row")
+    return lax.ppermute(block, "row", [(i, (i + k) % count) for i in range(count)])
+
+
+def row_stack(part, *earlier):
+    count = lax.axis_size("row")
+    here = lax.axis_index("row")
+    part = after(part, *earlier)
+    whole = jnp.zeros((count,) + part.shape, part.dtype)
+    for k in range(count):
+        block = part if k == 0 else shift_row(part, k)
+        whole = lax.dynamic_update_slice_in_dim(whole, block[None], (here - k) % count, 0)
+    return whole
+
+
+def crossing_units():
+    count = lax.axis_size("row")
+    units = []
+    for k in range(1, count):
+        parts = 1 if k in (1, count - 1) else 2
+        units = units + [(k, part, parts) for part in range(parts)]
+    return units
+
+
+def home_unit(weight, unit, *earlier):
+    k, part, parts = unit
+    groups = lax.axis_size("row")
+    share = weight.shape[1] // groups
+    to = (lax.axis_index("row") + k) % groups
+    block = lax.dynamic_slice_in_dim(
+        after(weight, *earlier), to * share + part * (share // parts), share // parts, 1
+    )
+    return shift_row(block, k)
+
+
+def at_home(weight, units, blocks):
     groups = lax.axis_size("row")
     here = lax.axis_index("row")
     depth, columns = weight.shape
     share = columns // groups
+    own = lax.dynamic_slice_in_dim(weight, here * share, share, 1)
     whole = jnp.zeros((depth * groups, share), weight.dtype)
-    for k in range(groups):
-        to = (here + k) % groups
-        block = lax.dynamic_slice_in_dim(weight, to * share, share, 1)
-        if k > 0:
-            block = lax.ppermute(block, "row", [(i, (i + k) % groups) for i in range(groups)])
-        whole = lax.dynamic_update_slice_in_dim(
-            whole, block, ((here - k) % groups) * depth, 0
-        )
+    whole = lax.dynamic_update_slice(whole, own, (here * depth, 0))
+    for (k, part, parts), block in zip(units, blocks):
+        row = ((here - k) % groups) * depth
+        whole = lax.dynamic_update_slice(whole, block, (row, part * (share // parts)))
     return whole
 
 
-def rows_back(grad):
+def back_units(count):
+    rows = lax.axis_size("row")
+    units = []
+    for k in range(1, rows):
+        if k in (1, rows - 1):
+            units.append((k, tuple(range(count))))
+        else:
+            units = units + [(k, (e,)) for e in range(count)]
+    return units
+
+
+def back_unit(grads, unit, *earlier):
+    k, which = unit
+    groups = lax.axis_size("row")
+    depth = grads[0].shape[0] // groups
+    to = (lax.axis_index("row") + k) % groups
+    chosen = after([grads[e] for e in which], *earlier)
+    return [
+        shift_row(lax.dynamic_slice_in_dim(grad, to * depth, depth, 0), k) for grad in chosen
+    ]
+
+
+def at_owner(grads, units, received):
     groups = lax.axis_size("row")
     here = lax.axis_index("row")
-    depth, share = grad.shape[0] // groups, grad.shape[1]
+    depth, hidden = grads[0].shape[0] // groups, grads[0].shape[1]
+    share = hidden * len(grads)
     whole = jnp.zeros((depth, share * groups), jnp.float32)
-    for k in range(groups):
-        to = (here + k) % groups
-        block = lax.dynamic_slice_in_dim(grad, to * depth, depth, 0)
-        if k > 0:
-            block = lax.ppermute(block, "row", [(i, (i + k) % groups) for i in range(groups)])
-        whole = lax.dynamic_update_slice_in_dim(
-            whole, block.astype(jnp.float32), ((here - k) % groups) * share, 1
-        )
+    for e, grad in enumerate(grads):
+        own = lax.dynamic_slice_in_dim(grad, here * depth, depth, 0).astype(jnp.float32)
+        whole = lax.dynamic_update_slice(whole, own, (0, here * share + e * hidden))
+    for (k, which), blocks in zip(units, received):
+        for e, block in zip(which, blocks):
+            start = ((here - k) % groups) * share + e * hidden
+            whole = lax.dynamic_update_slice(whole, block.astype(jnp.float32), (0, start))
     return whole
 
 
-def total_home(partial_rows):
+def line_steps(part, *earlier):
+    count = lax.axis_size("row")
+    upward = downward = part
+    steps = []
+    for _ in range(count - 1):
+        upward, downward = after((upward, downward), *earlier)
+        upward = lax.ppermute(upward, "row", [(i, i + 1) for i in range(count - 1)])
+        downward = lax.ppermute(downward, "row", [(i + 1, i) for i in range(count - 1)])
+        earlier = (upward, downward)
+        steps.append((upward, downward))
+    return steps
+
+
+def line_gather(part, steps):
+    count = lax.axis_size("row")
+    here = lax.axis_index("row")
+    rows = part.shape[0]
+    whole = jnp.zeros((rows * count, part.shape[1]), part.dtype)
+    whole = lax.dynamic_update_slice_in_dim(whole, part, here * rows, 0)
+    for k in range(1, count):
+        block = jnp.where(here >= k, steps[k - 1][0], steps[count - k - 1][1])
+        whole = lax.dynamic_update_slice_in_dim(whole, block, ((here - k) % count) * rows, 0)
+    return whole
+
+
+def group_total(part):
     groups = lax.axis_size("row")
     here = lax.axis_index("row")
-    part = lax.psum_scatter(partial_rows, "col", scatter_dimension=1, tiled=True)
     rows = part.shape[0] // groups
     total = None
     for k in range(groups):
@@ -389,12 +572,6 @@
         block = block.astype(jnp.float32)
         total = block if total is None else total + block
     return total
-
-
-def gather_all(part_rows):
-    return lax.all_gather(
-        lax.all_gather(part_rows, "row", axis=0, tiled=True), "col", axis=1, tiled=True
-    )
 
 
 def body(
@@ -424,16 +601,22 @@
     heads = own_width // HD
     trees = parents.shape[0]
 
-    whole = lax.all_gather(tokens, "col", axis=1, tiled=True)
     qkv_cols = lax.all_gather(
         jnp.concatenate([w_query, w_key, w_value], 1), "row", axis=0, tiled=True
     )
-    out_cols = lax.all_gather(w_out, "row", axis=0, tiled=True)
+    out_cols = lax.all_gather(after(w_out, qkv_cols), "row", axis=0, tiled=True)
+    shifts = crossing_units()
+    last = len(shifts) - 1
+    gate_units = [home_unit(w_gate, shifts[0], out_cols)]
+    route_all, gate_all = row_stack(routes.T, out_cols), row_stack(gates.T, out_cols)
+
+    wide = jnp.concatenate(gather_blocks(tokens), 1).astype(jnp.float32)
     cos_table, sin_table = jax.vmap(rope_tables)(parents)
     cos_table, sin_table = cos_table.reshape(-1, HD), sin_table.reshape(-1, HD)
-    wide = whole.astype(jnp.float32)
     scale_one = lax.rsqrt(jnp.mean(wide * wide, 1, keepdims=True) + EPS)
-    normed_one = (wide * scale_one * attn_norm[None, :]).astype(jnp.bfloat16)
+    norm_gain = block_order(attn_norm, own_width)
+    normed_one = (wide * scale_one * norm_gain[None, :]).astype(jnp.bfloat16)
+    qkv_cols = block_order(qkv_cols, own_width)
     qkv = jnp.dot(normed_one, qkv_cols, preferred_element_type=jnp.float32)
     query, keyed = qkv[:, :own_width], qkv[:, own_width : 2 * own_width]
     squares = over_col(jnp.stack([jnp.sum(query * query, 1), jnp.sum(keyed * keyed, 1)]))
@@ -441,81 +624,121 @@
     k_scale = lax.rsqrt(squares[1] / width + EPS)[:, None]
     q_gain = lax.dynamic_slice_in_dim(q_norm, col_start, own_width)
     k_gain = lax.dynamic_slice_in_dim(k_norm, col_start, own_width)
+    q_scale = after(q_scale, gate_units[0])
+    gate_units.append(home_unit(w_gate, shifts[1], gate_units[0]))
     attended, q_rot, k_rot, value_low = attend(
         parents, qkv, q_scale, k_scale, q_gain, k_gain, cos_table, sin_table, heads
     )
     attn_sum = lax.psum_scatter(
-        contract_cols(attended, out_cols).astype(jnp.bfloat16),
+        after(contract_cols(attended, out_cols).astype(jnp.bfloat16), gate_units[1]),
         "col",
         scatter_dimension=1,
         tiled=True,
     )
+    for unit in shifts[2:]:
+        gate_units.append(home_unit(w_gate, unit, gate_units[1]))
+    attn_sum = after(attn_sum, gate_units, route_all, gate_all)
     residual = tokens.astype(jnp.float32) + attn_sum.astype(jnp.float32)
     mid_low = residual.astype(jnp.bfloat16)
     mid_own = mid_low.astype(jnp.float32)
-    mid_all = gather_all(mid_low)
-    scale_two = lax.rsqrt(over_col(jnp.sum(mid_own * mid_own, 1)) / width + EPS)[:, None]
+    mid_row = lax.all_gather(mid_low, "row", axis=0, tiled=True)
 
     share = w_gate.shape[1] // groups
     units, hidden_units = max(1, share // FF), min(share, FF)
     first_unit = col * (w_gate.shape[1] // FF) + (here * share) // FF
-    route_all = lax.all_gather(routes, "row", axis=0)
-    gate_all = lax.all_gather(gates, "row", axis=0)
     unit_ids = first_unit + jnp.arange(units, dtype=jnp.int32)
     match = route_all[None] == unit_ids[:, None, None, None]
-    named = jnp.any(match, -1)
-    token_gate = jnp.sum(jnp.where(match, gate_all[None], 0.0), -1)
+    named = jnp.any(match, 2)
+    token_gate = jnp.sum(jnp.where(match, gate_all[None], 0.0), 2)
     rank = jnp.cumsum(named.astype(jnp.int32), 2) - 1
     slot_of = jnp.where(named, rank, -1)
-    in_slot = slot_of[:, :, None, :] == jnp.arange(CAPP, dtype=jnp.int32)[None, None, :, None]
-    slot_token = jnp.sum(
-        jnp.where(in_slot, jnp.arange(tok_rows, dtype=jnp.int32)[None, None, None, :], 0), -1
-    )
-    slot_gate = jnp.sum(jnp.where(in_slot, token_gate[:, :, None, :], 0.0), -1)
-    slot_row = slot_token + (jnp.arange(groups, dtype=jnp.int32) * tok_rows)[None, :, None]
-    slot_row = slot_row.reshape(-1)
-    slot_gate = slot_gate.reshape(units, -1)[:, :, None]
-    slot_of = slot_of.transpose(1, 2, 0).reshape(groups * tok_rows, units)
-
-    gate_home, up_home, down_home = rows_home(w_gate), rows_home(w_up), rows_home(w_down)
-    grad_all = gather_all(cotangent)
-    slots = groups * CAPP
-    slot_mid = mid_all[slot_row].astype(jnp.float32)
-    slot_scale = lax.rsqrt(jnp.mean(slot_mid * slot_mid, 1, keepdims=True) + EPS)
-    expert_in = (slot_mid * slot_scale * moe_norm[None, :]).astype(jnp.bfloat16)
-    expert_in = expert_in.reshape(units, slots, width)
-    slot_grad = grad_all[slot_row].astype(jnp.float32).reshape(units, slots, width)
-    d_out = (slot_gate * slot_grad).astype(jnp.bfloat16)
-
-    gated, d_in, gate_grads, up_grads, down_grads = [], [], [], [], []
-    for e in range(units):
-        unit = slice(e * hidden_units, (e + 1) * hidden_units)
-        x_e, d_e = expert_in[e], d_out[e]
-        gate_w, up_w, down_w = gate_home[:, unit], up_home[:, unit], down_home[:, unit]
-        gate_act = dot_f32(x_e, gate_w, 1, 0)
-        up_act = dot_f32(x_e, up_w, 1, 0)
-        sigmoid_gate = jax.nn.sigmoid(gate_act)
-        silu_gate = gate_act * sigmoid_gate
+    slot_of, token_gate = slot_of.transpose(1, 0, 2), token_gate.transpose(1, 0, 2)
+    slot_column = slot_of.transpose(0, 2, 1).reshape(groups * tok_rows, units)
+    gate_home = at_home(w_gate, shifts, gate_units)
+    mid_row, slot_of, token_gate, slot_column, gate_home = after(
+        (mid_row, slot_of, token_gate, slot_column, gate_home)
+    )
+    mid_all = lax.all_gather(mid_row, "col", axis=1, tiled=True)
+    scale_two = lax.rsqrt(over_col(jnp.sum(mid_own * mid_own, 1)) / width + EPS)[:, None]
+    grad_steps = line_steps(cotangent, mid_row)
+    grad_row = line_gather(cotangent, grad_steps)
+    up_units = [home_unit(w_up, shifts[0], grad_steps[-1])]
+    for unit in shifts[1:last]:
+        up_units.append(home_unit(w_up, unit, up_units[-1]))
+    mid_all = after(mid_all, up_units[-2])
+    grad_all = lax.all_gather(after(grad_row, mid_all), "col", axis=1, tiled=True)
+
+    experts = range(units)
+    cut = [slice(e * hidden_units, (e + 1) * hidden_units) for e in experts]
+    expert_in, slot_gate = to_slots(slot_of, token_gate, moe_norm, mid_all, True)
+    expert_in = after(expert_in, up_units[-1])
+    up_units = after(up_units, expert_in)
+    up_units.append(home_unit(w_up, shifts[last], up_units[-1], expert_in))
+    gate_acts = [dot_f32(expert_in[e], gate_home[:, cut[e]], 1, 0) for e in experts]
+    up_home, gate_acts = after((at_home(w_up, shifts, up_units), gate_acts))
+    down_units = [home_unit(w_down, shifts[0], up_home)]
+    acts = []
+    for e in experts:
+        up_act = dot_f32(expert_in[e], up_home[:, cut[e]], 1, 0)
+        sigmoid_gate = jax.nn.sigmoid(gate_acts[e])
+        silu_gate = gate_acts[e] * sigmoid_gate
         hidden = (silu_gate * up_act).astype(jnp.bfloat16)
-        down_grads.append(contract_rows(d_e, hidden).astype(jnp.bfloat16))
-        d_hidden = dot_f32(d_e, down_w, 1, 0)
+        acts.append((gate_acts[e], up_act, sigmoid_gate, silu_gate, hidden))
+    hiddens = after([act[-1] for act in acts], down_units[0])
+    for unit in shifts[1:last]:
+        down_units.append(home_unit(w_down, unit, down_units[-1], hiddens))
+    grad_all = after(grad_all, down_units[-1])
+    down_units.append(home_unit(w_down, shifts[last], grad_all))
+    d_out, _ = to_slots(slot_of, token_gate, moe_norm, grad_all, False)
+    d_out = after(d_out, down_units[-1])
+    down_grads = [contract_rows(d_out[e], hiddens[e]).astype(jnp.bfloat16) for e in experts]
+    down_home, down_grads, d_out = after(
+        (at_home(w_down, shifts, down_units), down_grads, d_out)
+    )
+
+    leaving = back_units(units)
+    down_back = [back_unit(down_grads, leaving[0], down_home)]
+    d_acts, terms = [], []
+    for e in experts:
+        gate_act, up_act, sigmoid_gate, silu_gate, _ = acts[e]
+        d_hidden = dot_f32(d_out[e], down_home[:, cut[e]], 1, 0)
         d_gate = (
             d_hidden * up_act * sigmoid_gate * (1.0 + gate_act * (1.0 - sigmoid_gate))
         ).astype(jnp.bfloat16)
-        d_up = (d_hidden * silu_gate).astype(jnp.bfloat16)
-        d_in.append(
-            (contract_cols(d_gate, gate_w) + contract_cols(d_up, up_w)).astype(jnp.bfloat16)
-        )
-        gate_grads.append(contract_rows(x_e, d_gate).astype(jnp.bfloat16))
-        up_grads.append(contract_rows(x_e, d_up).astype(jnp.bfloat16))
-        gated.append((slot_gate[e] * contract_cols(hidden, down_w)).astype(jnp.bfloat16))
-    slot_shape = (units, groups, CAPP, width)
-    d_normed_two = total_home(combine(slot_of, jnp.stack(d_in).reshape(slot_shape), tok_rows))
-    moe_sum = total_home(combine(slot_of, jnp.stack(gated).reshape(slot_shape), tok_rows))
-    output = (residual + moe_sum).astype(jnp.bfloat16)
-    w_down_grad = rows_back(jnp.concatenate(down_grads, 1))
-    w_gate_grad = rows_back(jnp.concatenate(gate_grads, 1))
-    w_up_grad = rows_back(jnp.concatenate(up_grads, 1))
+        d_acts.append((d_gate, (d_hidden * silu_gate).astype(jnp.bfloat16)))
+    for e in experts:
+        terms.append(contract_cols(d_acts[e][0], gate_home[:, cut[e]]))
+    terms, d_acts = after((terms, d_acts), down_back[0])
+    for unit in leaving[1:-1]:
+        down_back.append(back_unit(down_grads, unit, terms))
+    d_in = [
+        (terms[e] + contract_cols(d_acts[e][1], up_home[:, cut[e]])).astype(jnp.bfloat16)
+        for e in experts
+    ]
+    d_rows = combine(slot_column, d_in, tok_rows)
+    d_rows, expert_in, d_acts = after((d_rows, expert_in, d_acts), down_back)
+    down_back.append(back_unit(down_grads, leaving[-1], d_rows))
+    d_rows = lax.psum_scatter(d_rows, "col", scatter_dimension=1, tiled=True)
+    gate_grads = [contract_rows(expert_in[e], d_acts[e][0]).astype(jnp.bfloat16) for e in experts]
+    up_grads = [contract_rows(expert_in[e], d_acts[e][1]).astype(jnp.bfloat16) for e in experts]
+    gate_grads, up_grads, hiddens = after((gate_grads, up_grads, hiddens), down_back[-1])
+    gate_back = [back_unit(gate_grads, leaving[0])]
+    gate_back.append(back_unit(gate_grads, leaving[1]))
+    gated = [
+        (slot_gate[e] * contract_cols(hiddens[e], down_home[:, cut[e]])).astype(jnp.bfloat16)
+        for e in experts
+    ]
+    halves = [combine(slot_column, gated, tok_rows, half) for half in (0, 1)]
+    halves = after(halves, gate_back)
+    for unit in leaving[2:]:
+        gate_back.append(back_unit(gate_grads, unit, halves))
+    d_rows = after(d_rows, gate_back)
+    d_normed_two = group_total(d_rows)
+    halves[0] = lax.psum_scatter(
+        after(halves[0], d_rows), "col", scatter_dimension=1, tiled=True
+    )
+    w_down_grad = at_owner(down_grads, leaving, down_back)
+    w_gate_grad = at_owner(gate_grads, leaving, gate_back)
 
     gain_two = lax.dynamic_slice_in_dim(moe_norm, col_start, own_width)
     moe_dot = over_col(jnp.sum(d_normed_two * gain_two * mid_own, 1))
@@ -525,16 +748,26 @@
         - mid_own * scale_two**3 * (moe_dot / width)[:, None]
     )
     moe_gain_grad = jnp.sum(d_normed_two * mid_own * scale_two, 0)
-    d_attn_whole = lax.all_gather(d_residual.astype(jnp.bfloat16), "col", axis=1, tiled=True)
-    d_attended = jnp.dot(d_attn_whole, out_cols, preferred_element_type=jnp.float32).astype(
-        jnp.bfloat16
-    )
+    d_res_low = d_residual.astype(jnp.bfloat16)
+    up_back = [back_unit(up_grads, unit, d_normed_two) for unit in leaving[:2]]
+    d_res_low, halves[0] = after((d_res_low, halves[0]))
+    d_attn_whole = after(lax.all_gather(d_res_low, "col", axis=1, tiled=True), up_back)
+    halves[1] = lax.psum_scatter(
+        after(halves[1], d_attn_whole), "col", scatter_dimension=1, tiled=True
+    )
+    moe_sums = [group_total(after(halves[0], d_attn_whole))]
+    d_attended = jnp.dot(
+        d_attn_whole, out_cols, preferred_element_type=jnp.float32
+    ).astype(jnp.bfloat16)
     d_qn, d_kn, d_values = attend_back(
         parents, q_rot, k_rot, value_low, d_attended, cos_table, sin_table, heads
     )
     qk_dots = over_col(
         jnp.stack([jnp.sum(query * q_gain * d_qn, 1), jnp.sum(keyed * k_gain * d_kn, 1)])
     )
+    qk_dots = after(qk_dots, moe_sums[0])
+    for unit in leaving[2:-1]:
+        up_back.append(back_unit(up_grads, unit, qk_dots))
     d_query = (
         q_scale * q_gain * d_qn - query * q_scale**3 * (qk_dots[0] / width)[:, None]
     ).astype(jnp.bfloat16)
@@ -544,20 +777,23 @@
     q_gain_grad = jnp.sum(d_qn * query * q_scale, 0)
     k_gain_grad = jnp.sum(d_kn * keyed * k_scale, 0)
     d_qkv = jnp.concatenate([d_query, d_keyed, d_values], 1)
-    d_normed_one = lax.psum_scatter(
-        contract_cols(d_qkv, qkv_cols).astype(jnp.bfloat16),
-        "col",
-        scatter_dimension=1,
-        tiled=True,
-    ).astype(jnp.float32)
-    attn_grads = lax.psum_scatter(
-        jnp.concatenate(
-            [contract_rows(normed_one, d_qkv), contract_rows(d_attn_whole, attended)], 1
-        ).astype(jnp.bfloat16),
-        "row",
-        scatter_dimension=0,
-        tiled=True,
-    ).astype(jnp.float32)
+    d_one = block_order(contract_cols(qkv_cols, d_qkv).astype(jnp.bfloat16), own_width)
+    d_one = after(d_one, up_back)
+    d_qkv, attended, d_attn_whole = after((d_qkv, attended, d_attn_whole), d_one)
+    attn_grads = jnp.concatenate(
+        [
+            block_order(contract_rows(normed_one, d_qkv).astype(jnp.bfloat16), own_width),
+            contract_rows(d_attn_whole, attended).astype(jnp.bfloat16),
+        ],
+        1,
+    )
+    d_one, attn_grads, halves[1] = after((d_one, attn_grads, halves[1]))
+    d_normed_one = lax.psum_scatter(d_one, "col", scatter_dimension=0, tiled=True)
+    attn_grads = group_total(attn_grads)
+    d_normed_one = after(d_normed_one, attn_grads).astype(jnp.float32).T
+    moe_sums.append(group_total(after(halves[1], attn_grads)))
+    up_back.append(back_unit(up_grads, leaving[-1], moe_sums))
+    w_up_grad = at_owner(up_grads, leaving, up_back)
     w_query_grad = attn_grads[:, :own_width]
     w_key_grad = attn_grads[:, own_width : 2 * own_width]
     w_value_grad = attn_grads[:, 2 * own_width : 3 * own_width]
@@ -570,12 +806,11 @@
         + scale_one * gain_one * d_normed_one
         - tokens_own * scale_one**3 * (attn_dot / width)[:, None]
     )
+    moe_sum = jnp.concatenate(moe_sums, 0)
+    output = (residual + moe_sum).astype(jnp.bfloat16)
     attn_gain_grad = jnp.sum(d_normed_one * tokens_own * scale_one, 0)
     gain_grads = jnp.sum(
-        lax.all_gather(
-            jnp.stack([attn_gain_grad, q_gain_grad, k_gain_grad, moe_gain_grad]), "row", axis=0
-        ),
-        0,
+        row_stack(jnp.stack([attn_gain_grad, q_gain_grad, k_gain_grad, moe_gain_grad])), 0
     )
     return (
         output,

time: 2890 us -> 2020 us (0.70)
  blocking collectives: 463 us -> 46.5 us
  waiting for transfers between devices: 1250 us -> 981 us
  local copies, waits for them, and re-layouts: 321 us -> 183 us
  starting transfers between devices: 248 us -> 137 us
  Pallas kernels: 146 us -> 248 us
  other arithmetic: 150 us -> 114 us
    all_gather x3 -> x0, blocking collectives: 417 us -> none  [the longest x1 308 us: body(): route_all = lax.all_gather(routes, 'row', axis=0)]
    reduce_scatter x5, waiting for transfers between devices: 448 us -> 36 us  [the longest x1 27.7 us: body(): lax.psum_scatter(after(halves[0], d_rows), 'col', scatter_dimension=1, ti...]
    ppermute x24 -> x65, waiting for transfers between devices: 495 us -> 844 us  [the longest x39 568 us: shift_row(): lax.ppermute(block, 'row', [(i, (i + k) % count) for i in range(count)])]
    all_gather x7 -> x5, waiting for transfers between devices: 245 us -> 92.7 us  [the longest x1 68.4 us: body(): mid_row = lax.all_gather(mid_low, 'row', axis=0, tiled=True)]
    gather x2 -> x0, local copies, waits for them, and re-layouts: 114 us -> none  [the longest x1 57.1 us: body(): slot_mid = mid_all[slot_row].astype(jnp.float32)]
    ppermute x24 -> x65, starting transfers between devices: 247 us -> 135 us  [the longest x39 73.7 us: shift_row(): lax.ppermute(block, 'row', [(i, (i + k) % count) for i in range(count)])]
    pallas_call x0 -> x2, Pallas kernels: none -> 102 us  [to_slots(): pl.pallas_call(functools.partial(slots_kernel, normed=normed), grid=(grou...]
    convert_element_type x12 -> x0, local copies, waits for them, and re-layouts: 54.1 us -> none  [rows_back(): block.astype(jnp.float32)]
  transfers between devices with their start and end apart: 37 -> 76, of which waited for: 13 -> 44; matrix products, arithmetic and copies ran while one was open for 18% -> 26% of each run, Pallas kernels for 3% -> 12%
where the time goes in v2:
time: 2020 us; the launch traced here: 2010 us
  waiting for transfers between devices  981 us (49%)
  matrix products  286 us (14%)
  Pallas kernels  248 us (12%)
  local copies, waits for them, and re-layouts  183 us (9%)
  starting transfers between devices  137 us (7%)
  other arithmetic  114 us (6%)
  blocking collectives  46.5 us (2%)
    ppermute x39, waiting for transfers between devices, shift_row(): lax.ppermute(block, 'row', [(i, (i + k) % count) for i in range(count)])  568 us
    dot_general x22, matrix products, dot_f32(): lax.dot_general(left, right, (((left_dim,), (right_dim,)), ((), ())), pre...  262 us
    ppermute x12, waiting for transfers between devices, group_total(): lax.ppermute(block, 'row', [(i, (i + k) % groups) for i in range(groups)])  169 us
    pallas_call x3, Pallas kernels, combine(): pl.pallas_call(combine_kernel, grid=(groups, steps), in_specs=[pl.BlockSp...  107 us
    pallas_call x2, Pallas kernels, to_slots(): pl.pallas_call(functools.partial(slots_kernel, normed=normed), grid=(grou...  102 us
    ppermute x39, starting transfers between devices, shift_row(): lax.ppermute(block, 'row', [(i, (i + k) % count) for i in range(count)])  73.7 us
    all_gather x1, waiting for transfers between devices, body(): mid_row = lax.all_gather(mid_low, 'row', axis=0, tiled=True)  68.4 us
    ppermute x3, waiting for transfers between devices, line_steps(): upward = lax.ppermute(upward, 'row', [(i, i + 1) for i in range(count - 1)])  53 us
  transfers between devices with their start and end apart: 76, of which 44 were waited for; matrix products, arithmetic and copies ran while one was open for 26% of the time, Pallas kernels for 12%

profile of v2, /device:TPU:0, one launch (start us, length us, event | category | flops | bytes accessed | tf_op | source)
XLA Modules:
  0.0 2010.7 jit_solution(11174849650209121305)
XLA Ops:
  90.3 14.7 all-gather.19.cloned.1.call-done
  109.7 12.5 fusion.26.q_ref.k_ref.v_ref
  135.7 21.8 %collective-permute-done.8 = bf16[512,2048]{1,0:T(8,128)(2,1)S(1)} collective-permute-done((bf16[512,2048]{1,0:T(8,128)(2,1)}, bf16[512,2048]{1,0:T(8,128)(2,1)S(1)}, u32[]{:S(2)}, u32[]{:S(2)}) %collective-permute-start.8) | collective-permute-done | bytes 2097184 | tf_op jit(solution)/shard_map/ppermute | solution.py:451
  164.4 17.9 tree_forward.1
  189.0 18.0 collective-permute-done.9
  227.2 89.2 %collective-permute-done.10 = bf16[512,1024]{1,0:T(8,128)(2,1)} collective-permute-done((bf16[512,1024]{1,0:T(8,128)(2,1)S(1)}, bf16[512,1024]{1,0:T(8,128)(2,1)}, u32[]{:S(2)}, u32[]{:S(2)}) %collective-permute-start.10) | collective-permute-done | bytes 1048608 | tf_op jit(solution)/shard_map/ppermute | solution.py:451
  347.9 68.4 %all-gather.21.cloned.1.call-done = bf16[10240,256]{1,0:T(8,128)(2,1)} async-done(((bf16[2560,256]{1,0:T(8,128)(2,1)}), bf16[10240,256]{1,0:T(8,128)(2,1)}) %all-gather.21.cloned.1.call-update) | async-done | bytes 5242896 | tf_op jit(solution)/shard_map/all_gather | solution.py:644
  419.0 27.4 %collective-permute-done.18 = bf16[2560,256]{1,0:T(8,128)(2,1)S(1)} collective-permute-done((bf16[2560,256]{1,0:T(8,128)(2,1)}, bf16[2560,256]{1,0:T(8,128)(2,1)S(1)}, u32[]{:S(2)}, u32[]{:S(2)}) %collective-permute-start.18) | collective-permute-done | bytes 1310752 | tf_op jit(solution)/shard_map/ppermute | solution.py:543
  455.2 25.5 %collective-permute-done.20 = bf16[2560,256]{1,0:T(8,128)(2,1)S(1)} collective-permute-done((bf16[2560,256]{1,0:T(8,128)(2,1)S(1)}, bf16[2560,256]{1,0:T(8,128)(2,1)S(1)}, u32[]{:S(2)}, u32[]{:S(2)}) %collective-permute-start.20) | collective-permute-done | bytes 1310752 | tf_op jit(solution)/shard_map/ppermute | solution.py:543
  491.8 23.3 %collective-permute-done.23 = bf16[2560,256]{1,0:T(8,128)(2,1)S(1)} collective-permute-done((bf16[2560,256]{1,0:T(8,128)(2,1)S(1)}, bf16[2560,256]{1,0:T(8,128)(2,1)S(1)}, u32[]{:S(2)}, u32[]{:S(2)}) %collective-permute-start.23) | collective-permute-done | bytes 1310752 | tf_op jit(solution)/shard_map/ppermute | solution.py:544
  527.8 38.0 %collective-permute-done.24 = bf16[512,2048]{1,0:T(8,128)(2,1)} collective-permute-done((bf16[512,2048]{1,0:T(8,128)(2,1)}, bf16[512,2048]{1,0:T(8,128)(2,1)}, u32[]{:S(2)}, u32[]{:S(2)}) %collective-permute-start.24) | collective-permute-done | bytes 2097184 | tf_op jit(solution)/shard_map/ppermute | solution.py:451
  572.1 40.2 %collective-permute-done.25 = bf16[512,1024]{1,0:T(8,128)(2,1)} collective-permute-done((bf16[512,1024]{1,0:T(8,128)(2,1)}, bf16[512,1024]{1,0:T(8,128)(2,1)}, u32[]{:S(2)}, u32[]{:S(2)}) %collective-permute-start.25) | collective-permute-done | bytes 1048608 | tf_op jit(solution)/shard_map/ppermute | solution.py:451
  633.4 52.8 %slots.2 = (bf16[1728,2048]{1,0:T(8,128)(2,1)}, bf16[1728,2048]{1,0:T(8,128)(2,1)}, f32[2,1728,1]{2,1,0:T(8,128)}) custom-call(s32[4,2,2560]{2,1,0:T(2,128)} %get-tuple-element.149.slot_ref, f32[4,2,2560]{2,1,0:T(2,128)} %bitcast.131, f32[1,2048]{1,0:T(1,128)} %bitcast.142, bf16[10240,2048]{1,0:T(8,128)(2,1)} %all-gather.23.cloned.1.call-done.x_ref), custom_call_target="tpu_custom_call" | custom-call | flops 36238786560 | bytes 41943040 | tf_op jit(solution)/shard_map/slots/pallas_call | solution.py:386
  719.9 16.0 collective-permute-done.27
  739.4 15.7 multiply_convert_fusion.6
  755.1 13.3 multiply_convert_fusion.7
  768.4 18.3 collective-permute-done.28
  786.9 46.2 %collective-permute-done.29 = bf16[512,1024]{1,0:T(8,128)(2,1)} collective-permute-done((bf16[512,1024]{1,0:T(8,128)(2,1)S(1)}, bf16[512,1024]{1,0:T(8,128)(2,1)}, u32[]{:S(2)}, u32[]{:S(2)}) %collective-permute-start.29) | collective-permute-done | bytes 1048608 | tf_op jit(solution)/shard_map/ppermute | solution.py:451
  845.5 36.7 %collective-permute-done.30 = bf16[512,1024]{1,0:T(8,128)(2,1)} collective-permute-done((bf16[512,1024]{1,0:T(8,128)(2,1)}, bf16[512,1024]{1,0:T(8,128)(2,1)}, u32[]{:S(2)}, u32[]{:S(2)}) %collective-permute-start.30) | collective-permute-done | bytes 1048608 | tf_op jit(solution)/shard_map/ppermute | solution.py:451
  888.8 48.9 %slots.3 = (bf16[1728,2048]{1,0:T(8,128)(2,1)}, bf16[1728,2048]{1,0:T(8,128)(2,1)}, f32[2,1728,1]{2,1,0:T(8,128)}) custom-call(s32[4,2,2560]{2,1,0:T(2,128)} %get-tuple-element.149.slot_ref, f32[4,2,2560]{2,1,0:T(2,128)} %bitcast.132, f32[1,2048]{1,0:T(1,128)} %bitcast.143, bf16[10240,2048]{1,0:T(8,128)(2,1)} %all-gather.25.cloned.1.call-done.x_ref), custom_call_target="tpu_custom_call" | custom-call | flops 36238786560 | bytes 41943040 | tf_op jit(solution)/shard_map/slots/pallas_call | solution.py:386
  959.8 18.9 multiply_convert_fusion.2
  978.7 13.4 fusion.17
  992.1 19.4 multiply_convert_fusion.3
  1011.4 13.4 fusion.21
  1031.2 14.4 add_convert_fusion
  1045.6 13.7 add_convert_fusion.1
  1059.4 51.2 %combine.3 = bf16[10240,2048]{1,0:T(8,128)(2,1)} custom-call(s32[10240,2]{1,0:T(8,128)} %bitcast.120, bf16[4,432,2048]{2,1,0:T(8,128)(2,1)} %bitcast.151, bf16[4,432,2048]{2,1,0:T(8,128)(2,1)} %bitcast.150), custom_call_target="tpu_custom_call" | custom-call | flops 36238786560 | bytes 41943040 | tf_op jit(solution)/shard_map/combine/pallas_call | solution.py:432
  1128.0 13.7 convolution_convert_fusion.3
  1178.8 11.7 multiply_convert_fusion
  1202.1 28.1 %combine.5 = bf16[5120,2048]{1,0:T(8,128)(2,1)} custom-call(s32[10240,2]{1,0:T(8,128)} %bitcast.121, bf16[4,432,2048]{2,1,0:T(8,128)(2,1)} %bitcast.148, bf16[4,432,2048]{2,1,0:T(8,128)(2,1)} %bitcast.146), custom_call_target="tpu_custom_call" | custom-call | flops 18119393280 | bytes 20971520 | tf_op jit(solution)/shard_map/combine/pallas_call | solution.py:432
  1230.2 28.0 %combine.4 = bf16[5120,2048]{1,0:T(8,128)(2,1)} custom-call(s32[10240,2]{1,0:T(8,128)} %bitcast.122, bf16[4,432,2048]{2,1,0:T(8,128)(2,1)} %bitcast.149, bf16[4,432,2048]{2,1,0:T(8,128)(2,1)} %bitcast.147), custom_call_target="tpu_custom_call" | custom-call | flops 18119393280 | bytes 20971520 | tf_op jit(solution)/shard_map/combine/pallas_call | solution.py:432
  1273.8 19.8 collective-permute-done.43
  1293.6 22.9 %collective-permute-done.42 = bf16[512,1024]{1,0:T(8,128)(2,1)S(1)} collective-permute-done((bf16[512,1024]{1,0:T(8,128)(2,1)S(1)}, bf16[512,1024]{1,0:T(8,128)(2,1)S(1)}, u32[]{:S(2)}, u32[]{:S(2)}) %collective-permute-start.42) | collective-permute-done | bytes 1048608 | tf_op jit(solution)/shard_map/ppermute | solution.py:451
  1317.4 40.7 %collective-permute-done.41 = bf16[512,1024]{1,0:T(8,128)(2,1)} collective-permute-done((bf16[512,1024]{1,0:T(8,128)(2,1)S(1)}, bf16[512,1024]{1,0:T(8,128)(2,1)}, u32[]{:S(2)}, u32[]{:S(2)}) %collective-permute-start.41) | collective-permute-done | bytes 1048608 | tf_op jit(solution)/shard_map/ppermute | solution.py:451
  1383.9 18.6 collective-permute-done.44
  1402.5 55.0 %collective-permute-done.45 = bf16[2560,256]{1,0:T(8,128)(2,1)} collective-permute-done((bf16[2560,256]{1,0:T(8,128)(2,1)}, bf16[2560,256]{1,0:T(8,128)(2,1)}, u32[]{:S(2)}, u32[]{:S(2)}) %collective-permute-start.45) | collective-permute-done | bytes 1310752 | tf_op jit(solution)/shard_map/ppermute | solution.py:571
  1476.7 27.7 %reduce-scatter.10.cloned.1.call-done = bf16[5120,256]{1,0:T(8,128)(2,1)} async-done(((bf16[5120,2048]{1,0:T(8,128)(2,1)}), bf16[5120,256]{1,0:T(8,128)(2,1)}) %reduce-scatter.10.cloned.1.call-update) | async-done | bytes 2621456 | tf_op jit(solution)/shard_map/reduce_scatter | solution.py:737
  1512.8 86.3 %collective-permute-done.49 = bf16[512,1024]{1,0:T(8,128)(2,1)S(1)} collective-permute-done((bf16[512,1024]{1,0:T(8,128)(2,1)S(1)}, bf16[512,1024]{1,0:T(8,128)(2,1)S(1)}, u32[]{:S(2)}, u32[]{:S(2)}) %collective-permute-start.49) | collective-permute-done | bytes 1048608 | tf_op jit(solution)/shard_map/ppermute | solution.py:451
  1619.2 21.7 %tree_backward.1 = (f32[2560,256]{1,0:T(8,128)}, f32[2560,256]{1,0:T(8,128)}, bf16[2560,256]{1,0:T(8,128)(2,1)S(1)}) custom-call(s32[1,20]{1,0:T(1,128)S(1)} %copy-done.4, bf16[2560,256]{1,0:T(8,128)(2,1)S(1)} %get-tuple-element.223.qr_ref, bf16[2560,256]{1,0:T(8,128)(2,1)S(1)} %get-tuple-element.224.kr_ref, bf16[2560,256]{1,0:T(8,128)(2,1)} %get-tuple-element.225.vl_ref, ...), custom_call_target="tpu_custom_call" | custom-call | tf_op jit(solution)/shard_map/tree_backward/pallas_call | solution.py:333
  1698.3 15.0 collective-permute-done.53
  1713.3 12.7 convolution_convert_fusion.9
  1786.1 15.9 collective-permute-done.54
  1802.0 44.2 %collective-permute-done.55 = bf16[512,1024]{1,0:T(8,128)(2,1)S(1)} collective-permute-done((bf16[512,1024]{1,0:T(8,128)(2,1)S(1)}, bf16[512,1024]{1,0:T(8,128)(2,1)S(1)}, u32[]{:S(2)}, u32[]{:S(2)}) %collective-permute-start.55) | collective-permute-done | bytes 1048608 | tf_op jit(solution)/shard_map/ppermute | solution.py:571
  1847.2 23.0 %collective-permute-start.57 = (bf16[1280,256]{1,0:T(8,128)(2,1)S(1)}, bf16[1280,256]{1,0:T(8,128)(2,1)S(1)}, u32[]{:S(2)}, u32[]{:S(2)}) collective-permute-start(bf16[1280,256]{1,0:T(8,128)(2,1)S(1)} %get-tuple-element.278), channel_id=1, source_target_pairs={{0,8},{8,16},{16,24},{24,0},{1,9},{9,17},{17,25},{25,1},{2,10},{10... | collective-permute-start | bytes 1966088 | tf_op jit(solution)/shard_map/ppermute | solution.py:571
  1886.9 26.3 %collective-permute-done.58 = bf16[1280,256]{1,0:T(8,128)(2,1)S(1)} collective-permute-done((bf16[1280,256]{1,0:T(8,128)(2,1)S(1)}, bf16[1280,256]{1,0:T(8,128)(2,1)S(1)}, u32[]{:S(2)}, u32[]{:S(2)}) %collective-permute-start.58) | collective-permute-done | bytes 655392 | tf_op jit(solution)/shard_map/ppermute | solution.py:571
  1916.0 16.4 collective-permute-start.63
  1941.1 14.9 collective-permute-done.63
  1957.6 19.4 collective-permute-done.64
  (546 shorter events, 643.9 us)
Async XLA Ops:
  7.2 69.7 %all-gather.17.cloned.1.call-start = ((), (), s32[]{:S(2)}) async-start(), calls=%async_computation.5 | async-start | bytes 3932160 | tf_op jit(solution)/shard_map/all_gather | solution.py:604
  13.8 91.2 %all-gather.19.cloned.1.call-start = ((), (), s32[]{:S(2)}) async-start(), calls=%async_computation.6 | async-start | bytes 1310720 | tf_op jit(solution)/shard_map/all_gather | solution.py:607
  76.9 239.5 %reduce-scatter.6.cloned.1.call-start = ((), (), s32[]{:S(2)}) async-start(), calls=%async_computation.7 | async-start | bytes 11796480 | tf_op jit(solution)/shard_map/reduce_scatter | solution.py:632
  108.2 49.2 %collective-permute-start.8 = (bf16[512,2048]{1,0:T(8,128)(2,1)}, bf16[512,2048]{1,0:T(8,128)(2,1)S(1)}, u32[]{:S(2)}, u32[]{:S(2)}) collective-permute-start(bf16[512,2048]{1,0:T(8,128)(2,1)} %constant_dynamic-slice_fusion.41), channel_id=1, source_target_pairs={{0,8},{8,16},{16,24},{24,0},{1,9},{9,17},{17,25},{25,1},{2,10},{10... | collective-permute-start | bytes 6291464 | tf_op jit(solution)/shard_map/ppermute | solution.py:451
  160.5 46.5 %collective-permute-start.9 = (bf16[512,1024]{1,0:T(8,128)(2,1)}, bf16[512,1024]{1,0:T(8,128)(2,1)}, u32[]{:S(2)}, u32[]{:S(2)}) collective-permute-start(bf16[512,1024]{1,0:T(8,128)(2,1)} %constant_dynamic-slice_fusion.40), channel_id=1, source_target_pairs={{0,16},{8,24},{16,0},{24,8},{1,17},{9,25},{17,1},{25,9},{2,18},{10... | collective-permute-start | bytes 3145736 | tf_op jit(solution)/shard_map/ppermute | solution.py:451
  207.0 209.3 %all-gather.21.cloned.1.call-start = ((), (), s32[]{:S(2)}) async-start(), calls=%async_computation.8 | async-start | bytes 6553600 | tf_op jit(solution)/shard_map/all_gather | solution.py:644
  221.9 94.5 %collective-permute-start.11 = (bf16[512,2048]{1,0:T(8,128)(2,1)S(1)}, bf16[512,2048]{1,0:T(8,128)(2,1)}, u32[]{:S(2)}, u32[]{:S(2)}) collective-permute-start(bf16[512,2048]{1,0:T(8,128)(2,1)S(1)} %constant_dynamic-slice_fusion.38), channel_id=1, source_target_pairs={{0,24},{8,0},{16,8},{24,16},{1,25},{9,1},{17,9},{25,17},{2,26},{10... | collective-permute-start | bytes 6291464 | tf_op jit(solution)/shard_map/ppermute | solution.py:451
  226.2 90.2 %collective-permute-start.10 = (bf16[512,1024]{1,0:T(8,128)(2,1)S(1)}, bf16[512,1024]{1,0:T(8,128)(2,1)}, u32[]{:S(2)}, u32[]{:S(2)}) collective-permute-start(bf16[512,1024]{1,0:T(8,128)(2,1)S(1)} %constant_dynamic-slice_fusion.39), channel_id=1, source_target_pairs={{0,16},{8,24},{16,0},{24,8},{1,17},{9,25},{17,1},{25,9},{2,18},{10... | collective-permute-start | bytes 3145736 | tf_op jit(solution)/shard_map/ppermute | solution.py:451
  320.2 301.6 %all-gather.23.cloned.1.call-start = ((), (), s32[]{:S(2)}) async-start(), calls=%async_computation.9 | async-start | bytes 47185920 | tf_op jit(solution)/shard_map/all_gather | solution.py:661
  416.3 468.3 %all-gather.25.cloned.1.call-start = ((), (), s32[]{:S(2)}) async-start(), calls=%async_computation.10 | async-start | bytes 47185920 | tf_op jit(solution)/shard_map/all_gather | solution.py:669
  519.5 46.3 %collective-permute-start.24 = (bf16[512,2048]{1,0:T(8,128)(2,1)}, bf16[512,2048]{1,0:T(8,128)(2,1)}, u32[]{:S(2)}, u32[]{:S(2)}) collective-permute-start(bf16[512,2048]{1,0:T(8,128)(2,1)} %constant_dynamic-slice_fusion.37), channel_id=1, source_target_pairs={{0,8},{8,16},{16,24},{24,0},{1,9},{9,17},{17,25},{25,1},{2,10},{10... | collective-permute-start | bytes 6291464 | tf_op jit(solution)/shard_map/ppermute | solution.py:451
  568.1 44.2 %collective-permute-start.25 = (bf16[512,1024]{1,0:T(8,128)(2,1)}, bf16[512,1024]{1,0:T(8,128)(2,1)}, u32[]{:S(2)}, u32[]{:S(2)}) collective-permute-start(bf16[512,1024]{1,0:T(8,128)(2,1)} %constant_dynamic-slice_fusion.36), channel_id=1, source_target_pairs={{0,16},{8,24},{16,0},{24,8},{1,17},{9,25},{17,1},{25,9},{2,18},{10... | collective-permute-start | bytes 3145736 | tf_op jit(solution)/shard_map/ppermute | solution.py:451
  621.9 742.5 %reduce-scatter.8.cloned.1.call-start = ((), (), s32[]{:S(2)}) async-start(), calls=%async_computation.11 | async-start | bytes 47185920 | tf_op jit(solution)/shard_map/reduce_scatter | solution.py:721
  631.2 55.0 %collective-permute-start.26 = (bf16[512,1024]{1,0:T(8,128)(2,1)S(1)}, bf16[512,1024]{1,0:T(8,128)(2,1)S(1)}, u32[]{:S(2)}, u32[]{:S(2)}) collective-permute-start(bf16[512,1024]{1,0:T(8,128)(2,1)S(1)} %constant_dynamic-slice_fusion.35), channel_id=1, source_target_pairs={{0,16},{8,24},{16,0},{24,8},{1,17},{9,25},{17,1},{25,9},{2,18},{10... | collective-permute-start | bytes 3145736 | tf_op jit(solution)/shard_map/ppermute | solution.py:451
  688.0 47.9 %collective-permute-start.27 = (bf16[512,2048]{1,0:T(8,128)(2,1)S(1)}, bf16[512,2048]{1,0:T(8,128)(2,1)S(1)}, u32[]{:S(2)}, u32[]{:S(2)}) collective-permute-start(bf16[512,2048]{1,0:T(8,128)(2,1)S(1)} %constant_dynamic-slice_fusion.34), channel_id=1, source_target_pairs={{0,24},{8,0},{16,8},{24,16},{1,25},{9,1},{17,9},{25,17},{2,26},{10... | collective-permute-start | bytes 6291464 | tf_op jit(solution)/shard_map/ppermute | solution.py:451
  737.7 49.0 %collective-permute-start.28 = (bf16[512,2048]{1,0:T(8,128)(2,1)S(1)}, bf16[512,2048]{1,0:T(8,128)(2,1)S(1)}, u32[]{:S(2)}, u32[]{:S(2)}) collective-permute-start(bf16[512,2048]{1,0:T(8,128)(2,1)S(1)} %constant_dynamic-slice_fusion.33), channel_id=1, source_target_pairs={{0,8},{8,16},{16,24},{24,0},{1,9},{9,17},{17,25},{25,1},{2,10},{10... | collective-permute-start | bytes 6291464 | tf_op jit(solution)/shard_map/ppermute | solution.py:451
  786.8 46.3 %collective-permute-start.29 = (bf16[512,1024]{1,0:T(8,128)(2,1)S(1)}, bf16[512,1024]{1,0:T(8,128)(2,1)}, u32[]{:S(2)}, u32[]{:S(2)}) collective-permute-start(bf16[512,1024]{1,0:T(8,128)(2,1)S(1)} %constant_dynamic-slice_fusion.32), channel_id=1, source_target_pairs={{0,16},{8,24},{16,0},{24,8},{1,17},{9,25},{17,1},{25,9},{2,18},{10... | collective-permute-start | bytes 3145736 | tf_op jit(solution)/shard_map/ppermute | solution.py:451
  834.2 48.1 %collective-permute-start.30 = (bf16[512,1024]{1,0:T(8,128)(2,1)}, bf16[512,1024]{1,0:T(8,128)(2,1)}, u32[]{:S(2)}, u32[]{:S(2)}) collective-permute-start(bf16[512,1024]{1,0:T(8,128)(2,1)} %constant_dynamic-slice_fusion.31), channel_id=1, source_target_pairs={{0,16},{8,24},{16,0},{24,8},{1,17},{9,25},{17,1},{25,9},{2,18},{10... | collective-permute-start | bytes 3145736 | tf_op jit(solution)/shard_map/ppermute | solution.py:451
  886.4 51.3 %collective-permute-start.31 = (bf16[512,2048]{1,0:T(8,128)(2,1)S(1)}, bf16[512,2048]{1,0:T(8,128)(2,1)S(1)}, u32[]{:S(2)}, u32[]{:S(2)}) collective-permute-start(bf16[512,2048]{1,0:T(8,128)(2,1)S(1)} %constant_dynamic-slice_fusion.30), channel_id=1, source_target_pairs={{0,24},{8,0},{16,8},{24,16},{1,25},{9,1},{17,9},{25,17},{2,26},{10... | collective-permute-start | bytes 6291464 | tf_op jit(solution)/shard_map/ppermute | solution.py:451
  959.5 65.3 %collective-permute-start.32 = (bf16[512,1024]{1,0:T(8,128)(2,1)S(1)}, bf16[512,1024]{1,0:T(8,128)(2,1)S(1)}, u32[]{:S(2)}, u32[]{:S(2)}) collective-permute-start(bf16[512,1024]{1,0:T(8,128)(2,1)S(1)} %constant_dynamic-slice_fusion.29), channel_id=1, source_target_pairs={{0,8},{8,16},{16,24},{24,0},{1,9},{9,17},{17,25},{25,1},{2,10},{10... | collective-permute-start | bytes 3145736 | tf_op jit(solution)/shard_map/ppermute | solution.py:451
  959.8 65.0 %collective-permute-start.33 = (bf16[512,1024]{1,0:T(8,128)(2,1)S(1)}, bf16[512,1024]{1,0:T(8,128)(2,1)S(1)}, u32[]{:S(2)}, u32[]{:S(2)}) collective-permute-start(bf16[512,1024]{1,0:T(8,128)(2,1)S(1)} %constant_dynamic-slice_fusion.28), channel_id=1, source_target_pairs={{0,8},{8,16},{16,24},{24,0},{1,9},{9,17},{17,25},{25,1},{2,10},{10... | collective-permute-start | bytes 3145736 | tf_op jit(solution)/shard_map/ppermute | solution.py:451
  1026.0 84.6 %collective-permute-start.34 = (bf16[512,1024]{1,0:T(8,128)(2,1)}, bf16[512,1024]{1,0:T(8,128)(2,1)}, u32[]{:S(2)}, u32[]{:S(2)}) collective-permute-start(bf16[512,1024]{1,0:T(8,128)(2,1)} %constant_dynamic-slice_fusion.27), channel_id=1, source_target_pairs={{0,16},{8,24},{16,0},{24,8},{1,17},{9,25},{17,1},{25,9},{2,18},{10... | collective-permute-start | bytes 3145736 | tf_op jit(solution)/shard_map/ppermute | solution.py:451
  1031.2 88.9 %collective-permute-start.35 = (bf16[512,1024]{1,0:T(8,128)(2,1)}, bf16[512,1024]{1,0:T(8,128)(2,1)}, u32[]{:S(2)}, u32[]{:S(2)}) collective-permute-start(bf16[512,1024]{1,0:T(8,128)(2,1)} %constant_dynamic-slice_fusion.26), channel_id=1, source_target_pairs={{0,16},{8,24},{16,0},{24,8},{1,17},{9,25},{17,1},{25,9},{2,18},{10... | collective-permute-start | bytes 3145736 | tf_op jit(solution)/shard_map/ppermute | solution.py:451
  1120.2 384.2 %reduce-scatter.10.cloned.1.call-start = ((), (), s32[]{:S(2)}) async-start(), calls=%async_computation.12 | async-start | bytes 23592960 | tf_op jit(solution)/shard_map/reduce_scatter | solution.py:737
  1123.7 45.2 %collective-permute-start.36 = (bf16[512,1024]{1,0:T(8,128)(2,1)S(1)}, bf16[512,1024]{1,0:T(8,128)(2,1)S(1)}, u32[]{:S(2)}, u32[]{:S(2)}) collective-permute-start(bf16[512,1024]{1,0:T(8,128)(2,1)S(1)} %constant_dynamic-slice_fusion.25), channel_id=1, source_target_pairs={{0,24},{8,0},{16,8},{24,16},{1,25},{9,1},{17,9},{25,17},{2,26},{10... | collective-permute-start | bytes 3145736 | tf_op jit(solution)/shard_map/ppermute | solution.py:451
  1127.9 43.3 %collective-permute-start.37 = (bf16[512,1024]{1,0:T(8,128)(2,1)S(1)}, bf16[512,1024]{1,0:T(8,128)(2,1)S(1)}, u32[]{:S(2)}, u32[]{:S(2)}) collective-permute-start(bf16[512,1024]{1,0:T(8,128)(2,1)S(1)} %constant_dynamic-slice_fusion.24), channel_id=1, source_target_pairs={{0,24},{8,0},{16,8},{24,16},{1,25},{9,1},{17,9},{25,17},{2,26},{10... | collective-permute-start | bytes 3145736 | tf_op jit(solution)/shard_map/ppermute | solution.py:451
  1172.3 85.9 %collective-permute-start.39 = (bf16[512,1024]{1,0:T(8,128)(2,1)}, bf16[512,1024]{1,0:T(8,128)(2,1)}, u32[]{:S(2)}, u32[]{:S(2)}) collective-permute-start(bf16[512,1024]{1,0:T(8,128)(2,1)} %constant_dynamic-slice_fusion.22), channel_id=1, source_target_pairs={{0,8},{8,16},{16,24},{24,0},{1,9},{9,17},{17,25},{25,1},{2,10},{10... | collective-permute-start | bytes 3145736 | tf_op jit(solution)/shard_map/ppermute | solution.py:451
  1173.4 92.8 %collective-permute-start.40 = (bf16[512,1024]{1,0:T(8,128)(2,1)}, bf16[512,1024]{1,0:T(8,128)(2,1)}, u32[]{:S(2)}, u32[]{:S(2)}) collective-permute-start(bf16[512,1024]{1,0:T(8,128)(2,1)} %constant_dynamic-slice_fusion.21), channel_id=1, source_target_pairs={{0,16},{8,24},{16,0},{24,8},{1,17},{9,25},{17,1},{25,9},{2,18},{10... | collective-permute-start | bytes 3145736 | tf_op jit(solution)/shard_map/ppermute | solution.py:451
  1178.3 87.9 %collective-permute-start.38 = (bf16[512,1024]{1,0:T(8,128)(2,1)}, bf16[512,1024]{1,0:T(8,128)(2,1)}, u32[]{:S(2)}, u32[]{:S(2)}) collective-permute-start(bf16[512,1024]{1,0:T(8,128)(2,1)} %constant_dynamic-slice_fusion.23), channel_id=1, source_target_pairs={{0,8},{8,16},{16,24},{24,0},{1,9},{9,17},{17,25},{25,1},{2,10},{10... | collective-permute-start | bytes 3145736 | tf_op jit(solution)/shard_map/ppermute | solution.py:451
  1268.9 47.5 %collective-permute-start.42 = (bf16[512,1024]{1,0:T(8,128)(2,1)S(1)}, bf16[512,1024]{1,0:T(8,128)(2,1)S(1)}, u32[]{:S(2)}, u32[]{:S(2)}) collective-permute-start(bf16[512,1024]{1,0:T(8,128)(2,1)S(1)} %constant_dynamic-slice_fusion.19), channel_id=1, source_target_pairs={{0,24},{8,0},{16,8},{24,16},{1,25},{9,1},{17,9},{25,17},{2,26},{10... | collective-permute-start | bytes 3145736 | tf_op jit(solution)/shard_map/ppermute | solution.py:451
  1271.4 86.7 %collective-permute-start.41 = (bf16[512,1024]{1,0:T(8,128)(2,1)S(1)}, bf16[512,1024]{1,0:T(8,128)(2,1)}, u32[]{:S(2)}, u32[]{:S(2)}) collective-permute-start(bf16[512,1024]{1,0:T(8,128)(2,1)S(1)} %constant_dynamic-slice_fusion.20), channel_id=1, source_target_pairs={{0,16},{8,24},{16,0},{24,8},{1,17},{9,25},{17,1},{25,9},{2,18},{10... | collective-permute-start | bytes 3145736 | tf_op jit(solution)/shard_map/ppermute | solution.py:451
  1364.4 236.7 %all-gather.27.cloned.1.call-start = ((), (), s32[]{:S(2)}) async-start(), calls=%async_computation.13 | async-start | bytes 11796480 | tf_op jit(solution)/shard_map/all_gather | solution.py:754
  1370.1 87.5 %collective-permute-start.45 = (bf16[2560,256]{1,0:T(8,128)(2,1)}, bf16[2560,256]{1,0:T(8,128)(2,1)}, u32[]{:S(2)}, u32[]{:S(2)}) collective-permute-start(bf16[2560,256]{1,0:T(8,128)(2,1)} %get-tuple-element.274), channel_id=1, source_target_pairs={{0,16},{8,24},{16,0},{24,8},{1,17},{9,25},{17,1},{25,9},{2,18},{10... | collective-permute-start | bytes 3932168 | tf_op jit(solution)/shard_map/ppermute | solution.py:571
  1372.5 85.1 %collective-permute-start.46 = (bf16[2560,256]{1,0:T(8,128)(2,1)}, bf16[2560,256]{1,0:T(8,128)(2,1)}, u32[]{:S(2)}, u32[]{:S(2)}) collective-permute-start(bf16[2560,256]{1,0:T(8,128)(2,1)} %get-tuple-element.273), channel_id=1, source_target_pairs={{0,24},{8,0},{16,8},{24,16},{1,25},{9,1},{17,9},{25,17},{2,26},{10... | collective-permute-start | bytes 3932168 | tf_op jit(solution)/shard_map/ppermute | solution.py:571
  1504.4 231.0 %reduce-scatter.12.cloned.1.call-start = ((), (), s32[]{:S(2)}) async-start(), calls=%async_computation.14 | async-start | bytes 23592960 | tf_op jit(solution)/shard_map/reduce_scatter | solution.py:755
  1505.8 93.4 %collective-permute-start.49 = (bf16[512,1024]{1,0:T(8,128)(2,1)S(1)}, bf16[512,1024]{1,0:T(8,128)(2,1)S(1)}, u32[]{:S(2)}, u32[]{:S(2)}) collective-permute-start(bf16[512,1024]{1,0:T(8,128)(2,1)S(1)} %constant_dynamic-slice_fusion.12), channel_id=1, source_target_pairs={{0,16},{8,24},{16,0},{24,8},{1,17},{9,25},{17,1},{25,9},{2,18},{10... | collective-permute-start | bytes 3145736 | tf_op jit(solution)/shard_map/ppermute | solution.py:451
  1509.9 89.3 %collective-permute-start.48 = (bf16[512,1024]{1,0:T(8,128)(2,1)S(1)}, bf16[512,1024]{1,0:T(8,128)(2,1)S(1)}, u32[]{:S(2)}, u32[]{:S(2)}) collective-permute-start(bf16[512,1024]{1,0:T(8,128)(2,1)S(1)} %constant_dynamic-slice_fusion.13), channel_id=1, source_target_pairs={{0,8},{8,16},{16,24},{24,0},{1,9},{9,17},{17,25},{25,1},{2,10},{10... | collective-permute-start | bytes 3145736 | tf_op jit(solution)/shard_map/ppermute | solution.py:451
  1512.7 88.4 %collective-permute-start.47 = (bf16[512,1024]{1,0:T(8,128)(2,1)S(1)}, bf16[512,1024]{1,0:T(8,128)(2,1)}, u32[]{:S(2)}, u32[]{:S(2)}) collective-permute-start(bf16[512,1024]{1,0:T(8,128)(2,1)S(1)} %constant_dynamic-slice_fusion.14), channel_id=1, source_target_pairs={{0,8},{8,16},{16,24},{24,0},{1,9},{9,17},{17,25},{25,1},{2,10},{10... | collective-permute-start | bytes 3145736 | tf_op jit(solution)/shard_map/ppermute | solution.py:451
  1601.2 377.4 %reduce-scatter.14.cloned.1.call-start = ((), (), s32[]{:S(2)}) async-start(), calls=%async_computation.15 | async-start | bytes 11796480 | tf_op jit(solution)/shard_map/reduce_scatter | solution.py:791
  1604.1 51.3 %collective-permute-start.50 = (bf16[1280,256]{1,0:T(8,128)(2,1)}, bf16[1280,256]{1,0:T(8,128)(2,1)S(1)}, u32[]{:S(2)}, u32[]{:S(2)}) collective-permute-start(bf16[1280,256]{1,0:T(8,128)(2,1)} %get-tuple-element.281), channel_id=1, source_target_pairs={{0,8},{8,16},{16,24},{24,0},{1,9},{9,17},{17,25},{25,1},{2,10},{10... | collective-permute-start | bytes 1966088 | tf_op jit(solution)/shard_map/ppermute | solution.py:571
  1604.1 51.3 %collective-permute-start.51 = (bf16[1280,256]{1,0:T(8,128)(2,1)}, bf16[1280,256]{1,0:T(8,128)(2,1)}, u32[]{:S(2)}, u32[]{:S(2)}) collective-permute-start(bf16[1280,256]{1,0:T(8,128)(2,1)} %get-tuple-element.283), channel_id=1, source_target_pairs={{0,16},{8,24},{16,0},{24,8},{1,17},{9,25},{17,1},{25,9},{2,18},{10... | collective-permute-start | bytes 1966088 | tf_op jit(solution)/shard_map/ppermute | solution.py:571
  1604.9 50.5 %collective-permute-start.52 = (bf16[1280,256]{1,0:T(8,128)(2,1)}, bf16[1280,256]{1,0:T(8,128)(2,1)}, u32[]{:S(2)}, u32[]{:S(2)}) collective-permute-start(bf16[1280,256]{1,0:T(8,128)(2,1)} %get-tuple-element.282), channel_id=1, source_target_pairs={{0,24},{8,0},{16,8},{24,16},{1,25},{9,1},{17,9},{25,17},{2,26},{10... | collective-permute-start | bytes 1966088 | tf_op jit(solution)/shard_map/ppermute | solution.py:571
  1661.0 52.4 %collective-permute-start.53 = (bf16[512,1024]{1,0:T(8,128)(2,1)}, bf16[512,1024]{1,0:T(8,128)(2,1)}, u32[]{:S(2)}, u32[]{:S(2)}) collective-permute-start(bf16[512,1024]{1,0:T(8,128)(2,1)} %constant_dynamic-slice_fusion.8), channel_id=1, source_target_pairs={{0,16},{8,24},{16,0},{24,8},{1,17},{9,25},{17,1},{25,9},{2,18},{10... | collective-permute-start | bytes 3145736 | tf_op jit(solution)/shard_map/ppermute | solution.py:451
  1775.9 70.3 %collective-permute-start.55 = (bf16[512,1024]{1,0:T(8,128)(2,1)S(1)}, bf16[512,1024]{1,0:T(8,128)(2,1)S(1)}, u32[]{:S(2)}, u32[]{:S(2)}) collective-permute-start(bf16[512,1024]{1,0:T(8,128)(2,1)S(1)} %get-tuple-element.277), channel_id=1, source_target_pairs={{0,16},{8,24},{16,0},{24,8},{1,17},{9,25},{17,1},{25,9},{2,18},{10... | collective-permute-start | bytes 3145736 | tf_op jit(solution)/shard_map/ppermute | solution.py:571
  1778.3 67.9 %collective-permute-start.56 = (bf16[512,1024]{1,0:T(8,128)(2,1)S(1)}, bf16[512,1024]{1,0:T(8,128)(2,1)S(1)}, u32[]{:S(2)}, u32[]{:S(2)}) collective-permute-start(bf16[512,1024]{1,0:T(8,128)(2,1)S(1)} %get-tuple-element.276), channel_id=1, source_target_pairs={{0,24},{8,0},{16,8},{24,16},{1,25},{9,1},{17,9},{25,17},{2,26},{10... | collective-permute-start | bytes 3145736 | tf_op jit(solution)/shard_map/ppermute | solution.py:571
  1870.2 43.1 %collective-permute-start.58 = (bf16[1280,256]{1,0:T(8,128)(2,1)S(1)}, bf16[1280,256]{1,0:T(8,128)(2,1)S(1)}, u32[]{:S(2)}, u32[]{:S(2)}) collective-permute-start(bf16[1280,256]{1,0:T(8,128)(2,1)S(1)} %get-tuple-element.280), channel_id=1, source_target_pairs={{0,16},{8,24},{16,0},{24,8},{1,17},{9,25},{17,1},{25,9},{2,18},{10... | collective-permute-start | bytes 1966088 | tf_op jit(solution)/shard_map/ppermute | solution.py:571
  1871.7 41.6 %collective-permute-start.59 = (bf16[1280,256]{1,0:T(8,128)(2,1)S(1)}, bf16[1280,256]{1,0:T(8,128)(2,1)S(1)}, u32[]{:S(2)}, u32[]{:S(2)}) collective-permute-start(bf16[1280,256]{1,0:T(8,128)(2,1)S(1)} %get-tuple-element.279), channel_id=1, source_target_pairs={{0,24},{8,0},{16,8},{24,16},{1,25},{9,1},{17,9},{25,17},{2,26},{10... | collective-permute-start | bytes 1966088 | tf_op jit(solution)/shard_map/ppermute | solution.py:571
  1935.3 41.7 %collective-permute-start.64 = (bf16[512,1024]{1,0:T(8,128)(2,1)S(1)}, bf16[512,1024]{1,0:T(8,128)(2,1)S(1)}, u32[]{:S(2)}, u32[]{:S(2)}) collective-permute-start(bf16[512,1024]{1,0:T(8,128)(2,1)S(1)} %constant_dynamic-slice_fusion), channel_id=1, source_target_pairs={{0,24},{8,0},{16,8},{24,16},{1,25},{9,1},{17,9},{25,17},{2,26},{10... | collective-permute-start | bytes 3145736 | tf_op jit(solution)/shard_map/ppermute | solution.py:451
  (113 other events, 2649.6 us)
Sparse Core Ops, SparseCore 0:
  14.0 62.8 all-gather.16
  78.4 26.5 all-gather.18
  207.1 80.9 reduce-scatter.5
  320.3 95.8 all-gather.20
  418.0 203.7 all-gather.22
  624.2 205.4 all-gather.24
  1120.3 244.0 reduce-scatter.7
  1368.4 135.9 reduce-scatter.9
  1507.0 65.5 all-gather.26
  1601.3 134.0 reduce-scatter.11
  1739.3 81.5 reduce-scatter.13

commit v3 on v2

--- a/solution.py
+++ b/solution.py
@@ -482,18 +482,42 @@
     return shift_row(block, k)
 
 
+def home_kernel(here_ref, own_ref, *refs, units, groups):
+    out_ref = refs[-1]
+    source = lax.rem(here_ref[0] - pl.program_id(0) + groups, groups)
+
+    @pl.when(source == 0)
+    def _():
+        out_ref[...] = own_ref[...]
+
+    for (k, part, parts), block_ref in zip(units, refs[:-1]):
+        wide = out_ref.shape[1] // parts
+
+        @pl.when(source == k)
+        def _(block_ref=block_ref, start=part * wide, wide=wide):
+            out_ref[:, start : start + wide] = block_ref[...]
+
+
 def at_home(weight, units, blocks):
     groups = lax.axis_size("row")
-    here = lax.axis_index("row")
     depth, columns = weight.shape
     share = columns // groups
-    own = lax.dynamic_slice_in_dim(weight, here * share, share, 1)
-    whole = jnp.zeros((depth * groups, share), weight.dtype)
-    whole = lax.dynamic_update_slice(whole, own, (here * depth, 0))
-    for (k, part, parts), block in zip(units, blocks):
-        row = ((here - k) % groups) * depth
-        whole = lax.dynamic_update_slice(whole, block, (row, part * (share // parts)))
-    return whole
+    return pl.pallas_call(
+        functools.partial(home_kernel, units=units, groups=groups),
+        grid_spec=pltpu.PrefetchScalarGridSpec(
+            num_scalar_prefetch=1,
+            grid=(groups,),
+            in_specs=[pl.BlockSpec((depth, share), lambda j, here: (0, here[0]))]
+            + [pl.BlockSpec(block.shape, lambda j, here: (0, 0)) for block in blocks],
+            out_specs=pl.BlockSpec((depth, share), lambda j, here: (j, 0)),
+        ),
+        out_shape=jax.ShapeDtypeStruct((depth * groups, share), weight.dtype),
+        compiler_params=pltpu.CompilerParams(vmem_limit_bytes=50 * MIB),
+        cost_estimate=pl.CostEstimate(
+            flops=0, bytes_accessed=4 * depth * columns, transcendentals=0
+        ),
+        name="at_home",
+    )(lax.axis_index("row").astype(jnp.int32)[None], weight, *blocks)
 
 
 def back_units(count):
@@ -518,20 +542,41 @@
     ]
 
 
+def owner_kernel(here_ref, *refs, units, groups, count):
+    out_ref = refs[-1]
+    hidden = refs[0].shape[1]
+    source = lax.rem(here_ref[0] - pl.program_id(0) + groups, groups)
+    places = [(0, e) for e in range(count)]
+    places = places + [(k, e) for k, which in units for e in which]
+    for (k, e), block_ref in zip(places, refs[:-1]):
+
+        @pl.when(source == k)
+        def _(block_ref=block_ref, start=e * hidden):
+            out_ref[:, start : start + hidden] = block_ref[...].astype(jnp.float32)
+
+
 def at_owner(grads, units, received):
     groups = lax.axis_size("row")
-    here = lax.axis_index("row")
     depth, hidden = grads[0].shape[0] // groups, grads[0].shape[1]
-    share = hidden * len(grads)
-    whole = jnp.zeros((depth, share * groups), jnp.float32)
-    for e, grad in enumerate(grads):
-        own = lax.dynamic_slice_in_dim(grad, here * depth, depth, 0).astype(jnp.float32)
-        whole = lax.dynamic_update_slice(whole, own, (0, here * share + e * hidden))
-    for (k, which), blocks in zip(units, received):
-        for e, block in zip(which, blocks):
-            start = ((here - k) % groups) * share + e * hidden
-            whole = lax.dynamic_update_slice(whole, block.astype(jnp.float32), (0, start))
-    return whole
+    count = len(grads)
+    share = hidden * count
+    blocks = [block for pair in received for block in pair]
+    return pl.pallas_call(
+        functools.partial(owner_kernel, units=units, groups=groups, count=count),
+        grid_spec=pltpu.PrefetchScalarGridSpec(
+            num_scalar_prefetch=1,
+            grid=(groups,),
+            in_specs=[pl.BlockSpec((depth, hidden), lambda j, here: (here[0], 0))] * count
+            + [pl.BlockSpec((depth, hidden), lambda j, here: (0, 0))] * len(blocks),
+            out_specs=pl.BlockSpec((depth, share), lambda j, here: (0, j)),
+        ),
+        out_shape=jax.ShapeDtypeStruct((depth, share * groups), jnp.float32),
+        compiler_params=pltpu.CompilerParams(vmem_limit_bytes=50 * MIB),
+        cost_estimate=pl.CostEstimate(
+            flops=0, bytes_accessed=6 * depth * share * groups, transcendentals=0
+        ),
+        name="at_owner",
+    )(lax.axis_index("row").astype(jnp.int32)[None], *grads, *blocks)
 
 
 def line_steps(part, *earlier):
@@ -559,19 +604,24 @@
     return whole
 
 
-def group_total(part):
+def group_total(part, along=()):
     groups = lax.axis_size("row")
     here = lax.axis_index("row")
     rows = part.shape[0] // groups
-    total = None
-    for k in range(groups):
-        to = (here + k) % groups
-        block = lax.dynamic_slice_in_dim(part, to * rows, rows, 0)
-        if k > 0:
-            block = lax.ppermute(block, "row", [(i, (i + k) % groups) for i in range(groups)])
-        block = block.astype(jnp.float32)
-        total = block if total is None else total + block
-    return total
+
+    def rows_of(group):
+        start = jnp.clip(group, 0, groups - 1) * rows
+        return lax.dynamic_slice_in_dim(part, start, rows, 0).astype(jnp.float32)
+
+    upward = downward = 0.0
+    for step in range(1, groups):
+        upward = (rows_of(here + groups - step) + upward).astype(jnp.bfloat16)
+        downward = (rows_of(here - groups + step) + downward).astype(jnp.bfloat16)
+        upward = lax.ppermute(upward, "row", [(i, i + 1) for i in range(step)])
+        downward = lax.ppermute(downward, "row", [(groups - 1 - i, groups - 2 - i) for i in range(step)])
+        upward, downward = after((upward, downward), *(along if step == groups - 2 else ()))
+        upward, downward = upward.astype(jnp.float32), downward.astype(jnp.float32)
+    return rows_of(here) + upward + downward
 
 
 def body(
@@ -607,8 +657,7 @@
     out_cols = lax.all_gather(after(w_out, qkv_cols), "row", axis=0, tiled=True)
     shifts = crossing_units()
     last = len(shifts) - 1
-    gate_units = [home_unit(w_gate, shifts[0], out_cols)]
-    route_all, gate_all = row_stack(routes.T, out_cols), row_stack(gates.T, out_cols)
+    grad_steps = line_steps(cotangent, qkv_cols)
 
     wide = jnp.concatenate(gather_blocks(tokens), 1).astype(jnp.float32)
     cos_table, sin_table = jax.vmap(rope_tables)(parents)
@@ -624,24 +673,26 @@
     k_scale = lax.rsqrt(squares[1] / width + EPS)[:, None]
     q_gain = lax.dynamic_slice_in_dim(q_norm, col_start, own_width)
     k_gain = lax.dynamic_slice_in_dim(k_norm, col_start, own_width)
-    q_scale = after(q_scale, gate_units[0])
-    gate_units.append(home_unit(w_gate, shifts[1], gate_units[0]))
+    q_scale = after(q_scale, grad_steps[0])
     attended, q_rot, k_rot, value_low = attend(
         parents, qkv, q_scale, k_scale, q_gain, k_gain, cos_table, sin_table, heads
     )
     attn_sum = lax.psum_scatter(
-        after(contract_cols(attended, out_cols).astype(jnp.bfloat16), gate_units[1]),
+        after(contract_cols(attended, out_cols).astype(jnp.bfloat16), grad_steps[:-1]),
         "col",
         scatter_dimension=1,
         tiled=True,
     )
-    for unit in shifts[2:]:
-        gate_units.append(home_unit(w_gate, unit, gate_units[1]))
-    attn_sum = after(attn_sum, gate_units, route_all, gate_all)
+    route_all = row_stack(routes.T, grad_steps[:-1])
+    gate_all = row_stack(gates.T, grad_steps[:-1])
+    gate_units = [home_unit(w_gate, shifts[0], grad_steps[:-1])]
+    attn_sum = after(attn_sum, gate_units, grad_steps, route_all, gate_all)
     residual = tokens.astype(jnp.float32) + attn_sum.astype(jnp.float32)
     mid_low = residual.astype(jnp.bfloat16)
     mid_own = mid_low.astype(jnp.float32)
     mid_row = lax.all_gather(mid_low, "row", axis=0, tiled=True)
+    gate_units.append(home_unit(w_gate, shifts[1], mid_low))
+    grad_row = line_gather(cotangent, grad_steps)
 
     share = w_gate.shape[1] // groups
     units, hidden_units = max(1, share // FF), min(share, FF)
@@ -654,18 +705,18 @@
     slot_of = jnp.where(named, rank, -1)
     slot_of, token_gate = slot_of.transpose(1, 0, 2), token_gate.transpose(1, 0, 2)
     slot_column = slot_of.transpose(0, 2, 1).reshape(groups * tok_rows, units)
-    gate_home = at_home(w_gate, shifts, gate_units)
-    mid_row, slot_of, token_gate, slot_column, gate_home = after(
-        (mid_row, slot_of, token_gate, slot_column, gate_home)
+    mid_row, slot_of, token_gate, slot_column, grad_row = after(
+        (mid_row, slot_of, token_gate, slot_column, grad_row), gate_units
     )
     mid_all = lax.all_gather(mid_row, "col", axis=1, tiled=True)
     scale_two = lax.rsqrt(over_col(jnp.sum(mid_own * mid_own, 1)) / width + EPS)[:, None]
-    grad_steps = line_steps(cotangent, mid_row)
-    grad_row = line_gather(cotangent, grad_steps)
-    up_units = [home_unit(w_up, shifts[0], grad_steps[-1])]
+    for unit in shifts[2:]:
+        gate_units.append(home_unit(w_gate, unit, gate_units[-1], mid_row))
+    gate_home = at_home(w_gate, shifts, gate_units)
+    up_units = [home_unit(w_up, shifts[0], gate_units[-1])]
     for unit in shifts[1:last]:
         up_units.append(home_unit(w_up, unit, up_units[-1]))
-    mid_all = after(mid_all, up_units[-2])
+    mid_all, gate_home = after((mid_all, gate_home), up_units[-2])
     grad_all = lax.all_gather(after(grad_row, mid_all), "col", axis=1, tiled=True)
 
     experts = range(units)
@@ -685,19 +736,19 @@
         hidden = (silu_gate * up_act).astype(jnp.bfloat16)
         acts.append((gate_acts[e], up_act, sigmoid_gate, silu_gate, hidden))
     hiddens = after([act[-1] for act in acts], down_units[0])
-    for unit in shifts[1:last]:
-        down_units.append(home_unit(w_down, unit, down_units[-1], hiddens))
-    grad_all = after(grad_all, down_units[-1])
-    down_units.append(home_unit(w_down, shifts[last], grad_all))
+    down_units.append(home_unit(w_down, shifts[1], hiddens))
+    grad_all = after(grad_all, down_units[1])
+    for unit in shifts[2:last]:
+        down_units.append(home_unit(w_down, unit, grad_all))
     d_out, _ = to_slots(slot_of, token_gate, moe_norm, grad_all, False)
     d_out = after(d_out, down_units[-1])
+    down_units.append(home_unit(w_down, shifts[last], d_out))
     down_grads = [contract_rows(d_out[e], hiddens[e]).astype(jnp.bfloat16) for e in experts]
-    down_home, down_grads, d_out = after(
-        (at_home(w_down, shifts, down_units), down_grads, d_out)
-    )
+    down_grads, d_out, down_units = after((down_grads, d_out, down_units))
+    down_home = at_home(w_down, shifts, down_units)
 
     leaving = back_units(units)
-    down_back = [back_unit(down_grads, leaving[0], down_home)]
+    down_back = [back_unit(down_grads, leaving[0])]
     d_acts, terms = [], []
     for e in experts:
         gate_act, up_act, sigmoid_gate, silu_gate, _ = acts[e]
@@ -733,7 +784,8 @@
     for unit in leaving[2:]:
         gate_back.append(back_unit(gate_grads, unit, halves))
     d_rows = after(d_rows, gate_back)
-    d_normed_two = group_total(d_rows)
+    up_back = [back_unit(up_grads, leaving[0], d_rows)]
+    d_normed_two = group_total(d_rows, up_back[0])
     halves[0] = lax.psum_scatter(
         after(halves[0], d_rows), "col", scatter_dimension=1, tiled=True
     )
@@ -749,9 +801,10 @@
     )
     moe_gain_grad = jnp.sum(d_normed_two * mid_own * scale_two, 0)
     d_res_low = d_residual.astype(jnp.bfloat16)
-    up_back = [back_unit(up_grads, unit, d_normed_two) for unit in leaving[:2]]
-    d_res_low, halves[0] = after((d_res_low, halves[0]))
-    d_attn_whole = after(lax.all_gather(d_res_low, "col", axis=1, tiled=True), up_back)
+    up_back.append(back_unit(up_grads, leaving[1], d_normed_two))
+    d_res_low, halves[0], w_down_grad = after((d_res_low, halves[0], w_down_grad))
+    d_attn_whole = lax.all_gather(d_res_low, "col", axis=1, tiled=True)
+    d_attn_whole, w_gate_grad = after((d_attn_whole, w_gate_grad), up_back)
     halves[1] = lax.psum_scatter(
         after(halves[1], d_attn_whole), "col", scatter_dimension=1, tiled=True
     )
@@ -765,9 +818,10 @@
     qk_dots = over_col(
         jnp.stack([jnp.sum(query * q_gain * d_qn, 1), jnp.sum(keyed * k_gain * d_kn, 1)])
     )
-    qk_dots = after(qk_dots, moe_sums[0])
-    for unit in leaving[2:-1]:
-        up_back.append(back_unit(up_grads, unit, qk_dots))
+    up_back.append(back_unit(up_grads, leaving[2], d_attn_whole))
+    qk_dots = after(qk_dots, moe_sums[0], up_back)
+    for unit in leaving[3:]:
+        up_back.append(back_unit(up_grads, unit, up_back[2], qk_dots))
     d_query = (
         q_scale * q_gain * d_qn - query * q_scale**3 * (qk_dots[0] / width)[:, None]
     ).astype(jnp.bfloat16)
@@ -778,7 +832,6 @@
     k_gain_grad = jnp.sum(d_kn * keyed * k_scale, 0)
     d_qkv = jnp.concatenate([d_query, d_keyed, d_values], 1)
     d_one = block_order(contract_cols(qkv_cols, d_qkv).astype(jnp.bfloat16), own_width)
-    d_one = after(d_one, up_back)
     d_qkv, attended, d_attn_whole = after((d_qkv, attended, d_attn_whole), d_one)
     attn_grads = jnp.concatenate(
         [
@@ -787,13 +840,13 @@
         ],
         1,
     )
-    d_one, attn_grads, halves[1] = after((d_one, attn_grads, halves[1]))
+    d_one, attn_grads, halves[1] = after((d_one, attn_grads, halves[1]), up_back[-1])
+    w_up_grad = at_owner(up_grads, leaving, up_back)
     d_normed_one = lax.psum_scatter(d_one, "col", scatter_dimension=0, tiled=True)
     attn_grads = group_total(attn_grads)
-    d_normed_one = after(d_normed_one, attn_grads).astype(jnp.float32).T
-    moe_sums.append(group_total(after(halves[1], attn_grads)))
-    up_back.append(back_unit(up_grads, leaving[-1], moe_sums))
-    w_up_grad = at_owner(up_grads, leaving, up_back)
+    moe_sums.append(group_total(halves[1]))
+    d_normed_one, w_up_grad = after((d_normed_one, w_up_grad))
+    d_normed_one = d_normed_one.astype(jnp.float32).T
     w_query_grad = attn_grads[:, :own_width]
     w_key_grad = attn_grads[:, own_width : 2 * own_width]
     w_value_grad = attn_grads[:, 2 * own_width : 3 * own_width]
@@ -806,12 +859,12 @@
         + scale_one * gain_one * d_normed_one
         - tokens_own * scale_one**3 * (attn_dot / width)[:, None]
     )
-    moe_sum = jnp.concatenate(moe_sums, 0)
-    output = (residual + moe_sum).astype(jnp.bfloat16)
     attn_gain_grad = jnp.sum(d_normed_one * tokens_own * scale_one, 0)
     gain_grads = jnp.sum(
         row_stack(jnp.stack([attn_gain_grad, q_gain_grad, k_gain_grad, moe_gain_grad])), 0
     )
+    moe_sum = after(jnp.concatenate(moe_sums, 0), gain_grads)
+    output = (residual + moe_sum).astype(jnp.bfloat16)
     return (
         output,
         tokens_grad,

time: 2020 us -> 1920 us (0.950)
  waiting for transfers between devices: 981 us -> 884 us
  local copies, waits for them, and re-layouts: 183 us -> 116 us
  Pallas kernels: 248 us -> 295 us
  starting transfers between devices: 137 us -> 162 us
    ppermute x12 -> x24, waiting for transfers between devices: 169 us -> 89.1 us  [the longest x12 83.7 us: group_total(): upward = lax.ppermute(upward, 'row', [(i, i + 1) for i in range(step)])]
    ppermute x39, waiting for transfers between devices: 568 us -> 621 us  [shift_row(): lax.ppermute(block, 'row', [(i, (i + k) % count) for i in range(count)])]
    all_gather x1, waiting for transfers between devices: 68.4 us -> 16.3 us  [body(): mid_row = lax.all_gather(mid_low, 'row', axis=0, tiled=True)]
    pallas_call x0 -> x6, Pallas kernels: none -> 47.9 us  [the longest x3 27.5 us: at_owner(): pl.pallas_call(functools.partial(owner_kernel, units=units, groups=groups...]
    ppermute x12 -> x24, starting transfers between devices: 40.5 us -> 82.6 us  [the longest x12 68.2 us: group_total(): upward = lax.ppermute(upward, 'row', [(i, i + 1) for i in range(step)])]
    dynamic_update_slice x24 -> x0, other arithmetic: 38.6 us -> none  [the longest x18 26.7 us: at_owner(): lax.dynamic_update_slice(whole, block.astype(jnp.float32), (0, start))]
    dynamic_update_slice x15 -> x0, local copies, waits for them, and re-layouts: 36.8 us -> none  [the longest x12 26.9 us: at_home(): lax.dynamic_update_slice(whole, block, (row, part * (share // parts)))]
    convert_element_type x0 -> x8, other arithmetic: none -> 29.3 us  [group_total(): downward = (rows_of(here - groups + step) + downward).astype(jnp.bfloat16)]
  transfers between devices with their start and end apart: 76 -> 88, of which waited for: 44 -> 43; matrix products, arithmetic and copies ran while one was open for 26% -> 24% of each run, Pallas kernels for 12% -> 15%
where the time goes in v3:
time: 1920 us; the launch traced here: 1910 us
  waiting for transfers between devices  884 us (46%)
  Pallas kernels  295 us (15%)
  matrix products  280 us (15%)
  starting transfers between devices  162 us (8%)
  local copies, waits for them, and re-layouts  116 us (6%)
  other arithmetic  107 us (6%)
  blocking collectives  45.9 us (2%)
    ppermute x39, waiting for transfers between devices, shift_row(): lax.ppermute(block, 'row', [(i, (i + k) % count) for i in range(count)])  621 us
    dot_general x22, matrix products, dot_f32(): lax.dot_general(left, right, (((left_dim,), (right_dim,)), ((), ())), pre...  259 us
    pallas_call x3, Pallas kernels, combine(): pl.pallas_call(combine_kernel, grid=(groups, steps), in_specs=[pl.BlockSp...  107 us
    pallas_call x2, Pallas kernels, to_slots(): pl.pallas_call(functools.partial(slots_kernel, normed=normed), grid=(grou...  100 us
    ppermute x12, waiting for transfers between devices, group_total(): upward = lax.ppermute(upward, 'row', [(i, i + 1) for i in range(step)])  83.7 us
    ppermute x12, starting transfers between devices, group_total(): upward = lax.ppermute(upward, 'row', [(i, i + 1) for i in range(step)])  68.2 us
    ppermute x39, starting transfers between devices, shift_row(): lax.ppermute(block, 'row', [(i, (i + k) % count) for i in range(count)])  55.6 us
    ppermute x3, waiting for transfers between devices, line_steps(): lax.ppermute(downward, 'row', [(i + 1, i) for i in range(count - 1)])  52.7 us
  transfers between devices with their start and end apart: 88, of which 43 were waited for; matrix products, arithmetic and copies ran while one was open for 24% of the time, Pallas kernels for 15%

profile of v3, /device:TPU:0, one launch (start us, length us, event | category | flops | bytes accessed | tf_op | source)
XLA Modules:
  0.0 1906.5 jit_solution(2237595206204598348)
XLA Ops:
  85.6 12.6 fusion.26.q_ref.k_ref.v_ref
  102.1 21.5 %collective-permute-done.8 = bf16[2560,256]{1,0:T(8,128)(2,1)} collective-permute-done((bf16[2560,256]{1,0:T(8,128)(2,1)S(1)}, bf16[2560,256]{1,0:T(8,128)(2,1)}, u32[]{:S(2)}, u32[]{:S(2)}) %collective-permute-start.8) | collective-permute-done | bytes 1310752 | tf_op jit(solution)/shard_map/ppermute | solution.py:588
  147.1 17.8 tree_forward.1
  199.3 25.7 %collective-permute-done.13 = bf16[2560,256]{1,0:T(8,128)(2,1)} collective-permute-done((bf16[2560,256]{1,0:T(8,128)(2,1)}, bf16[2560,256]{1,0:T(8,128)(2,1)}, u32[]{:S(2)}, u32[]{:S(2)}) %collective-permute-start.13) | collective-permute-done | bytes 1310752 | tf_op jit(solution)/shard_map/ppermute | solution.py:588
  224.9 47.4 %collective-permute-done.14 = bf16[2560,256]{1,0:T(8,128)(2,1)} collective-permute-done((bf16[2560,256]{1,0:T(8,128)(2,1)}, bf16[2560,256]{1,0:T(8,128)(2,1)}, u32[]{:S(2)}, u32[]{:S(2)}) %collective-permute-start.14) | collective-permute-done | bytes 1310752 | tf_op jit(solution)/shard_map/ppermute | solution.py:589
  298.1 101.5 %collective-permute-done.21.refs_1_ = bf16[512,1024]{1,0:T(8,128)(2,1)S(1)} collective-permute-done((bf16[512,1024]{1,0:T(8,128)(2,1)S(1)}, bf16[512,1024]{1,0:T(8,128)(2,1)S(1)}, u32[]{:S(2)}, u32[]{:S(2)}) %collective-permute-start.21) | collective-permute-done | bytes 1048608 | tf_op jit(solution)/shard_map/ppermute | solution.py:451
  399.6 16.3 all-gather.21.cloned.1.call-done
  417.4 46.3 %collective-permute-done.22.refs_2_ = bf16[512,1024]{1,0:T(8,128)(2,1)} collective-permute-done((bf16[512,1024]{1,0:T(8,128)(2,1)S(1)}, bf16[512,1024]{1,0:T(8,128)(2,1)}, u32[]{:S(2)}, u32[]{:S(2)}) %collective-permute-start.22) | collective-permute-done | bytes 1048608 | tf_op jit(solution)/shard_map/ppermute | solution.py:451
  468.3 44.9 %collective-permute-done.23.refs_3_ = bf16[512,2048]{1,0:T(8,128)(2,1)S(1)} collective-permute-done((bf16[512,2048]{1,0:T(8,128)(2,1)S(1)}, bf16[512,2048]{1,0:T(8,128)(2,1)S(1)}, u32[]{:S(2)}, u32[]{:S(2)}) %collective-permute-start.23) | collective-permute-done | bytes 2097184 | tf_op jit(solution)/shard_map/ppermute | solution.py:451
  515.9 48.7 %collective-permute-done.24.refs_0_ = bf16[512,2048]{1,0:T(8,128)(2,1)} collective-permute-done((bf16[512,2048]{1,0:T(8,128)(2,1)S(1)}, bf16[512,2048]{1,0:T(8,128)(2,1)}, u32[]{:S(2)}, u32[]{:S(2)}) %collective-permute-start.24) | collective-permute-done | bytes 2097184 | tf_op jit(solution)/shard_map/ppermute | solution.py:451
  572.9 38.2 %collective-permute-done.25.refs_1_ = bf16[512,1024]{1,0:T(8,128)(2,1)S(1)} collective-permute-done((bf16[512,1024]{1,0:T(8,128)(2,1)S(1)}, bf16[512,1024]{1,0:T(8,128)(2,1)S(1)}, u32[]{:S(2)}, u32[]{:S(2)}) %collective-permute-start.25) | collective-permute-done | bytes 1048608 | tf_op jit(solution)/shard_map/ppermute | solution.py:451
  625.3 51.5 %slots.2 = (bf16[1728,2048]{1,0:T(8,128)(2,1)}, bf16[1728,2048]{1,0:T(8,128)(2,1)}, f32[2,1728,1]{2,1,0:T(8,128)}) custom-call(s32[4,2,2560]{2,1,0:T(2,128)} %get-tuple-element.175.slot_ref, f32[4,2,2560]{2,1,0:T(2,128)} %bitcast.138, f32[1,2048]{1,0:T(1,128)} %bitcast.149, bf16[10240,2048]{1,0:T(8,128)(2,1)} %all-gather.23.cloned.1.call-done.x_ref), custom_call_target="tpu_custom_call" | custom-call | flops 36238786560 | bytes 41943040 | tf_op jit(solution)/shard_map/slots/pallas_call | solution.py:386
  680.5 13.5 fusion.23
  694.1 10.4 fusion.19
  704.5 22.2 %collective-permute-done.27.refs_3_ = bf16[512,2048]{1,0:T(8,128)(2,1)S(1)} collective-permute-done((bf16[512,2048]{1,0:T(8,128)(2,1)S(1)}, bf16[512,2048]{1,0:T(8,128)(2,1)S(1)}, u32[]{:S(2)}, u32[]{:S(2)}) %collective-permute-start.27) | collective-permute-done | bytes 2097184 | tf_op jit(solution)/shard_map/ppermute | solution.py:451
  738.7 16.5 multiply_convert_fusion.7
  755.2 12.0 multiply_convert_fusion.6
  767.2 18.7 collective-permute-done.28.refs_0_
  788.6 46.0 %collective-permute-done.29.refs_1_ = bf16[512,1024]{1,0:T(8,128)(2,1)S(1)} collective-permute-done((bf16[512,1024]{1,0:T(8,128)(2,1)S(1)}, bf16[512,1024]{1,0:T(8,128)(2,1)S(1)}, u32[]{:S(2)}, u32[]{:S(2)}) %collective-permute-start.29) | collective-permute-done | bytes 1048608 | tf_op jit(solution)/shard_map/ppermute | solution.py:451
  835.9 48.9 %slots.3 = (bf16[1728,2048]{1,0:T(8,128)(2,1)}, bf16[1728,2048]{1,0:T(8,128)(2,1)}, f32[2,1728,1]{2,1,0:T(8,128)}) custom-call(s32[4,2,2560]{2,1,0:T(2,128)} %get-tuple-element.175.slot_ref, f32[4,2,2560]{2,1,0:T(2,128)} %bitcast.139, f32[1,2048]{1,0:T(1,128)} %bitcast.150, bf16[10240,2048]{1,0:T(8,128)(2,1)} %all-gather.25.cloned.1.call-done.x_ref), custom_call_target="tpu_custom_call" | custom-call | flops 36238786560 | bytes 41943040 | tf_op jit(solution)/shard_map/slots/pallas_call | solution.py:386
  884.9 11.5 convolution_convert_fusion.8.refs_0_
  910.2 37.6 %collective-permute-done.31.refs_3_ = bf16[512,2048]{1,0:T(8,128)(2,1)S(1)} collective-permute-done((bf16[512,2048]{1,0:T(8,128)(2,1)S(1)}, bf16[512,2048]{1,0:T(8,128)(2,1)S(1)}, u32[]{:S(2)}, u32[]{:S(2)}) %collective-permute-start.31) | collective-permute-done | bytes 2097184 | tf_op jit(solution)/shard_map/ppermute | solution.py:451
  957.6 18.9 multiply_convert_fusion.2
  976.5 13.4 fusion.17
  989.9 19.3 %multiply_convert_fusion.3 = (bf16[1728,1024]{1,0:T(8,128)(2,1)}, bf16[1728,1024]{1,0:T(8,128)(2,1)}) fusion(f32[1728,1024]{1,0:T(8,128)} %fusion.23, f32[1728,1024]{1,0:T(8,128)} %get-tuple-element.381, bf16[1728,2048]{1,0:T(8,128)(2,1)} %get-tuple-element.209, bf16[2048,2048]{1,0:T(8,128)(2,1)} %at_home.5), kind=kOutput, calls=%fused_computation.12 | convolution fusion | flops 7270760448 | bytes 32505856 | tf_op jit(solution)/shard_map/dot_general | solution.py:59
  1009.1 13.4 fusion.21
  1029.0 14.2 add_convert_fusion.1
  1043.3 13.8 add_convert_fusion
  1057.1 51.2 %combine.3 = bf16[10240,2048]{1,0:T(8,128)(2,1)} custom-call(s32[10240,2]{1,0:T(8,128)} %bitcast.127, bf16[4,432,2048]{2,1,0:T(8,128)(2,1)} %bitcast.157, bf16[4,432,2048]{2,1,0:T(8,128)(2,1)} %bitcast.158), custom_call_target="tpu_custom_call" | custom-call | flops 36238786560 | bytes 41943040 | tf_op jit(solution)/shard_map/combine/pallas_call | solution.py:432
  1127.0 12.4 convolution_convert_fusion.6.refs_0_
  1149.2 10.5 convolution_convert_fusion.5.refs_1_
  1196.5 28.1 %combine.5 = bf16[5120,2048]{1,0:T(8,128)(2,1)} custom-call(s32[10240,2]{1,0:T(8,128)} %bitcast.128, bf16[4,432,2048]{2,1,0:T(8,128)(2,1)} %bitcast.153, bf16[4,432,2048]{2,1,0:T(8,128)(2,1)} %bitcast.155), custom_call_target="tpu_custom_call" | custom-call | flops 18119393280 | bytes 20971520 | tf_op jit(solution)/shard_map/combine/pallas_call | solution.py:432
  1224.6 28.0 %combine.4 = bf16[5120,2048]{1,0:T(8,128)(2,1)} custom-call(s32[10240,2]{1,0:T(8,128)} %bitcast.129, bf16[4,432,2048]{2,1,0:T(8,128)(2,1)} %bitcast.154, bf16[4,432,2048]{2,1,0:T(8,128)(2,1)} %bitcast.156), custom_call_target="tpu_custom_call" | custom-call | flops 18119393280 | bytes 20971520 | tf_op jit(solution)/shard_map/combine/pallas_call | solution.py:432
  1252.6 10.3 collective-permute-done.40.refs_4_
  1270.8 22.7 %collective-permute-done.43.refs_7_ = bf16[512,1024]{1,0:T(8,128)(2,1)} collective-permute-done((bf16[512,1024]{1,0:T(8,128)(2,1)S(1)}, bf16[512,1024]{1,0:T(8,128)(2,1)}, u32[]{:S(2)}, u32[]{:S(2)}) %collective-permute-start.43) | collective-permute-done | bytes 1048608 | tf_op jit(solution)/shard_map/ppermute | solution.py:451
  1293.5 19.9 %collective-permute-done.42.refs_6_ = bf16[512,1024]{1,0:T(8,128)(2,1)} collective-permute-done((bf16[512,1024]{1,0:T(8,128)(2,1)S(1)}, bf16[512,1024]{1,0:T(8,128)(2,1)}, u32[]{:S(2)}, u32[]{:S(2)}) %collective-permute-start.42) | collective-permute-done | bytes 1048608 | tf_op jit(solution)/shard_map/ppermute | solution.py:451
  1313.4 46.2 %collective-permute-done.41.refs_5_ = bf16[512,1024]{1,0:T(8,128)(2,1)} collective-permute-done((bf16[512,1024]{1,0:T(8,128)(2,1)S(1)}, bf16[512,1024]{1,0:T(8,128)(2,1)}, u32[]{:S(2)}, u32[]{:S(2)}) %collective-permute-start.41) | collective-permute-done | bytes 1048608 | tf_op jit(solution)/shard_map/ppermute | solution.py:451
  1371.0 27.3 %collective-permute-done.44 = bf16[2560,256]{1,0:T(8,128)(2,1)} collective-permute-done((bf16[2560,256]{1,0:T(8,128)(2,1)}, bf16[2560,256]{1,0:T(8,128)(2,1)}, u32[]{:S(2)}, u32[]{:S(2)}) %collective-permute-start.44) | collective-permute-done | bytes 1310752 | tf_op jit(solution)/shard_map/ppermute | solution.py:620
  1414.7 46.2 %collective-permute-done.49.refs_3_ = bf16[512,1024]{1,0:T(8,128)(2,1)S(1)} collective-permute-done((bf16[512,1024]{1,0:T(8,128)(2,1)}, bf16[512,1024]{1,0:T(8,128)(2,1)S(1)}, u32[]{:S(2)}, u32[]{:S(2)}) %collective-permute-start.49) | collective-permute-done | bytes 1048608 | tf_op jit(solution)/shard_map/ppermute | solution.py:451
  1460.9 20.6 %collective-permute-done.48.refs_2_ = bf16[512,1024]{1,0:T(8,128)(2,1)} collective-permute-done((bf16[512,1024]{1,0:T(8,128)(2,1)S(1)}, bf16[512,1024]{1,0:T(8,128)(2,1)}, u32[]{:S(2)}, u32[]{:S(2)}) %collective-permute-start.48) | collective-permute-done | bytes 1048608 | tf_op jit(solution)/shard_map/ppermute | solution.py:451
  1551.7 36.4 %collective-permute-done.52.refs_4_ = bf16[512,1024]{1,0:T(8,128)(2,1)S(1)} collective-permute-done((bf16[512,1024]{1,0:T(8,128)(2,1)S(1)}, bf16[512,1024]{1,0:T(8,128)(2,1)S(1)}, u32[]{:S(2)}, u32[]{:S(2)}) %collective-permute-start.52) | collective-permute-done | bytes 1048608 | tf_op jit(solution)/shard_map/ppermute | solution.py:451
  1589.1 15.4 all-gather.27.cloned.1.call-done
  1614.8 11.9 collective-permute-done.53
  1645.5 21.4 %tree_backward.1 = (f32[2560,256]{1,0:T(8,128)}, f32[2560,256]{1,0:T(8,128)}, bf16[2560,256]{1,0:T(8,128)(2,1)S(1)}) custom-call(s32[1,20]{1,0:T(1,128)S(1)} %copy-done.18, bf16[2560,256]{1,0:T(8,128)(2,1)S(1)} %get-tuple-element.271.qr_ref, bf16[2560,256]{1,0:T(8,128)(2,1)S(1)} %copy-done.3, bf16[2560,256]{1,0:T(8,128)(2,1)} %get-tuple-element.273.vl_ref, ...), custom_call_target="tpu_custom_call" | custom-call | tf_op jit(solution)/shard_map/tree_backward/pallas_call | solution.py:333
  1671.0 14.5 collective-permute-start.57
  1737.5 12.6 convolution_convert_fusion.9
  1789.1 11.7 collective-permute-done.71
  1824.8 12.5 collective-permute-done.73
  (556 shorter events, 627.8 us)
Async XLA Ops:
  7.2 69.7 %all-gather.17.cloned.1.call-start = ((), (), s32[]{:S(2)}) async-start(), calls=%async_computation.5 | async-start | bytes 3932160 | tf_op jit(solution)/shard_map/all_gather | solution.py:654
  13.8 152.2 %all-gather.19.cloned.1.call-start = ((), (), s32[]{:S(2)}) async-start(), calls=%async_computation.6 | async-start | bytes 1310720 | tf_op jit(solution)/shard_map/all_gather | solution.py:657
  76.9 195.5 %reduce-scatter.6.cloned.1.call-start = ((), (), s32[]{:S(2)}) async-start(), calls=%async_computation.7 | async-start | bytes 11796480 | tf_op jit(solution)/shard_map/reduce_scatter | solution.py:680
  76.9 46.7 %collective-permute-start.8 = (bf16[2560,256]{1,0:T(8,128)(2,1)S(1)}, bf16[2560,256]{1,0:T(8,128)(2,1)}, u32[]{:S(2)}, u32[]{:S(2)}) collective-permute-start(bf16[2560,256]{1,0:T(8,128)(2,1)S(1)} %copy-done.30), channel_id=1, source_target_pairs={{0,8},{8,16},{16,24},{1,9},{9,17},{17,25},{2,10},{10,18},{18,26},{... | collective-permute-start | bytes 3932168 | tf_op jit(solution)/shard_map/ppermute | solution.py:588
  79.6 49.3 %collective-permute-start.9 = (bf16[2560,256]{1,0:T(8,128)(2,1)S(1)}, bf16[2560,256]{1,0:T(8,128)(2,1)}, u32[]{:S(2)}, u32[]{:S(2)}) collective-permute-start(bf16[2560,256]{1,0:T(8,128)(2,1)S(1)} %copy-done.30), channel_id=1, source_target_pairs={{8,0},{16,8},{24,16},{9,1},{17,9},{25,17},{10,2},{18,10},{26,18},{... | collective-permute-start | bytes 3932168 | tf_op jit(solution)/shard_map/ppermute | solution.py:589
  128.9 44.4 %collective-permute-start.10 = (bf16[2560,256]{1,0:T(8,128)(2,1)}, bf16[2560,256]{1,0:T(8,128)(2,1)}, u32[]{:S(2)}, u32[]{:S(2)}) collective-permute-start(bf16[2560,256]{1,0:T(8,128)(2,1)} %collective-permute-done.8), channel_id=1, source_target_pairs={{0,8},{8,16},{16,24},{1,9},{9,17},{17,25},{2,10},{10,18},{18,26},{... | collective-permute-start | bytes 3932168 | tf_op jit(solution)/shard_map/ppermute | solution.py:588
  132.9 40.5 %collective-permute-start.11 = (bf16[2560,256]{1,0:T(8,128)(2,1)}, bf16[2560,256]{1,0:T(8,128)(2,1)}, u32[]{:S(2)}, u32[]{:S(2)}) collective-permute-start(bf16[2560,256]{1,0:T(8,128)(2,1)} %collective-permute-done.9), channel_id=1, source_target_pairs={{8,0},{16,8},{24,16},{9,1},{17,9},{25,17},{10,2},{18,10},{26,18},{... | collective-permute-start | bytes 3932168 | tf_op jit(solution)/shard_map/ppermute | solution.py:589
  173.4 242.5 %all-gather.21.cloned.1.call-start = ((), (), s32[]{:S(2)}) async-start(), calls=%async_computation.8 | async-start | bytes 6553600 | tf_op jit(solution)/shard_map/all_gather | solution.py:693
  196.5 75.9 %collective-permute-start.12 = (bf16[512,2048]{1,0:T(8,128)(2,1)S(1)}, bf16[512,2048]{1,0:T(8,128)(2,1)}, u32[]{:S(2)}, u32[]{:S(2)}) collective-permute-start(bf16[512,2048]{1,0:T(8,128)(2,1)S(1)} %constant_dynamic-slice_fusion.37), channel_id=1, source_target_pairs={{0,8},{8,16},{16,24},{24,0},{1,9},{9,17},{17,25},{25,1},{2,10},{10... | collective-permute-start | bytes 6291464 | tf_op jit(solution)/shard_map/ppermute | solution.py:451
  197.9 74.5 %collective-permute-start.14 = (bf16[2560,256]{1,0:T(8,128)(2,1)}, bf16[2560,256]{1,0:T(8,128)(2,1)}, u32[]{:S(2)}, u32[]{:S(2)}) collective-permute-start(bf16[2560,256]{1,0:T(8,128)(2,1)} %collective-permute-done.11), channel_id=1, source_target_pairs={{8,0},{16,8},{24,16},{9,1},{17,9},{25,17},{10,2},{18,10},{26,18},{... | collective-permute-start | bytes 3932168 | tf_op jit(solution)/shard_map/ppermute | solution.py:589
  275.8 345.6 %all-gather.23.cloned.1.call-start = ((), (), s32[]{:S(2)}) async-start(), calls=%async_computation.9 | async-start | bytes 47185920 | tf_op jit(solution)/shard_map/all_gather | solution.py:711
  292.1 107.6 %collective-permute-start.21 = (bf16[512,1024]{1,0:T(8,128)(2,1)S(1)}, bf16[512,1024]{1,0:T(8,128)(2,1)S(1)}, u32[]{:S(2)}, u32[]{:S(2)}) collective-permute-start(bf16[512,1024]{1,0:T(8,128)(2,1)S(1)} %constant_dynamic-slice_fusion.36), channel_id=1, source_target_pairs={{0,16},{8,24},{16,0},{24,8},{1,17},{9,25},{17,1},{25,9},{2,18},{10... | collective-permute-start | bytes 3145736 | tf_op jit(solution)/shard_map/ppermute | solution.py:451
  416.0 418.6 %all-gather.25.cloned.1.call-start = ((), (), s32[]{:S(2)}) async-start(), calls=%async_computation.10 | async-start | bytes 47185920 | tf_op jit(solution)/shard_map/all_gather | solution.py:720
  417.3 46.4 %collective-permute-start.22 = (bf16[512,1024]{1,0:T(8,128)(2,1)S(1)}, bf16[512,1024]{1,0:T(8,128)(2,1)}, u32[]{:S(2)}, u32[]{:S(2)}) collective-permute-start(bf16[512,1024]{1,0:T(8,128)(2,1)S(1)} %constant_dynamic-slice_fusion.35), channel_id=1, source_target_pairs={{0,16},{8,24},{16,0},{24,8},{1,17},{9,25},{17,1},{25,9},{2,18},{10... | collective-permute-start | bytes 3145736 | tf_op jit(solution)/shard_map/ppermute | solution.py:451
  465.6 47.6 %collective-permute-start.23 = (bf16[512,2048]{1,0:T(8,128)(2,1)S(1)}, bf16[512,2048]{1,0:T(8,128)(2,1)S(1)}, u32[]{:S(2)}, u32[]{:S(2)}) collective-permute-start(bf16[512,2048]{1,0:T(8,128)(2,1)S(1)} %constant_dynamic-slice_fusion.34), channel_id=1, source_target_pairs={{0,24},{8,0},{16,8},{24,16},{1,25},{9,1},{17,9},{25,17},{2,26},{10... | collective-permute-start | bytes 6291464 | tf_op jit(solution)/shard_map/ppermute | solution.py:451
  515.9 48.8 %collective-permute-start.24 = (bf16[512,2048]{1,0:T(8,128)(2,1)S(1)}, bf16[512,2048]{1,0:T(8,128)(2,1)}, u32[]{:S(2)}, u32[]{:S(2)}) collective-permute-start(bf16[512,2048]{1,0:T(8,128)(2,1)S(1)} %constant_dynamic-slice_fusion.33), channel_id=1, source_target_pairs={{0,8},{8,16},{16,24},{24,0},{1,9},{9,17},{17,25},{25,1},{2,10},{10... | collective-permute-start | bytes 6291464 | tf_op jit(solution)/shard_map/ppermute | solution.py:451
  565.9 45.1 %collective-permute-start.25 = (bf16[512,1024]{1,0:T(8,128)(2,1)S(1)}, bf16[512,1024]{1,0:T(8,128)(2,1)S(1)}, u32[]{:S(2)}, u32[]{:S(2)}) collective-permute-start(bf16[512,1024]{1,0:T(8,128)(2,1)S(1)} %constant_dynamic-slice_fusion.32), channel_id=1, source_target_pairs={{0,16},{8,24},{16,0},{24,8},{1,17},{9,25},{17,1},{25,9},{2,18},{10... | collective-permute-start | bytes 3145736 | tf_op jit(solution)/shard_map/ppermute | solution.py:451
  621.5 741.0 %reduce-scatter.8.cloned.1.call-start = ((), (), s32[]{:S(2)}) async-start(), calls=%async_computation.11 | async-start | bytes 47185920 | tf_op jit(solution)/shard_map/reduce_scatter | solution.py:772
  622.8 54.0 %collective-permute-start.26 = (bf16[512,1024]{1,0:T(8,128)(2,1)S(1)}, bf16[512,1024]{1,0:T(8,128)(2,1)S(1)}, u32[]{:S(2)}, u32[]{:S(2)}) collective-permute-start(bf16[512,1024]{1,0:T(8,128)(2,1)S(1)} %constant_dynamic-slice_fusion.31), channel_id=1, source_target_pairs={{0,16},{8,24},{16,0},{24,8},{1,17},{9,25},{17,1},{25,9},{2,18},{10... | collective-permute-start | bytes 3145736 | tf_op jit(solution)/shard_map/ppermute | solution.py:451
  678.8 47.8 %collective-permute-start.27 = (bf16[512,2048]{1,0:T(8,128)(2,1)S(1)}, bf16[512,2048]{1,0:T(8,128)(2,1)S(1)}, u32[]{:S(2)}, u32[]{:S(2)}) collective-permute-start(bf16[512,2048]{1,0:T(8,128)(2,1)S(1)} %constant_dynamic-slice_fusion.30), channel_id=1, source_target_pairs={{0,24},{8,0},{16,8},{24,16},{1,25},{9,1},{17,9},{25,17},{2,26},{10... | collective-permute-start | bytes 6291464 | tf_op jit(solution)/shard_map/ppermute | solution.py:451
  736.7 49.2 %collective-permute-start.28 = (bf16[512,2048]{1,0:T(8,128)(2,1)S(1)}, bf16[512,2048]{1,0:T(8,128)(2,1)S(1)}, u32[]{:S(2)}, u32[]{:S(2)}) collective-permute-start(bf16[512,2048]{1,0:T(8,128)(2,1)S(1)} %constant_dynamic-slice_fusion.29), channel_id=1, source_target_pairs={{0,8},{8,16},{16,24},{24,0},{1,9},{9,17},{17,25},{25,1},{2,10},{10... | collective-permute-start | bytes 6291464 | tf_op jit(solution)/shard_map/ppermute | solution.py:451
  788.5 46.1 %collective-permute-start.29 = (bf16[512,1024]{1,0:T(8,128)(2,1)S(1)}, bf16[512,1024]{1,0:T(8,128)(2,1)S(1)}, u32[]{:S(2)}, u32[]{:S(2)}) collective-permute-start(bf16[512,1024]{1,0:T(8,128)(2,1)S(1)} %constant_dynamic-slice_fusion.28), channel_id=1, source_target_pairs={{0,16},{8,24},{16,0},{24,8},{1,17},{9,25},{17,1},{25,9},{2,18},{10... | collective-permute-start | bytes 3145736 | tf_op jit(solution)/shard_map/ppermute | solution.py:451
  835.9 49.0 %collective-permute-start.30 = (bf16[512,1024]{1,0:T(8,128)(2,1)S(1)}, bf16[512,1024]{1,0:T(8,128)(2,1)S(1)}, u32[]{:S(2)}, u32[]{:S(2)}) collective-permute-start(bf16[512,1024]{1,0:T(8,128)(2,1)S(1)} %constant_dynamic-slice_fusion.27), channel_id=1, source_target_pairs={{0,16},{8,24},{16,0},{24,8},{1,17},{9,25},{17,1},{25,9},{2,18},{10... | collective-permute-start | bytes 3145736 | tf_op jit(solution)/shard_map/ppermute | solution.py:451
  899.8 48.0 %collective-permute-start.31 = (bf16[512,2048]{1,0:T(8,128)(2,1)S(1)}, bf16[512,2048]{1,0:T(8,128)(2,1)S(1)}, u32[]{:S(2)}, u32[]{:S(2)}) collective-permute-start(bf16[512,2048]{1,0:T(8,128)(2,1)S(1)} %constant_dynamic-slice_fusion.26), channel_id=1, source_target_pairs={{0,24},{8,0},{16,8},{24,16},{1,25},{9,1},{17,9},{25,17},{2,26},{10... | collective-permute-start | bytes 6291464 | tf_op jit(solution)/shard_map/ppermute | solution.py:451
  948.0 74.5 %collective-permute-start.33 = (bf16[512,1024]{1,0:T(8,128)(2,1)S(1)}, bf16[512,1024]{1,0:T(8,128)(2,1)S(1)}, u32[]{:S(2)}, u32[]{:S(2)}) collective-permute-start(bf16[512,1024]{1,0:T(8,128)(2,1)S(1)} %constant_dynamic-slice_fusion.24), channel_id=1, source_target_pairs={{0,8},{8,16},{16,24},{24,0},{1,9},{9,17},{17,25},{25,1},{2,10},{10... | collective-permute-start | bytes 3145736 | tf_op jit(solution)/shard_map/ppermute | solution.py:451
  949.8 72.7 %collective-permute-start.32 = (bf16[512,1024]{1,0:T(8,128)(2,1)S(1)}, bf16[512,1024]{1,0:T(8,128)(2,1)S(1)}, u32[]{:S(2)}, u32[]{:S(2)}) collective-permute-start(bf16[512,1024]{1,0:T(8,128)(2,1)S(1)} %constant_dynamic-slice_fusion.25), channel_id=1, source_target_pairs={{0,8},{8,16},{16,24},{24,0},{1,9},{9,17},{17,25},{25,1},{2,10},{10... | collective-permute-start | bytes 3145736 | tf_op jit(solution)/shard_map/ppermute | solution.py:451
  1026.1 82.2 %collective-permute-start.35 = (bf16[512,1024]{1,0:T(8,128)(2,1)}, bf16[512,1024]{1,0:T(8,128)(2,1)S(1)}, u32[]{:S(2)}, u32[]{:S(2)}) collective-permute-start(bf16[512,1024]{1,0:T(8,128)(2,1)} %constant_dynamic-slice_fusion.22), channel_id=1, source_target_pairs={{0,16},{8,24},{16,0},{24,8},{1,17},{9,25},{17,1},{25,9},{2,18},{10... | collective-permute-start | bytes 3145736 | tf_op jit(solution)/shard_map/ppermute | solution.py:451
  1027.7 90.2 %collective-permute-start.34 = (bf16[512,1024]{1,0:T(8,128)(2,1)}, bf16[512,1024]{1,0:T(8,128)(2,1)S(1)}, u32[]{:S(2)}, u32[]{:S(2)}) collective-permute-start(bf16[512,1024]{1,0:T(8,128)(2,1)} %constant_dynamic-slice_fusion.23), channel_id=1, source_target_pairs={{0,16},{8,24},{16,0},{24,8},{1,17},{9,25},{17,1},{25,9},{2,18},{10... | collective-permute-start | bytes 3145736 | tf_op jit(solution)/shard_map/ppermute | solution.py:451
  1118.9 417.6 %reduce-scatter.10.cloned.1.call-start = ((), (), s32[]{:S(2)}) async-start(), calls=%async_computation.12 | async-start | bytes 23592960 | tf_op jit(solution)/shard_map/reduce_scatter | solution.py:789
  1122.3 47.2 %collective-permute-start.37 = (bf16[512,1024]{1,0:T(8,128)(2,1)S(1)}, bf16[512,1024]{1,0:T(8,128)(2,1)S(1)}, u32[]{:S(2)}, u32[]{:S(2)}) collective-permute-start(bf16[512,1024]{1,0:T(8,128)(2,1)S(1)} %constant_dynamic-slice_fusion.20), channel_id=1, source_target_pairs={{0,24},{8,0},{16,8},{24,16},{1,25},{9,1},{17,9},{25,17},{2,26},{10... | collective-permute-start | bytes 3145736 | tf_op jit(solution)/shard_map/ppermute | solution.py:451
  1126.9 43.4 %collective-permute-start.36 = (bf16[512,1024]{1,0:T(8,128)(2,1)S(1)}, bf16[512,1024]{1,0:T(8,128)(2,1)S(1)}, u32[]{:S(2)}, u32[]{:S(2)}) collective-permute-start(bf16[512,1024]{1,0:T(8,128)(2,1)S(1)} %constant_dynamic-slice_fusion.21), channel_id=1, source_target_pairs={{0,24},{8,0},{16,8},{24,16},{1,25},{9,1},{17,9},{25,17},{2,26},{10... | collective-permute-start | bytes 3145736 | tf_op jit(solution)/shard_map/ppermute | solution.py:451
  1170.3 92.6 %collective-permute-start.40 = (bf16[512,1024]{1,0:T(8,128)(2,1)S(1)}, bf16[512,1024]{1,0:T(8,128)(2,1)S(1)}, u32[]{:S(2)}, u32[]{:S(2)}) collective-permute-start(bf16[512,1024]{1,0:T(8,128)(2,1)S(1)} %constant_dynamic-slice_fusion.17), channel_id=1, source_target_pairs={{0,16},{8,24},{16,0},{24,8},{1,17},{9,25},{17,1},{25,9},{2,18},{10... | collective-permute-start | bytes 3145736 | tf_op jit(solution)/shard_map/ppermute | solution.py:451
  1172.7 90.2 %collective-permute-start.39 = (bf16[512,1024]{1,0:T(8,128)(2,1)}, bf16[512,1024]{1,0:T(8,128)(2,1)}, u32[]{:S(2)}, u32[]{:S(2)}) collective-permute-start(bf16[512,1024]{1,0:T(8,128)(2,1)} %constant_dynamic-slice_fusion.18), channel_id=1, source_target_pairs={{0,8},{8,16},{16,24},{24,0},{1,9},{9,17},{17,25},{25,1},{2,10},{10... | collective-permute-start | bytes 3145736 | tf_op jit(solution)/shard_map/ppermute | solution.py:451
  1177.3 85.6 %collective-permute-start.38 = (bf16[512,1024]{1,0:T(8,128)(2,1)}, bf16[512,1024]{1,0:T(8,128)(2,1)}, u32[]{:S(2)}, u32[]{:S(2)}) collective-permute-start(bf16[512,1024]{1,0:T(8,128)(2,1)} %constant_dynamic-slice_fusion.19), channel_id=1, source_target_pairs={{0,8},{8,16},{16,24},{24,0},{1,9},{9,17},{17,25},{25,1},{2,10},{10... | collective-permute-start | bytes 3145736 | tf_op jit(solution)/shard_map/ppermute | solution.py:451
  1267.3 46.1 %collective-permute-start.42 = (bf16[512,1024]{1,0:T(8,128)(2,1)S(1)}, bf16[512,1024]{1,0:T(8,128)(2,1)}, u32[]{:S(2)}, u32[]{:S(2)}) collective-permute-start(bf16[512,1024]{1,0:T(8,128)(2,1)S(1)} %constant_dynamic-slice_fusion.15), channel_id=1, source_target_pairs={{0,24},{8,0},{16,8},{24,16},{1,25},{9,1},{17,9},{25,17},{2,26},{10... | collective-permute-start | bytes 3145736 | tf_op jit(solution)/shard_map/ppermute | solution.py:451
  1270.3 89.4 %collective-permute-start.41 = (bf16[512,1024]{1,0:T(8,128)(2,1)S(1)}, bf16[512,1024]{1,0:T(8,128)(2,1)}, u32[]{:S(2)}, u32[]{:S(2)}) collective-permute-start(bf16[512,1024]{1,0:T(8,128)(2,1)S(1)} %constant_dynamic-slice_fusion.16), channel_id=1, source_target_pairs={{0,16},{8,24},{16,0},{24,8},{1,17},{9,25},{17,1},{25,9},{2,18},{10... | collective-permute-start | bytes 3145736 | tf_op jit(solution)/shard_map/ppermute | solution.py:451
  1362.4 242.1 %all-gather.27.cloned.1.call-start = ((), (), s32[]{:S(2)}) async-start(), calls=%async_computation.13 | async-start | bytes 11796480 | tf_op jit(solution)/shard_map/all_gather | solution.py:806
  1402.6 78.9 %collective-permute-start.47 = (bf16[2560,256]{1,0:T(8,128)(2,1)}, bf16[2560,256]{1,0:T(8,128)(2,1)}, u32[]{:S(2)}, u32[]{:S(2)}) collective-permute-start(bf16[2560,256]{1,0:T(8,128)(2,1)} %get-tuple-element.336), channel_id=1, source_target_pairs={{24,16},{16,8},{25,17},{17,9},{26,18},{18,10},{27,19},{19,11},{28,... | collective-permute-start | bytes 3932168 | tf_op jit(solution)/shard_map/ppermute | solution.py:621
  1404.3 77.1 %collective-permute-start.46 = (bf16[2560,256]{1,0:T(8,128)(2,1)}, bf16[2560,256]{1,0:T(8,128)(2,1)}, u32[]{:S(2)}, u32[]{:S(2)}) collective-permute-start(bf16[2560,256]{1,0:T(8,128)(2,1)} %get-tuple-element.337), channel_id=1, source_target_pairs={{0,8},{8,16},{1,9},{9,17},{2,10},{10,18},{3,11},{11,19},{4,12},{12... | collective-permute-start | bytes 3932168 | tf_op jit(solution)/shard_map/ppermute | solution.py:620
  1413.0 47.9 %collective-permute-start.49 = (bf16[512,1024]{1,0:T(8,128)(2,1)}, bf16[512,1024]{1,0:T(8,128)(2,1)S(1)}, u32[]{:S(2)}, u32[]{:S(2)}) collective-permute-start(bf16[512,1024]{1,0:T(8,128)(2,1)} %constant_dynamic-slice_fusion.10), channel_id=1, source_target_pairs={{0,8},{8,16},{16,24},{24,0},{1,9},{9,17},{17,25},{25,1},{2,10},{10... | collective-permute-start | bytes 3145736 | tf_op jit(solution)/shard_map/ppermute | solution.py:451
  1414.5 67.0 %collective-permute-start.48 = (bf16[512,1024]{1,0:T(8,128)(2,1)S(1)}, bf16[512,1024]{1,0:T(8,128)(2,1)}, u32[]{:S(2)}, u32[]{:S(2)}) collective-permute-start(bf16[512,1024]{1,0:T(8,128)(2,1)S(1)} %constant_dynamic-slice_fusion.11), channel_id=1, source_target_pairs={{0,8},{8,16},{16,24},{24,0},{1,9},{9,17},{17,25},{25,1},{2,10},{10... | collective-permute-start | bytes 3145736 | tf_op jit(solution)/shard_map/ppermute | solution.py:451
  1536.5 219.9 %reduce-scatter.12.cloned.1.call-start = ((), (), s32[]{:S(2)}) async-start(), calls=%async_computation.14 | async-start | bytes 23592960 | tf_op jit(solution)/shard_map/reduce_scatter | solution.py:808
  1537.9 50.3 %collective-permute-start.52 = (bf16[512,1024]{1,0:T(8,128)(2,1)S(1)}, bf16[512,1024]{1,0:T(8,128)(2,1)S(1)}, u32[]{:S(2)}, u32[]{:S(2)}) collective-permute-start(bf16[512,1024]{1,0:T(8,128)(2,1)S(1)} %constant_dynamic-slice_fusion.9), channel_id=1, source_target_pairs={{0,16},{8,24},{16,0},{24,8},{1,17},{9,25},{17,1},{25,9},{2,18},{10... | collective-permute-start | bytes 3145736 | tf_op jit(solution)/shard_map/ppermute | solution.py:451
  1604.6 270.7 %reduce-scatter.14.cloned.1.call-start = ((), (), s32[]{:S(2)}) async-start(), calls=%async_computation.15 | async-start | bytes 11796480 | tf_op jit(solution)/shard_map/reduce_scatter | solution.py:845
  1614.5 87.9 %collective-permute-start.59 = (bf16[512,1024]{1,0:T(8,128)(2,1)}, bf16[512,1024]{1,0:T(8,128)(2,1)}, u32[]{:S(2)}, u32[]{:S(2)}) collective-permute-start(bf16[512,1024]{1,0:T(8,128)(2,1)} %constant_dynamic-slice_fusion.6), channel_id=1, source_target_pairs={{0,16},{8,24},{16,0},{24,8},{1,17},{9,25},{17,1},{25,9},{2,18},{10... | collective-permute-start | bytes 3145736 | tf_op jit(solution)/shard_map/ppermute | solution.py:451
  1704.7 51.7 %collective-permute-start.61 = (bf16[512,1024]{1,0:T(8,128)(2,1)}, bf16[512,1024]{1,0:T(8,128)(2,1)}, u32[]{:S(2)}, u32[]{:S(2)}) collective-permute-start(bf16[512,1024]{1,0:T(8,128)(2,1)} %constant_dynamic-slice_fusion.4), channel_id=1, source_target_pairs={{0,24},{8,0},{16,8},{24,16},{1,25},{9,1},{17,9},{25,17},{2,26},{10... | collective-permute-start | bytes 3145736 | tf_op jit(solution)/shard_map/ppermute | solution.py:451
  1709.5 46.9 %collective-permute-start.60 = (bf16[512,1024]{1,0:T(8,128)(2,1)}, bf16[512,1024]{1,0:T(8,128)(2,1)}, u32[]{:S(2)}, u32[]{:S(2)}) collective-permute-start(bf16[512,1024]{1,0:T(8,128)(2,1)} %constant_dynamic-slice_fusion.5), channel_id=1, source_target_pairs={{0,24},{8,0},{16,8},{24,16},{1,25},{9,1},{17,9},{25,17},{2,26},{10... | collective-permute-start | bytes 3145736 | tf_op jit(solution)/shard_map/ppermute | solution.py:451
  1817.7 40.2 %collective-permute-start.67 = (bf16[1280,256]{1,0:T(8,128)(2,1)}, bf16[1280,256]{1,0:T(8,128)(2,1)}, u32[]{:S(2)}, u32[]{:S(2)}) collective-permute-start(bf16[1280,256]{1,0:T(8,128)(2,1)} %get-tuple-element.346), channel_id=1, source_target_pairs={{24,16},{16,8},{8,0},{25,17},{17,9},{9,1},{26,18},{18,10},{10,2},{... | collective-permute-start | bytes 1966088 | tf_op jit(solution)/shard_map/ppermute | solution.py:621
  (131 other events, 2563.6 us)
Sparse Core Ops, SparseCore 0:
  13.9 62.8 all-gather.16
  78.4 40.6 all-gather.18
  173.5 80.8 reduce-scatter.5
  276.0 139.9 all-gather.20
  417.7 203.7 all-gather.22
  623.8 205.4 all-gather.24
  1118.1 244.2 reduce-scatter.7
  1366.5 136.1 reduce-scatter.9
  1536.6 67.9 all-gather.26
  1608.5 136.6 reduce-scatter.11
  1756.5 79.1 reduce-scatter.13

commit v4 on v3

--- a/solution.py
+++ b/solution.py
@@ -604,7 +604,7 @@
     return whole
 
 
-def group_total(part, along=()):
+def group_total(part, along=(), beside=None):
     groups = lax.axis_size("row")
     here = lax.axis_index("row")
     rows = part.shape[0] // groups
@@ -619,7 +619,10 @@
         downward = (rows_of(here - groups + step) + downward).astype(jnp.bfloat16)
         upward = lax.ppermute(upward, "row", [(i, i + 1) for i in range(step)])
         downward = lax.ppermute(downward, "row", [(groups - 1 - i, groups - 2 - i) for i in range(step)])
-        upward, downward = after((upward, downward), *(along if step == groups - 2 else ()))
+        ties = along if step == groups - 2 else ()
+        if step == groups - 1 and beside is not None:
+            ties = beside()
+        upward, downward = after((upward, downward), *ties)
         upward, downward = upward.astype(jnp.float32), downward.astype(jnp.float32)
     return rows_of(here) + upward + downward
 
@@ -743,12 +746,16 @@
     d_out, _ = to_slots(slot_of, token_gate, moe_norm, grad_all, False)
     d_out = after(d_out, down_units[-1])
     down_units.append(home_unit(w_down, shifts[last], d_out))
-    down_grads = [contract_rows(d_out[e], hiddens[e]).astype(jnp.bfloat16) for e in experts]
-    down_grads, d_out, down_units = after((down_grads, d_out, down_units))
+    leaving = back_units(units)
+    early, late = leaving[1:2], [leaving[0]] + leaving[2:]
+    down_grads = [contract_rows(d_out[0], hiddens[0]).astype(jnp.bfloat16)]
+    down_grads, d_out, hiddens, down_units = after((down_grads, d_out, hiddens, down_units))
+    down_back = [back_unit(down_grads, unit) for unit in early]
+    for e in experts[1:]:
+        down_grads.append(contract_rows(d_out[e], hiddens[e]).astype(jnp.bfloat16))
     down_home = at_home(w_down, shifts, down_units)
-
-    leaving = back_units(units)
-    down_back = [back_unit(down_grads, leaving[0])]
+    down_grads, down_home, d_out = after((down_grads, down_home, d_out))
+
     d_acts, terms = [], []
     for e in experts:
         gate_act, up_act, sigmoid_gate, silu_gate, _ = acts[e]
@@ -757,10 +764,12 @@
             d_hidden * up_act * sigmoid_gate * (1.0 + gate_act * (1.0 - sigmoid_gate))
         ).astype(jnp.bfloat16)
         d_acts.append((d_gate, (d_hidden * silu_gate).astype(jnp.bfloat16)))
-    for e in experts:
-        terms.append(contract_cols(d_acts[e][0], gate_home[:, cut[e]]))
-    terms, d_acts = after((terms, d_acts), down_back[0])
-    for unit in leaving[1:-1]:
+        terms.append(contract_cols(d_gate, gate_home[:, cut[e]]))
+        if e == 0:
+            terms, d_acts, d_out = after((terms, d_acts, d_out), down_back)
+            down_back.append(back_unit(down_grads, late[0], terms))
+    terms, d_acts = after((terms, d_acts), down_back)
+    for unit in late[1:-1]:
         down_back.append(back_unit(down_grads, unit, terms))
     d_in = [
         (terms[e] + contract_cols(d_acts[e][1], up_home[:, cut[e]])).astype(jnp.bfloat16)
@@ -768,7 +777,7 @@
     ]
     d_rows = combine(slot_column, d_in, tok_rows)
     d_rows, expert_in, d_acts = after((d_rows, expert_in, d_acts), down_back)
-    down_back.append(back_unit(down_grads, leaving[-1], d_rows))
+    down_back.append(back_unit(down_grads, late[-1], d_rows))
     d_rows = lax.psum_scatter(d_rows, "col", scatter_dimension=1, tiled=True)
     gate_grads = [contract_rows(expert_in[e], d_acts[e][0]).astype(jnp.bfloat16) for e in experts]
     up_grads = [contract_rows(expert_in[e], d_acts[e][1]).astype(jnp.bfloat16) for e in experts]
@@ -789,7 +798,7 @@
     halves[0] = lax.psum_scatter(
         after(halves[0], d_rows), "col", scatter_dimension=1, tiled=True
     )
-    w_down_grad = at_owner(down_grads, leaving, down_back)
+    w_down_grad = at_owner(down_grads, early + late, down_back)
     w_gate_grad = at_owner(gate_grads, leaving, gate_back)
 
     gain_two = lax.dynamic_slice_in_dim(moe_norm, col_start, own_width)
@@ -844,8 +853,6 @@
     w_up_grad = at_owner(up_grads, leaving, up_back)
     d_normed_one = lax.psum_scatter(d_one, "col", scatter_dimension=0, tiled=True)
     attn_grads = group_total(attn_grads)
-    moe_sums.append(group_total(halves[1]))
-    d_normed_one, w_up_grad = after((d_normed_one, w_up_grad))
     d_normed_one = d_normed_one.astype(jnp.float32).T
     w_query_grad = attn_grads[:, :own_width]
     w_key_grad = attn_grads[:, own_width : 2 * own_width]
@@ -863,7 +870,8 @@
     gain_grads = jnp.sum(
         row_stack(jnp.stack([attn_gain_grad, q_gain_grad, k_gain_grad, moe_gain_grad])), 0
     )
-    moe_sum = after(jnp.concatenate(moe_sums, 0), gain_grads)
+    moe_sums.append(group_total(halves[1], beside=lambda: (gain_grads, tokens_grad, w_up_grad)))
+    moe_sum = jnp.concatenate(moe_sums, 0)
     output = (residual + moe_sum).astype(jnp.bfloat16)
     return (
         output,

time: 1920 us -> 1900 us (0.990)
    unnamed x221 -> x225, local copies, waits for them, and re-layouts: 37.9 us -> 38.5 us
  transfers between devices with their start and end apart: 88 -> 88, of which waited for: 43 -> 41; matrix products, arithmetic and copies ran while one was open for 24% -> 25% of each run, Pallas kernels for 15% -> 16%
where the time goes in v4:
time: 1900 us; the launch traced here: 1890 us
  waiting for transfers between devices  876 us (46%)
  Pallas kernels  295 us (16%)
  matrix products  281 us (15%)
  starting transfers between devices  161 us (8%)
  local copies, waits for them, and re-layouts  112 us (6%)
  other arithmetic  106 us (6%)
  blocking collectives  46.7 us (2%)
    ppermute x39, waiting for transfers between devices, shift_row(): lax.ppermute(block, 'row', [(i, (i + k) % count) for i in range(count)])  618 us
    dot_general x22, matrix products, dot_f32(): lax.dot_general(left, right, (((left_dim,), (right_dim,)), ((), ())), pre...  260 us
    pallas_call x3, Pallas kernels, combine(): pl.pallas_call(combine_kernel, grid=(groups, steps), in_specs=[pl.BlockSp...  107 us
    pallas_call x2, Pallas kernels, to_slots(): pl.pallas_call(functools.partial(slots_kernel, normed=normed), grid=(grou...  101 us
    ppermute x12, waiting for transfers between devices, group_total(): upward = lax.ppermute(upward, 'row', [(i, i + 1) for i in range(step)])  75.2 us
    ppermute x12, starting transfers between devices, group_total(): upward = lax.ppermute(upward, 'row', [(i, i + 1) for i in range(step)])  68 us
    ppermute x39, starting transfers between devices, shift_row(): lax.ppermute(block, 'row', [(i, (i + k) % count) for i in range(count)])  54.4 us
    ppermute x3, waiting for transfers between devices, line_steps(): lax.ppermute(downward, 'row', [(i + 1, i) for i in range(count - 1)])  52.8 us
  transfers between devices with their start and end apart: 88, of which 41 were waited for; matrix products, arithmetic and copies ran while one was open for 25% of the time, Pallas kernels for 16%

profile of v4, /device:TPU:0, one launch (start us, length us, event | category | flops | bytes accessed | tf_op | source)
XLA Modules:
  0.0 1893.1 jit_solution(9074178139286242960)
XLA Ops:
  85.6 12.6 fusion.26.q_ref.k_ref.v_ref
  102.2 21.4 %collective-permute-done.8 = bf16[2560,256]{1,0:T(8,128)(2,1)} collective-permute-done((bf16[2560,256]{1,0:T(8,128)(2,1)S(1)}, bf16[2560,256]{1,0:T(8,128)(2,1)}, u32[]{:S(2)}, u32[]{:S(2)}) %collective-permute-start.8) | collective-permute-done | bytes 1310752 | tf_op jit(solution)/shard_map/ppermute | solution.py:588
  147.1 17.8 tree_forward.1
  199.2 25.7 %collective-permute-done.13 = bf16[2560,256]{1,0:T(8,128)(2,1)} collective-permute-done((bf16[2560,256]{1,0:T(8,128)(2,1)}, bf16[2560,256]{1,0:T(8,128)(2,1)}, u32[]{:S(2)}, u32[]{:S(2)}) %collective-permute-start.13) | collective-permute-done | bytes 1310752 | tf_op jit(solution)/shard_map/ppermute | solution.py:588
  224.9 47.5 %collective-permute-done.14 = bf16[2560,256]{1,0:T(8,128)(2,1)} collective-permute-done((bf16[2560,256]{1,0:T(8,128)(2,1)}, bf16[2560,256]{1,0:T(8,128)(2,1)}, u32[]{:S(2)}, u32[]{:S(2)}) %collective-permute-start.14) | collective-permute-done | bytes 1310752 | tf_op jit(solution)/shard_map/ppermute | solution.py:589
  298.2 101.5 %collective-permute-done.21.refs_1_ = bf16[512,1024]{1,0:T(8,128)(2,1)S(1)} collective-permute-done((bf16[512,1024]{1,0:T(8,128)(2,1)S(1)}, bf16[512,1024]{1,0:T(8,128)(2,1)S(1)}, u32[]{:S(2)}, u32[]{:S(2)}) %collective-permute-start.21) | collective-permute-done | bytes 1048608 | tf_op jit(solution)/shard_map/ppermute | solution.py:451
  399.7 16.3 all-gather.21.cloned.1.call-done
  417.4 46.3 %collective-permute-done.22.refs_2_ = bf16[512,1024]{1,0:T(8,128)(2,1)} collective-permute-done((bf16[512,1024]{1,0:T(8,128)(2,1)S(1)}, bf16[512,1024]{1,0:T(8,128)(2,1)}, u32[]{:S(2)}, u32[]{:S(2)}) %collective-permute-start.22) | collective-permute-done | bytes 1048608 | tf_op jit(solution)/shard_map/ppermute | solution.py:451
  468.3 44.9 %collective-permute-done.23.refs_3_ = bf16[512,2048]{1,0:T(8,128)(2,1)S(1)} collective-permute-done((bf16[512,2048]{1,0:T(8,128)(2,1)S(1)}, bf16[512,2048]{1,0:T(8,128)(2,1)S(1)}, u32[]{:S(2)}, u32[]{:S(2)}) %collective-permute-start.23) | collective-permute-done | bytes 2097184 | tf_op jit(solution)/shard_map/ppermute | solution.py:451
  515.9 48.7 %collective-permute-done.24.refs_0_ = bf16[512,2048]{1,0:T(8,128)(2,1)} collective-permute-done((bf16[512,2048]{1,0:T(8,128)(2,1)S(1)}, bf16[512,2048]{1,0:T(8,128)(2,1)}, u32[]{:S(2)}, u32[]{:S(2)}) %collective-permute-start.24) | collective-permute-done | bytes 2097184 | tf_op jit(solution)/shard_map/ppermute | solution.py:451
  572.8 38.2 %collective-permute-done.25.refs_1_ = bf16[512,1024]{1,0:T(8,128)(2,1)S(1)} collective-permute-done((bf16[512,1024]{1,0:T(8,128)(2,1)S(1)}, bf16[512,1024]{1,0:T(8,128)(2,1)S(1)}, u32[]{:S(2)}, u32[]{:S(2)}) %collective-permute-start.25) | collective-permute-done | bytes 1048608 | tf_op jit(solution)/shard_map/ppermute | solution.py:451
  625.3 51.6 %slots.2 = (bf16[1728,2048]{1,0:T(8,128)(2,1)}, bf16[1728,2048]{1,0:T(8,128)(2,1)}, f32[2,1728,1]{2,1,0:T(8,128)}) custom-call(s32[4,2,2560]{2,1,0:T(2,128)} %get-tuple-element.181.slot_ref, f32[4,2,2560]{2,1,0:T(2,128)} %bitcast.136, f32[1,2048]{1,0:T(1,128)} %bitcast.147, bf16[10240,2048]{1,0:T(8,128)(2,1)} %all-gather.23.cloned.1.call-done.x_ref), custom_call_target="tpu_custom_call" | custom-call | flops 36238786560 | bytes 41943040 | tf_op jit(solution)/shard_map/slots/pallas_call | solution.py:386
  680.6 13.5 fusion.23
  694.1 10.4 fusion.19
  704.5 22.1 %collective-permute-done.27.refs_3_ = bf16[512,2048]{1,0:T(8,128)(2,1)S(1)} collective-permute-done((bf16[512,2048]{1,0:T(8,128)(2,1)S(1)}, bf16[512,2048]{1,0:T(8,128)(2,1)S(1)}, u32[]{:S(2)}, u32[]{:S(2)}) %collective-permute-start.27) | collective-permute-done | bytes 2097184 | tf_op jit(solution)/shard_map/ppermute | solution.py:451
  738.6 16.5 multiply_convert_fusion.7
  755.1 11.9 multiply_convert_fusion.6
  767.1 18.6 collective-permute-done.28.refs_0_
  788.4 46.1 %collective-permute-done.29.refs_1_ = bf16[512,1024]{1,0:T(8,128)(2,1)S(1)} collective-permute-done((bf16[512,1024]{1,0:T(8,128)(2,1)S(1)}, bf16[512,1024]{1,0:T(8,128)(2,1)S(1)}, u32[]{:S(2)}, u32[]{:S(2)}) %collective-permute-start.29) | collective-permute-done | bytes 1048608 | tf_op jit(solution)/shard_map/ppermute | solution.py:451
  835.9 48.9 %slots.3 = (bf16[1728,2048]{1,0:T(8,128)(2,1)}, bf16[1728,2048]{1,0:T(8,128)(2,1)}, f32[2,1728,1]{2,1,0:T(8,128)}) custom-call(s32[4,2,2560]{2,1,0:T(2,128)} %get-tuple-element.181.slot_ref, f32[4,2,2560]{2,1,0:T(2,128)} %bitcast.137, f32[1,2048]{1,0:T(1,128)} %bitcast.148, bf16[10240,2048]{1,0:T(8,128)(2,1)} %all-gather.25.cloned.1.call-done.x_ref), custom_call_target="tpu_custom_call" | custom-call | flops 36238786560 | bytes 41943040 | tf_op jit(solution)/shard_map/slots/pallas_call | solution.py:386
  888.9 10.9 convolution_convert_fusion.8.refs_0_
  899.8 35.2 %collective-permute-done.31.refs_3_ = bf16[512,2048]{1,0:T(8,128)(2,1)S(1)} collective-permute-done((bf16[512,2048]{1,0:T(8,128)(2,1)S(1)}, bf16[512,2048]{1,0:T(8,128)(2,1)S(1)}, u32[]{:S(2)}, u32[]{:S(2)}) %collective-permute-start.31) | collective-permute-done | bytes 2097184 | tf_op jit(solution)/shard_map/ppermute | solution.py:451
  953.7 19.0 %multiply_convert_fusion.4 = (bf16[1728,1024]{1,0:T(8,128)(2,1)}, bf16[1728,1024]{1,0:T(8,128)(2,1)}) fusion(f32[1728,1024]{1,0:T(8,128)} %fusion.23, f32[1728,1024]{1,0:T(8,128)} %get-tuple-element.391, bf16[1728,2048]{1,0:T(8,128)(2,1)} %get-tuple-element.223, bf16[2048,2048]{1,0:T(8,128)(2,1)} %at_home.5), kind=kOutput, calls=%fused_computation.13 | convolution fusion | flops 7270760448 | bytes 32505856 | tf_op jit(solution)/shard_map/dot_general | solution.py:59
  972.7 13.5 fusion.21
  988.2 19.4 %multiply_convert_fusion.2 = (bf16[1728,1024]{1,0:T(8,128)(2,1)}, bf16[1728,1024]{1,0:T(8,128)(2,1)}) fusion(f32[1728,1024]{1,0:T(8,128)} %fusion.19, f32[1728,1024]{1,0:T(8,128)} %get-tuple-element.393, bf16[1728,2048]{1,0:T(8,128)(2,1)} %get-tuple-element.227, bf16[2048,2048]{1,0:T(8,128)(2,1)} %at_home.5), kind=kOutput, calls=%fused_computation.11 | convolution fusion | flops 7270760448 | bytes 32505856 | tf_op jit(solution)/shard_map/dot_general | solution.py:59
  1007.6 13.5 fusion.17
  1021.1 13.3 collective-permute-done.33.refs_3_
  1035.5 14.4 add_convert_fusion.1
  1049.9 13.7 add_convert_fusion
  1063.6 51.1 %combine.3 = bf16[10240,2048]{1,0:T(8,128)(2,1)} custom-call(s32[10240,2]{1,0:T(8,128)} %bitcast.125, bf16[4,432,2048]{2,1,0:T(8,128)(2,1)} %bitcast.155, bf16[4,432,2048]{2,1,0:T(8,128)(2,1)} %bitcast.156), custom_call_target="tpu_custom_call" | custom-call | flops 36238786560 | bytes 41943040 | tf_op jit(solution)/shard_map/combine/pallas_call | solution.py:432
  1124.2 12.4 convolution_convert_fusion.6.refs_0_
  1146.4 10.5 convolution_convert_fusion.5.refs_1_
  1191.5 28.1 %combine.5 = bf16[5120,2048]{1,0:T(8,128)(2,1)} custom-call(s32[10240,2]{1,0:T(8,128)} %bitcast.126, bf16[4,432,2048]{2,1,0:T(8,128)(2,1)} %bitcast.151, bf16[4,432,2048]{2,1,0:T(8,128)(2,1)} %bitcast.153), custom_call_target="tpu_custom_call" | custom-call | flops 18119393280 | bytes 20971520 | tf_op jit(solution)/shard_map/combine/pallas_call | solution.py:432
  1219.6 28.2 %combine.4 = bf16[5120,2048]{1,0:T(8,128)(2,1)} custom-call(s32[10240,2]{1,0:T(8,128)} %bitcast.127, bf16[4,432,2048]{2,1,0:T(8,128)(2,1)} %bitcast.152, bf16[4,432,2048]{2,1,0:T(8,128)(2,1)} %bitcast.154), custom_call_target="tpu_custom_call" | custom-call | flops 18119393280 | bytes 20971520 | tf_op jit(solution)/shard_map/combine/pallas_call | solution.py:432
  1263.7 22.7 %collective-permute-done.43.refs_7_ = bf16[512,1024]{1,0:T(8,128)(2,1)} collective-permute-done((bf16[512,1024]{1,0:T(8,128)(2,1)S(1)}, bf16[512,1024]{1,0:T(8,128)(2,1)}, u32[]{:S(2)}, u32[]{:S(2)}) %collective-permute-start.43) | collective-permute-done | bytes 1048608 | tf_op jit(solution)/shard_map/ppermute | solution.py:451
  1286.3 22.3 %collective-permute-done.42.refs_6_ = bf16[512,1024]{1,0:T(8,128)(2,1)} collective-permute-done((bf16[512,1024]{1,0:T(8,128)(2,1)S(1)}, bf16[512,1024]{1,0:T(8,128)(2,1)}, u32[]{:S(2)}, u32[]{:S(2)}) %collective-permute-start.42) | collective-permute-done | bytes 1048608 | tf_op jit(solution)/shard_map/ppermute | solution.py:451
  1308.6 43.4 %collective-permute-done.41.refs_5_ = bf16[512,1024]{1,0:T(8,128)(2,1)} collective-permute-done((bf16[512,1024]{1,0:T(8,128)(2,1)S(1)}, bf16[512,1024]{1,0:T(8,128)(2,1)}, u32[]{:S(2)}, u32[]{:S(2)}) %collective-permute-start.41) | collective-permute-done | bytes 1048608 | tf_op jit(solution)/shard_map/ppermute | solution.py:451
  1368.0 27.2 %collective-permute-done.44 = bf16[2560,256]{1,0:T(8,128)(2,1)} collective-permute-done((bf16[2560,256]{1,0:T(8,128)(2,1)}, bf16[2560,256]{1,0:T(8,128)(2,1)}, u32[]{:S(2)}, u32[]{:S(2)}) %collective-permute-start.44) | collective-permute-done | bytes 1310752 | tf_op jit(solution)/shard_map/ppermute | solution.py:620
  1411.5 46.2 %collective-permute-done.49.refs_3_ = bf16[512,1024]{1,0:T(8,128)(2,1)S(1)} collective-permute-done((bf16[512,1024]{1,0:T(8,128)(2,1)}, bf16[512,1024]{1,0:T(8,128)(2,1)S(1)}, u32[]{:S(2)}, u32[]{:S(2)}) %collective-permute-start.49) | collective-permute-done | bytes 1048608 | tf_op jit(solution)/shard_map/ppermute | solution.py:451
  1457.7 20.6 %collective-permute-done.48.refs_2_ = bf16[512,1024]{1,0:T(8,128)(2,1)} collective-permute-done((bf16[512,1024]{1,0:T(8,128)(2,1)S(1)}, bf16[512,1024]{1,0:T(8,128)(2,1)}, u32[]{:S(2)}, u32[]{:S(2)}) %collective-permute-start.48) | collective-permute-done | bytes 1048608 | tf_op jit(solution)/shard_map/ppermute | solution.py:451
  1548.6 36.4 %collective-permute-done.52.refs_4_ = bf16[512,1024]{1,0:T(8,128)(2,1)S(1)} collective-permute-done((bf16[512,1024]{1,0:T(8,128)(2,1)S(1)}, bf16[512,1024]{1,0:T(8,128)(2,1)S(1)}, u32[]{:S(2)}, u32[]{:S(2)}) %collective-permute-start.52) | collective-permute-done | bytes 1048608 | tf_op jit(solution)/shard_map/ppermute | solution.py:451
  1586.0 15.4 all-gather.27.cloned.1.call-done
  1611.7 11.9 collective-permute-done.53
  1642.4 21.4 %tree_backward.1 = (f32[2560,256]{1,0:T(8,128)}, f32[2560,256]{1,0:T(8,128)}, bf16[2560,256]{1,0:T(8,128)(2,1)S(1)}) custom-call(s32[1,20]{1,0:T(1,128)S(1)} %copy-done.18, bf16[2560,256]{1,0:T(8,128)(2,1)S(1)} %get-tuple-element.286.qr_ref, bf16[2560,256]{1,0:T(8,128)(2,1)S(1)} %copy-done.3, bf16[2560,256]{1,0:T(8,128)(2,1)} %get-tuple-element.288.vl_ref, ...), custom_call_target="tpu_custom_call" | custom-call | tf_op jit(solution)/shard_map/tree_backward/pallas_call | solution.py:333
  1668.0 14.5 collective-permute-start.57
  1734.7 12.5 convolution_convert_fusion.9
  1767.3 15.0 collective-permute-done.71
  1806.2 12.6 collective-permute-done.73
  (560 shorter events, 611.0 us)
Async XLA Ops:
  7.2 69.7 %all-gather.17.cloned.1.call-start = ((), (), s32[]{:S(2)}) async-start(), calls=%async_computation.5 | async-start | bytes 3932160 | tf_op jit(solution)/shard_map/all_gather | solution.py:657
  13.8 152.1 %all-gather.19.cloned.1.call-start = ((), (), s32[]{:S(2)}) async-start(), calls=%async_computation.6 | async-start | bytes 1310720 | tf_op jit(solution)/shard_map/all_gather | solution.py:660
  76.9 195.5 %reduce-scatter.6.cloned.1.call-start = ((), (), s32[]{:S(2)}) async-start(), calls=%async_computation.7 | async-start | bytes 11796480 | tf_op jit(solution)/shard_map/reduce_scatter | solution.py:683
  76.9 46.7 %collective-permute-start.8 = (bf16[2560,256]{1,0:T(8,128)(2,1)S(1)}, bf16[2560,256]{1,0:T(8,128)(2,1)}, u32[]{:S(2)}, u32[]{:S(2)}) collective-permute-start(bf16[2560,256]{1,0:T(8,128)(2,1)S(1)} %copy-done.30), channel_id=1, source_target_pairs={{0,8},{8,16},{16,24},{1,9},{9,17},{17,25},{2,10},{10,18},{18,26},{... | collective-permute-start | bytes 3932168 | tf_op jit(solution)/shard_map/ppermute | solution.py:588
  79.6 49.3 %collective-permute-start.9 = (bf16[2560,256]{1,0:T(8,128)(2,1)S(1)}, bf16[2560,256]{1,0:T(8,128)(2,1)}, u32[]{:S(2)}, u32[]{:S(2)}) collective-permute-start(bf16[2560,256]{1,0:T(8,128)(2,1)S(1)} %copy-done.30), channel_id=1, source_target_pairs={{8,0},{16,8},{24,16},{9,1},{17,9},{25,17},{10,2},{18,10},{26,18},{... | collective-permute-start | bytes 3932168 | tf_op jit(solution)/shard_map/ppermute | solution.py:589
  128.9 44.4 %collective-permute-start.10 = (bf16[2560,256]{1,0:T(8,128)(2,1)}, bf16[2560,256]{1,0:T(8,128)(2,1)}, u32[]{:S(2)}, u32[]{:S(2)}) collective-permute-start(bf16[2560,256]{1,0:T(8,128)(2,1)} %collective-permute-done.8), channel_id=1, source_target_pairs={{0,8},{8,16},{16,24},{1,9},{9,17},{17,25},{2,10},{10,18},{18,26},{... | collective-permute-start | bytes 3932168 | tf_op jit(solution)/shard_map/ppermute | solution.py:588
  132.8 40.5 %collective-permute-start.11 = (bf16[2560,256]{1,0:T(8,128)(2,1)}, bf16[2560,256]{1,0:T(8,128)(2,1)}, u32[]{:S(2)}, u32[]{:S(2)}) collective-permute-start(bf16[2560,256]{1,0:T(8,128)(2,1)} %collective-permute-done.9), channel_id=1, source_target_pairs={{8,0},{16,8},{24,16},{9,1},{17,9},{25,17},{10,2},{18,10},{26,18},{... | collective-permute-start | bytes 3932168 | tf_op jit(solution)/shard_map/ppermute | solution.py:589
  173.3 242.6 %all-gather.21.cloned.1.call-start = ((), (), s32[]{:S(2)}) async-start(), calls=%async_computation.8 | async-start | bytes 6553600 | tf_op jit(solution)/shard_map/all_gather | solution.py:696
  196.4 75.9 %collective-permute-start.12 = (bf16[512,2048]{1,0:T(8,128)(2,1)S(1)}, bf16[512,2048]{1,0:T(8,128)(2,1)}, u32[]{:S(2)}, u32[]{:S(2)}) collective-permute-start(bf16[512,2048]{1,0:T(8,128)(2,1)S(1)} %constant_dynamic-slice_fusion.37), channel_id=1, source_target_pairs={{0,8},{8,16},{16,24},{24,0},{1,9},{9,17},{17,25},{25,1},{2,10},{10... | collective-permute-start | bytes 6291464 | tf_op jit(solution)/shard_map/ppermute | solution.py:451
  197.8 74.5 %collective-permute-start.14 = (bf16[2560,256]{1,0:T(8,128)(2,1)}, bf16[2560,256]{1,0:T(8,128)(2,1)}, u32[]{:S(2)}, u32[]{:S(2)}) collective-permute-start(bf16[2560,256]{1,0:T(8,128)(2,1)} %collective-permute-done.11), channel_id=1, source_target_pairs={{8,0},{16,8},{24,16},{9,1},{17,9},{25,17},{10,2},{18,10},{26,18},{... | collective-permute-start | bytes 3932168 | tf_op jit(solution)/shard_map/ppermute | solution.py:589
  275.8 345.6 %all-gather.23.cloned.1.call-start = ((), (), s32[]{:S(2)}) async-start(), calls=%async_computation.9 | async-start | bytes 47185920 | tf_op jit(solution)/shard_map/all_gather | solution.py:714
  292.1 107.6 %collective-permute-start.21 = (bf16[512,1024]{1,0:T(8,128)(2,1)S(1)}, bf16[512,1024]{1,0:T(8,128)(2,1)S(1)}, u32[]{:S(2)}, u32[]{:S(2)}) collective-permute-start(bf16[512,1024]{1,0:T(8,128)(2,1)S(1)} %constant_dynamic-slice_fusion.36), channel_id=1, source_target_pairs={{0,16},{8,24},{16,0},{24,8},{1,17},{9,25},{17,1},{25,9},{2,18},{10... | collective-permute-start | bytes 3145736 | tf_op jit(solution)/shard_map/ppermute | solution.py:451
  416.0 418.6 %all-gather.25.cloned.1.call-start = ((), (), s32[]{:S(2)}) async-start(), calls=%async_computation.10 | async-start | bytes 47185920 | tf_op jit(solution)/shard_map/all_gather | solution.py:723
  417.3 46.4 %collective-permute-start.22 = (bf16[512,1024]{1,0:T(8,128)(2,1)S(1)}, bf16[512,1024]{1,0:T(8,128)(2,1)}, u32[]{:S(2)}, u32[]{:S(2)}) collective-permute-start(bf16[512,1024]{1,0:T(8,128)(2,1)S(1)} %constant_dynamic-slice_fusion.35), channel_id=1, source_target_pairs={{0,16},{8,24},{16,0},{24,8},{1,17},{9,25},{17,1},{25,9},{2,18},{10... | collective-permute-start | bytes 3145736 | tf_op jit(solution)/shard_map/ppermute | solution.py:451
  465.6 47.6 %collective-permute-start.23 = (bf16[512,2048]{1,0:T(8,128)(2,1)S(1)}, bf16[512,2048]{1,0:T(8,128)(2,1)S(1)}, u32[]{:S(2)}, u32[]{:S(2)}) collective-permute-start(bf16[512,2048]{1,0:T(8,128)(2,1)S(1)} %constant_dynamic-slice_fusion.34), channel_id=1, source_target_pairs={{0,24},{8,0},{16,8},{24,16},{1,25},{9,1},{17,9},{25,17},{2,26},{10... | collective-permute-start | bytes 6291464 | tf_op jit(solution)/shard_map/ppermute | solution.py:451
  515.9 48.8 %collective-permute-start.24 = (bf16[512,2048]{1,0:T(8,128)(2,1)S(1)}, bf16[512,2048]{1,0:T(8,128)(2,1)}, u32[]{:S(2)}, u32[]{:S(2)}) collective-permute-start(bf16[512,2048]{1,0:T(8,128)(2,1)S(1)} %constant_dynamic-slice_fusion.33), channel_id=1, source_target_pairs={{0,8},{8,16},{16,24},{24,0},{1,9},{9,17},{17,25},{25,1},{2,10},{10... | collective-permute-start | bytes 6291464 | tf_op jit(solution)/shard_map/ppermute | solution.py:451
  565.9 45.1 %collective-permute-start.25 = (bf16[512,1024]{1,0:T(8,128)(2,1)S(1)}, bf16[512,1024]{1,0:T(8,128)(2,1)S(1)}, u32[]{:S(2)}, u32[]{:S(2)}) collective-permute-start(bf16[512,1024]{1,0:T(8,128)(2,1)S(1)} %constant_dynamic-slice_fusion.32), channel_id=1, source_target_pairs={{0,16},{8,24},{16,0},{24,8},{1,17},{9,25},{17,1},{25,9},{2,18},{10... | collective-permute-start | bytes 3145736 | tf_op jit(solution)/shard_map/ppermute | solution.py:451
  621.5 737.8 %reduce-scatter.8.cloned.1.call-start = ((), (), s32[]{:S(2)}) async-start(), calls=%async_computation.11 | async-start | bytes 47185920 | tf_op jit(solution)/shard_map/reduce_scatter | solution.py:781
  622.8 54.1 %collective-permute-start.26 = (bf16[512,1024]{1,0:T(8,128)(2,1)S(1)}, bf16[512,1024]{1,0:T(8,128)(2,1)S(1)}, u32[]{:S(2)}, u32[]{:S(2)}) collective-permute-start(bf16[512,1024]{1,0:T(8,128)(2,1)S(1)} %constant_dynamic-slice_fusion.31), channel_id=1, source_target_pairs={{0,16},{8,24},{16,0},{24,8},{1,17},{9,25},{17,1},{25,9},{2,18},{10... | collective-permute-start | bytes 3145736 | tf_op jit(solution)/shard_map/ppermute | solution.py:451
  678.9 47.7 %collective-permute-start.27 = (bf16[512,2048]{1,0:T(8,128)(2,1)S(1)}, bf16[512,2048]{1,0:T(8,128)(2,1)S(1)}, u32[]{:S(2)}, u32[]{:S(2)}) collective-permute-start(bf16[512,2048]{1,0:T(8,128)(2,1)S(1)} %constant_dynamic-slice_fusion.30), channel_id=1, source_target_pairs={{0,24},{8,0},{16,8},{24,16},{1,25},{9,1},{17,9},{25,17},{2,26},{10... | collective-permute-start | bytes 6291464 | tf_op jit(solution)/shard_map/ppermute | solution.py:451
  736.6 49.1 %collective-permute-start.28 = (bf16[512,2048]{1,0:T(8,128)(2,1)S(1)}, bf16[512,2048]{1,0:T(8,128)(2,1)S(1)}, u32[]{:S(2)}, u32[]{:S(2)}) collective-permute-start(bf16[512,2048]{1,0:T(8,128)(2,1)S(1)} %constant_dynamic-slice_fusion.29), channel_id=1, source_target_pairs={{0,8},{8,16},{16,24},{24,0},{1,9},{9,17},{17,25},{25,1},{2,10},{10... | collective-permute-start | bytes 6291464 | tf_op jit(solution)/shard_map/ppermute | solution.py:451
  788.3 46.2 %collective-permute-start.29 = (bf16[512,1024]{1,0:T(8,128)(2,1)S(1)}, bf16[512,1024]{1,0:T(8,128)(2,1)S(1)}, u32[]{:S(2)}, u32[]{:S(2)}) collective-permute-start(bf16[512,1024]{1,0:T(8,128)(2,1)S(1)} %constant_dynamic-slice_fusion.28), channel_id=1, source_target_pairs={{0,16},{8,24},{16,0},{24,8},{1,17},{9,25},{17,1},{25,9},{2,18},{10... | collective-permute-start | bytes 3145736 | tf_op jit(solution)/shard_map/ppermute | solution.py:451
  835.8 49.0 %collective-permute-start.30 = (bf16[512,1024]{1,0:T(8,128)(2,1)S(1)}, bf16[512,1024]{1,0:T(8,128)(2,1)S(1)}, u32[]{:S(2)}, u32[]{:S(2)}) collective-permute-start(bf16[512,1024]{1,0:T(8,128)(2,1)S(1)} %constant_dynamic-slice_fusion.27), channel_id=1, source_target_pairs={{0,16},{8,24},{16,0},{24,8},{1,17},{9,25},{17,1},{25,9},{2,18},{10... | collective-permute-start | bytes 3145736 | tf_op jit(solution)/shard_map/ppermute | solution.py:451
  886.9 48.1 %collective-permute-start.31 = (bf16[512,2048]{1,0:T(8,128)(2,1)S(1)}, bf16[512,2048]{1,0:T(8,128)(2,1)S(1)}, u32[]{:S(2)}, u32[]{:S(2)}) collective-permute-start(bf16[512,2048]{1,0:T(8,128)(2,1)S(1)} %constant_dynamic-slice_fusion.26), channel_id=1, source_target_pairs={{0,24},{8,0},{16,8},{24,16},{1,25},{9,1},{17,9},{25,17},{2,26},{10... | collective-permute-start | bytes 6291464 | tf_op jit(solution)/shard_map/ppermute | solution.py:451
  935.1 51.2 %collective-permute-start.32 = (bf16[512,1024]{1,0:T(8,128)(2,1)S(1)}, bf16[512,1024]{1,0:T(8,128)(2,1)S(1)}, u32[]{:S(2)}, u32[]{:S(2)}) collective-permute-start(bf16[512,1024]{1,0:T(8,128)(2,1)S(1)} %constant_dynamic-slice_fusion.25), channel_id=1, source_target_pairs={{0,16},{8,24},{16,0},{24,8},{1,17},{9,25},{17,1},{25,9},{2,18},{10... | collective-permute-start | bytes 3145736 | tf_op jit(solution)/shard_map/ppermute | solution.py:451
  988.1 46.3 %collective-permute-start.33 = (bf16[512,1024]{1,0:T(8,128)(2,1)S(1)}, bf16[512,1024]{1,0:T(8,128)(2,1)S(1)}, u32[]{:S(2)}, u32[]{:S(2)}) collective-permute-start(bf16[512,1024]{1,0:T(8,128)(2,1)S(1)} %constant_dynamic-slice_fusion.24), channel_id=1, source_target_pairs={{0,8},{8,16},{16,24},{24,0},{1,9},{9,17},{17,25},{25,1},{2,10},{10... | collective-permute-start | bytes 3145736 | tf_op jit(solution)/shard_map/ppermute | solution.py:451
  1035.5 79.3 %collective-permute-start.35 = (bf16[512,1024]{1,0:T(8,128)(2,1)}, bf16[512,1024]{1,0:T(8,128)(2,1)}, u32[]{:S(2)}, u32[]{:S(2)}) collective-permute-start(bf16[512,1024]{1,0:T(8,128)(2,1)} %constant_dynamic-slice_fusion.22), channel_id=1, source_target_pairs={{0,16},{8,24},{16,0},{24,8},{1,17},{9,25},{17,1},{25,9},{2,18},{10... | collective-permute-start | bytes 3145736 | tf_op jit(solution)/shard_map/ppermute | solution.py:451
  1114.8 418.5 %reduce-scatter.10.cloned.1.call-start = ((), (), s32[]{:S(2)}) async-start(), calls=%async_computation.12 | async-start | bytes 23592960 | tf_op jit(solution)/shard_map/reduce_scatter | solution.py:798
  1118.1 48.9 %collective-permute-start.37 = (bf16[512,1024]{1,0:T(8,128)(2,1)S(1)}, bf16[512,1024]{1,0:T(8,128)(2,1)S(1)}, u32[]{:S(2)}, u32[]{:S(2)}) collective-permute-start(bf16[512,1024]{1,0:T(8,128)(2,1)S(1)} %constant_dynamic-slice_fusion.20), channel_id=1, source_target_pairs={{0,24},{8,0},{16,8},{24,16},{1,25},{9,1},{17,9},{25,17},{2,26},{10... | collective-permute-start | bytes 3145736 | tf_op jit(solution)/shard_map/ppermute | solution.py:451
  1122.0 45.0 %collective-permute-start.36 = (bf16[512,1024]{1,0:T(8,128)(2,1)S(1)}, bf16[512,1024]{1,0:T(8,128)(2,1)S(1)}, u32[]{:S(2)}, u32[]{:S(2)}) collective-permute-start(bf16[512,1024]{1,0:T(8,128)(2,1)S(1)} %constant_dynamic-slice_fusion.21), channel_id=1, source_target_pairs={{0,24},{8,0},{16,8},{24,16},{1,25},{9,1},{17,9},{25,17},{2,26},{10... | collective-permute-start | bytes 3145736 | tf_op jit(solution)/shard_map/ppermute | solution.py:451
  1167.1 88.6 %collective-permute-start.40 = (bf16[512,1024]{1,0:T(8,128)(2,1)S(1)}, bf16[512,1024]{1,0:T(8,128)(2,1)S(1)}, u32[]{:S(2)}, u32[]{:S(2)}) collective-permute-start(bf16[512,1024]{1,0:T(8,128)(2,1)S(1)} %constant_dynamic-slice_fusion.17), channel_id=1, source_target_pairs={{0,16},{8,24},{16,0},{24,8},{1,17},{9,25},{17,1},{25,9},{2,18},{10... | collective-permute-start | bytes 3145736 | tf_op jit(solution)/shard_map/ppermute | solution.py:451
  1168.2 87.5 %collective-permute-start.39 = (bf16[512,1024]{1,0:T(8,128)(2,1)}, bf16[512,1024]{1,0:T(8,128)(2,1)}, u32[]{:S(2)}, u32[]{:S(2)}) collective-permute-start(bf16[512,1024]{1,0:T(8,128)(2,1)} %constant_dynamic-slice_fusion.18), channel_id=1, source_target_pairs={{0,8},{8,16},{16,24},{24,0},{1,9},{9,17},{17,25},{25,1},{2,10},{10... | collective-permute-start | bytes 3145736 | tf_op jit(solution)/shard_map/ppermute | solution.py:451
  1170.4 85.3 %collective-permute-start.38 = (bf16[512,1024]{1,0:T(8,128)(2,1)}, bf16[512,1024]{1,0:T(8,128)(2,1)}, u32[]{:S(2)}, u32[]{:S(2)}) collective-permute-start(bf16[512,1024]{1,0:T(8,128)(2,1)} %constant_dynamic-slice_fusion.19), channel_id=1, source_target_pairs={{0,8},{8,16},{16,24},{24,0},{1,9},{9,17},{17,25},{25,1},{2,10},{10... | collective-permute-start | bytes 3145736 | tf_op jit(solution)/shard_map/ppermute | solution.py:451
  1260.2 48.4 %collective-permute-start.42 = (bf16[512,1024]{1,0:T(8,128)(2,1)S(1)}, bf16[512,1024]{1,0:T(8,128)(2,1)}, u32[]{:S(2)}, u32[]{:S(2)}) collective-permute-start(bf16[512,1024]{1,0:T(8,128)(2,1)S(1)} %constant_dynamic-slice_fusion.15), channel_id=1, source_target_pairs={{0,24},{8,0},{16,8},{24,16},{1,25},{9,1},{17,9},{25,17},{2,26},{10... | collective-permute-start | bytes 3145736 | tf_op jit(solution)/shard_map/ppermute | solution.py:451
  1262.6 89.4 %collective-permute-start.41 = (bf16[512,1024]{1,0:T(8,128)(2,1)S(1)}, bf16[512,1024]{1,0:T(8,128)(2,1)}, u32[]{:S(2)}, u32[]{:S(2)}) collective-permute-start(bf16[512,1024]{1,0:T(8,128)(2,1)S(1)} %constant_dynamic-slice_fusion.16), channel_id=1, source_target_pairs={{0,16},{8,24},{16,0},{24,8},{1,17},{9,25},{17,1},{25,9},{2,18},{10... | collective-permute-start | bytes 3145736 | tf_op jit(solution)/shard_map/ppermute | solution.py:451
  1359.3 242.2 %all-gather.27.cloned.1.call-start = ((), (), s32[]{:S(2)}) async-start(), calls=%async_computation.13 | async-start | bytes 11796480 | tf_op jit(solution)/shard_map/all_gather | solution.py:815
  1399.4 78.9 %collective-permute-start.47 = (bf16[2560,256]{1,0:T(8,128)(2,1)}, bf16[2560,256]{1,0:T(8,128)(2,1)}, u32[]{:S(2)}, u32[]{:S(2)}) collective-permute-start(bf16[2560,256]{1,0:T(8,128)(2,1)} %get-tuple-element.348), channel_id=1, source_target_pairs={{24,16},{16,8},{25,17},{17,9},{26,18},{18,10},{27,19},{19,11},{28,... | collective-permute-start | bytes 3932168 | tf_op jit(solution)/shard_map/ppermute | solution.py:621
  1401.2 77.1 %collective-permute-start.46 = (bf16[2560,256]{1,0:T(8,128)(2,1)}, bf16[2560,256]{1,0:T(8,128)(2,1)}, u32[]{:S(2)}, u32[]{:S(2)}) collective-permute-start(bf16[2560,256]{1,0:T(8,128)(2,1)} %get-tuple-element.349), channel_id=1, source_target_pairs={{0,8},{8,16},{1,9},{9,17},{2,10},{10,18},{3,11},{11,19},{4,12},{12... | collective-permute-start | bytes 3932168 | tf_op jit(solution)/shard_map/ppermute | solution.py:620
  1409.8 48.0 %collective-permute-start.49 = (bf16[512,1024]{1,0:T(8,128)(2,1)}, bf16[512,1024]{1,0:T(8,128)(2,1)S(1)}, u32[]{:S(2)}, u32[]{:S(2)}) collective-permute-start(bf16[512,1024]{1,0:T(8,128)(2,1)} %constant_dynamic-slice_fusion.10), channel_id=1, source_target_pairs={{0,8},{8,16},{16,24},{24,0},{1,9},{9,17},{17,25},{25,1},{2,10},{10... | collective-permute-start | bytes 3145736 | tf_op jit(solution)/shard_map/ppermute | solution.py:451
  1411.3 67.0 %collective-permute-start.48 = (bf16[512,1024]{1,0:T(8,128)(2,1)S(1)}, bf16[512,1024]{1,0:T(8,128)(2,1)}, u32[]{:S(2)}, u32[]{:S(2)}) collective-permute-start(bf16[512,1024]{1,0:T(8,128)(2,1)S(1)} %constant_dynamic-slice_fusion.11), channel_id=1, source_target_pairs={{0,8},{8,16},{16,24},{24,0},{1,9},{9,17},{17,25},{25,1},{2,10},{10... | collective-permute-start | bytes 3145736 | tf_op jit(solution)/shard_map/ppermute | solution.py:451
  1533.3 220.3 %reduce-scatter.12.cloned.1.call-start = ((), (), s32[]{:S(2)}) async-start(), calls=%async_computation.14 | async-start | bytes 23592960 | tf_op jit(solution)/shard_map/reduce_scatter | solution.py:817
  1534.7 50.4 %collective-permute-start.52 = (bf16[512,1024]{1,0:T(8,128)(2,1)S(1)}, bf16[512,1024]{1,0:T(8,128)(2,1)S(1)}, u32[]{:S(2)}, u32[]{:S(2)}) collective-permute-start(bf16[512,1024]{1,0:T(8,128)(2,1)S(1)} %constant_dynamic-slice_fusion.9), channel_id=1, source_target_pairs={{0,16},{8,24},{16,0},{24,8},{1,17},{9,25},{17,1},{25,9},{2,18},{10... | collective-permute-start | bytes 3145736 | tf_op jit(solution)/shard_map/ppermute | solution.py:451
  1601.5 257.7 %reduce-scatter.14.cloned.1.call-start = ((), (), s32[]{:S(2)}) async-start(), calls=%async_computation.15 | async-start | bytes 11796480 | tf_op jit(solution)/shard_map/reduce_scatter | solution.py:854
  1611.4 87.9 %collective-permute-start.59 = (bf16[512,1024]{1,0:T(8,128)(2,1)}, bf16[512,1024]{1,0:T(8,128)(2,1)}, u32[]{:S(2)}, u32[]{:S(2)}) collective-permute-start(bf16[512,1024]{1,0:T(8,128)(2,1)} %constant_dynamic-slice_fusion.6), channel_id=1, source_target_pairs={{0,16},{8,24},{16,0},{24,8},{1,17},{9,25},{17,1},{25,9},{2,18},{10... | collective-permute-start | bytes 3145736 | tf_op jit(solution)/shard_map/ppermute | solution.py:451
  1701.6 51.9 %collective-permute-start.61 = (bf16[512,1024]{1,0:T(8,128)(2,1)}, bf16[512,1024]{1,0:T(8,128)(2,1)}, u32[]{:S(2)}, u32[]{:S(2)}) collective-permute-start(bf16[512,1024]{1,0:T(8,128)(2,1)} %constant_dynamic-slice_fusion.4), channel_id=1, source_target_pairs={{0,24},{8,0},{16,8},{24,16},{1,25},{9,1},{17,9},{25,17},{2,26},{10... | collective-permute-start | bytes 3145736 | tf_op jit(solution)/shard_map/ppermute | solution.py:451
  1706.5 47.1 %collective-permute-start.60 = (bf16[512,1024]{1,0:T(8,128)(2,1)}, bf16[512,1024]{1,0:T(8,128)(2,1)}, u32[]{:S(2)}, u32[]{:S(2)}) collective-permute-start(bf16[512,1024]{1,0:T(8,128)(2,1)} %constant_dynamic-slice_fusion.5), channel_id=1, source_target_pairs={{0,24},{8,0},{16,8},{24,16},{1,25},{9,1},{17,9},{25,17},{2,26},{10... | collective-permute-start | bytes 3145736 | tf_op jit(solution)/shard_map/ppermute | solution.py:451
  1799.5 40.2 %collective-permute-start.65 = (bf16[1280,256]{1,0:T(8,128)(2,1)}, bf16[1280,256]{1,0:T(8,128)(2,1)}, u32[]{:S(2)}, u32[]{:S(2)}) collective-permute-start(bf16[1280,256]{1,0:T(8,128)(2,1)} %get-tuple-element.360), channel_id=1, source_target_pairs={{24,16},{16,8},{25,17},{17,9},{26,18},{18,10},{27,19},{19,11},{28,... | collective-permute-start | bytes 1966088 | tf_op jit(solution)/shard_map/ppermute | solution.py:621
  1842.5 40.5 %collective-permute-start.67 = (bf16[1280,256]{1,0:T(8,128)(2,1)}, bf16[1280,256]{1,0:T(8,128)(2,1)}, u32[]{:S(2)}, u32[]{:S(2)}) collective-permute-start(bf16[1280,256]{1,0:T(8,128)(2,1)} %get-tuple-element.358), channel_id=1, source_target_pairs={{24,16},{16,8},{8,0},{25,17},{17,9},{9,1},{26,18},{18,10},{10,2},{... | collective-permute-start | bytes 1966088 | tf_op jit(solution)/shard_map/ppermute | solution.py:621
  (133 other events, 2675.2 us)
Sparse Core Ops, SparseCore 0:
  13.9 62.8 all-gather.16
  78.4 40.6 all-gather.18
  173.4 80.8 reduce-scatter.5
  276.0 139.9 all-gather.20
  417.7 203.7 all-gather.22
  623.2 205.4 all-gather.24
  1114.9 244.2 reduce-scatter.7
  1363.3 136.1 reduce-scatter.9
  1533.4 68.0 all-gather.26
  1605.3 136.6 reduce-scatter.11
  1753.7 79.1 reduce-scatter.13

commit v5 on v4

--- a/solution.py
+++ b/solution.py
@@ -676,18 +676,17 @@
     k_scale = lax.rsqrt(squares[1] / width + EPS)[:, None]
     q_gain = lax.dynamic_slice_in_dim(q_norm, col_start, own_width)
     k_gain = lax.dynamic_slice_in_dim(k_norm, col_start, own_width)
-    q_scale = after(q_scale, grad_steps[0])
     attended, q_rot, k_rot, value_low = attend(
         parents, qkv, q_scale, k_scale, q_gain, k_gain, cos_table, sin_table, heads
     )
     attn_sum = lax.psum_scatter(
-        after(contract_cols(attended, out_cols).astype(jnp.bfloat16), grad_steps[:-1]),
+        after(contract_cols(attended, out_cols).astype(jnp.bfloat16), grad_steps[0]),
         "col",
         scatter_dimension=1,
         tiled=True,
     )
-    route_all = row_stack(routes.T, grad_steps[:-1])
-    gate_all = row_stack(gates.T, grad_steps[:-1])
+    route_all = row_stack(routes.T, grad_steps[0])
+    gate_all = row_stack(gates.T, grad_steps[0])
     gate_units = [home_unit(w_gate, shifts[0], grad_steps[:-1])]
     attn_sum = after(attn_sum, gate_units, grad_steps, route_all, gate_all)
     residual = tokens.astype(jnp.float32) + attn_sum.astype(jnp.float32)

time: 1900 us -> 1910 us (level)
    ppermute x3, waiting for transfers between devices: 52.8 us -> 3.91 us  [line_steps(): lax.ppermute(downward, 'row', [(i + 1, i) for i in range(count - 1)])]
    ppermute x3, waiting for transfers between devices: 47 us -> 88.2 us  [line_steps(): upward = lax.ppermute(upward, 'row', [(i, i + 1) for i in range(count - 1)])]
    unnamed x225 -> x235, local copies, waits for them, and re-layouts: 38.5 us -> 39.2 us
  transfers between devices with their start and end apart: 88 -> 88, of which waited for: 41 -> 40; matrix products, arithmetic and copies ran while one was open for 25% -> 25% of each run, Pallas kernels for 16% -> 16%
where the time goes in v5:
time: 1910 us; the launch traced here: 1890 us
  waiting for transfers between devices  868 us (45%)
  Pallas kernels  295 us (15%)
  matrix products  281 us (15%)
  starting transfers between devices  166 us (9%)
  local copies, waits for them, and re-layouts  113 us (6%)
  other arithmetic  103 us (5%)
  blocking collectives  46.7 us (2%)
    ppermute x39, waiting for transfers between devices, shift_row(): lax.ppermute(block, 'row', [(i, (i + k) % count) for i in range(count)])  617 us
    dot_general x22, matrix products, dot_f32(): lax.dot_general(left, right, (((left_dim,), (right_dim,)), ((), ())), pre...  260 us
    pallas_call x3, Pallas kernels, combine(): pl.pallas_call(combine_kernel, grid=(groups, steps), in_specs=[pl.BlockSp...  107 us
    pallas_call x2, Pallas kernels, to_slots(): pl.pallas_call(functools.partial(slots_kernel, normed=normed), grid=(grou...  100 us
    ppermute x3, waiting for transfers between devices, line_steps(): upward = lax.ppermute(upward, 'row', [(i, i + 1) for i in range(count - 1)])  88.2 us
    ppermute x12, waiting for transfers between devices, group_total(): upward = lax.ppermute(upward, 'row', [(i, i + 1) for i in range(step)])  75.7 us
    ppermute x12, starting transfers between devices, group_total(): upward = lax.ppermute(upward, 'row', [(i, i + 1) for i in range(step)])  68 us
    ppermute x39, starting transfers between devices, shift_row(): lax.ppermute(block, 'row', [(i, (i + k) % count) for i in range(count)])  62.9 us
  transfers between devices with their start and end apart: 88, of which 40 were waited for; matrix products, arithmetic and copies ran while one was open for 25% of the time, Pallas kernels for 16%

profile of v5, /device:TPU:0, one launch (start us, length us, event | category | flops | bytes accessed | tf_op | source)
XLA Modules:
  0.0 1888.8 jit_solution(98850541949235225)
XLA Ops:
  85.6 12.6 fusion.26.q_ref.k_ref.v_ref
  115.1 17.8 tree_forward.1
  160.9 21.8 %collective-permute-done.10 = bf16[2560,256]{1,0:T(8,128)(2,1)S(1)} collective-permute-done((bf16[2560,256]{1,0:T(8,128)(2,1)}, bf16[2560,256]{1,0:T(8,128)(2,1)S(1)}, u32[]{:S(2)}, u32[]{:S(2)}) %collective-permute-start.10) | collective-permute-done | bytes 1310752 | tf_op jit(solution)/shard_map/ppermute | solution.py:588
  196.8 66.4 %collective-permute-done.13 = bf16[2560,256]{1,0:T(8,128)(2,1)S(1)} collective-permute-done((bf16[2560,256]{1,0:T(8,128)(2,1)S(1)}, bf16[2560,256]{1,0:T(8,128)(2,1)S(1)}, u32[]{:S(2)}, u32[]{:S(2)}) %collective-permute-start.13) | collective-permute-done | bytes 1310752 | tf_op jit(solution)/shard_map/ppermute | solution.py:588
  294.3 101.2 %collective-permute-done.21.refs_1_ = bf16[512,1024]{1,0:T(8,128)(2,1)S(1)} collective-permute-done((bf16[512,1024]{1,0:T(8,128)(2,1)S(1)}, bf16[512,1024]{1,0:T(8,128)(2,1)S(1)}, u32[]{:S(2)}, u32[]{:S(2)}) %collective-permute-start.21) | collective-permute-done | bytes 1048608 | tf_op jit(solution)/shard_map/ppermute | solution.py:451
  395.5 16.3 all-gather.21.cloned.1.call-done
  413.2 46.4 %collective-permute-done.22.refs_2_ = bf16[512,1024]{1,0:T(8,128)(2,1)} collective-permute-done((bf16[512,1024]{1,0:T(8,128)(2,1)S(1)}, bf16[512,1024]{1,0:T(8,128)(2,1)}, u32[]{:S(2)}, u32[]{:S(2)}) %collective-permute-start.22) | collective-permute-done | bytes 1048608 | tf_op jit(solution)/shard_map/ppermute | solution.py:451
  464.2 44.9 %collective-permute-done.23.refs_3_ = bf16[512,2048]{1,0:T(8,128)(2,1)S(1)} collective-permute-done((bf16[512,2048]{1,0:T(8,128)(2,1)S(1)}, bf16[512,2048]{1,0:T(8,128)(2,1)S(1)}, u32[]{:S(2)}, u32[]{:S(2)}) %collective-permute-start.23) | collective-permute-done | bytes 2097184 | tf_op jit(solution)/shard_map/ppermute | solution.py:451
  511.8 48.7 %collective-permute-done.24.refs_0_ = bf16[512,2048]{1,0:T(8,128)(2,1)} collective-permute-done((bf16[512,2048]{1,0:T(8,128)(2,1)S(1)}, bf16[512,2048]{1,0:T(8,128)(2,1)}, u32[]{:S(2)}, u32[]{:S(2)}) %collective-permute-start.24) | collective-permute-done | bytes 2097184 | tf_op jit(solution)/shard_map/ppermute | solution.py:451
  568.7 38.2 %collective-permute-done.25.refs_1_ = bf16[512,1024]{1,0:T(8,128)(2,1)S(1)} collective-permute-done((bf16[512,1024]{1,0:T(8,128)(2,1)S(1)}, bf16[512,1024]{1,0:T(8,128)(2,1)S(1)}, u32[]{:S(2)}, u32[]{:S(2)}) %collective-permute-start.25) | collective-permute-done | bytes 1048608 | tf_op jit(solution)/shard_map/ppermute | solution.py:451
  621.1 51.5 %slots.2 = (bf16[1728,2048]{1,0:T(8,128)(2,1)}, bf16[1728,2048]{1,0:T(8,128)(2,1)}, f32[2,1728,1]{2,1,0:T(8,128)}) custom-call(s32[4,2,2560]{2,1,0:T(2,128)} %get-tuple-element.179.slot_ref, f32[4,2,2560]{2,1,0:T(2,128)} %bitcast.136, f32[1,2048]{1,0:T(1,128)} %bitcast.147, bf16[10240,2048]{1,0:T(8,128)(2,1)} %all-gather.23.cloned.1.call-done.x_ref), custom_call_target="tpu_custom_call" | custom-call | flops 36238786560 | bytes 41943040 | tf_op jit(solution)/shard_map/slots/pallas_call | solution.py:386
  676.5 13.5 fusion.23
  690.0 10.4 fusion.19
  700.4 22.2 %collective-permute-done.27.refs_3_ = bf16[512,2048]{1,0:T(8,128)(2,1)S(1)} collective-permute-done((bf16[512,2048]{1,0:T(8,128)(2,1)S(1)}, bf16[512,2048]{1,0:T(8,128)(2,1)S(1)}, u32[]{:S(2)}, u32[]{:S(2)}) %collective-permute-start.27) | collective-permute-done | bytes 2097184 | tf_op jit(solution)/shard_map/ppermute | solution.py:451
  734.5 16.5 multiply_convert_fusion.7
  751.1 11.9 multiply_convert_fusion.6
  763.0 18.7 collective-permute-done.28.refs_0_
  784.5 46.1 %collective-permute-done.29.refs_1_ = bf16[512,1024]{1,0:T(8,128)(2,1)S(1)} collective-permute-done((bf16[512,1024]{1,0:T(8,128)(2,1)S(1)}, bf16[512,1024]{1,0:T(8,128)(2,1)S(1)}, u32[]{:S(2)}, u32[]{:S(2)}) %collective-permute-start.29) | collective-permute-done | bytes 1048608 | tf_op jit(solution)/shard_map/ppermute | solution.py:451
  832.0 48.9 %slots.3 = (bf16[1728,2048]{1,0:T(8,128)(2,1)}, bf16[1728,2048]{1,0:T(8,128)(2,1)}, f32[2,1728,1]{2,1,0:T(8,128)}) custom-call(s32[4,2,2560]{2,1,0:T(2,128)} %get-tuple-element.179.slot_ref, f32[4,2,2560]{2,1,0:T(2,128)} %bitcast.137, f32[1,2048]{1,0:T(1,128)} %bitcast.148, bf16[10240,2048]{1,0:T(8,128)(2,1)} %all-gather.25.cloned.1.call-done.x_ref), custom_call_target="tpu_custom_call" | custom-call | flops 36238786560 | bytes 41943040 | tf_op jit(solution)/shard_map/slots/pallas_call | solution.py:386
  885.2 10.7 convolution_convert_fusion.8.refs_0_
  895.8 35.3 %collective-permute-done.31.refs_3_ = bf16[512,2048]{1,0:T(8,128)(2,1)S(1)} collective-permute-done((bf16[512,2048]{1,0:T(8,128)(2,1)S(1)}, bf16[512,2048]{1,0:T(8,128)(2,1)S(1)}, u32[]{:S(2)}, u32[]{:S(2)}) %collective-permute-start.31) | collective-permute-done | bytes 2097184 | tf_op jit(solution)/shard_map/ppermute | solution.py:451
  949.7 19.1 %multiply_convert_fusion.4 = (bf16[1728,1024]{1,0:T(8,128)(2,1)}, bf16[1728,1024]{1,0:T(8,128)(2,1)}) fusion(f32[1728,1024]{1,0:T(8,128)} %fusion.23, f32[1728,1024]{1,0:T(8,128)} %get-tuple-element.388, bf16[1728,2048]{1,0:T(8,128)(2,1)} %get-tuple-element.221, bf16[2048,2048]{1,0:T(8,128)(2,1)} %at_home.5), kind=kOutput, calls=%fused_computation.13 | convolution fusion | flops 7270760448 | bytes 32505856 | tf_op jit(solution)/shard_map/dot_general | solution.py:59
  968.8 13.5 fusion.21
  984.4 19.3 %multiply_convert_fusion.2 = (bf16[1728,1024]{1,0:T(8,128)(2,1)}, bf16[1728,1024]{1,0:T(8,128)(2,1)}) fusion(f32[1728,1024]{1,0:T(8,128)} %fusion.19, f32[1728,1024]{1,0:T(8,128)} %get-tuple-element.390, bf16[1728,2048]{1,0:T(8,128)(2,1)} %get-tuple-element.225, bf16[2048,2048]{1,0:T(8,128)(2,1)} %at_home.5), kind=kOutput, calls=%fused_computation.11 | convolution fusion | flops 7270760448 | bytes 32505856 | tf_op jit(solution)/shard_map/dot_general | solution.py:59
  1003.7 13.4 fusion.17
  1017.1 13.4 collective-permute-done.33.refs_3_
  1031.6 14.4 add_convert_fusion.1
  1046.0 13.7 add_convert_fusion
  1059.7 51.2 %combine.3 = bf16[10240,2048]{1,0:T(8,128)(2,1)} custom-call(s32[10240,2]{1,0:T(8,128)} %bitcast.125, bf16[4,432,2048]{2,1,0:T(8,128)(2,1)} %bitcast.155, bf16[4,432,2048]{2,1,0:T(8,128)(2,1)} %bitcast.156), custom_call_target="tpu_custom_call" | custom-call | flops 36238786560 | bytes 41943040 | tf_op jit(solution)/shard_map/combine/pallas_call | solution.py:432
  1120.4 12.4 convolution_convert_fusion.6.refs_0_
  1142.6 10.4 convolution_convert_fusion.5.refs_1_
  1153.1 10.1 convolution_convert_fusion.3.refs_1_
  1187.7 28.2 %combine.5 = bf16[5120,2048]{1,0:T(8,128)(2,1)} custom-call(s32[10240,2]{1,0:T(8,128)} %bitcast.126, bf16[4,432,2048]{2,1,0:T(8,128)(2,1)} %bitcast.151, bf16[4,432,2048]{2,1,0:T(8,128)(2,1)} %bitcast.153), custom_call_target="tpu_custom_call" | custom-call | flops 18119393280 | bytes 20971520 | tf_op jit(solution)/shard_map/combine/pallas_call | solution.py:432
  1215.9 28.1 %combine.4 = bf16[5120,2048]{1,0:T(8,128)(2,1)} custom-call(s32[10240,2]{1,0:T(8,128)} %bitcast.127, bf16[4,432,2048]{2,1,0:T(8,128)(2,1)} %bitcast.152, bf16[4,432,2048]{2,1,0:T(8,128)(2,1)} %bitcast.154), custom_call_target="tpu_custom_call" | custom-call | flops 18119393280 | bytes 20971520 | tf_op jit(solution)/shard_map/combine/pallas_call | solution.py:432
  1259.8 22.6 %collective-permute-done.43.refs_7_ = bf16[512,1024]{1,0:T(8,128)(2,1)} collective-permute-done((bf16[512,1024]{1,0:T(8,128)(2,1)S(1)}, bf16[512,1024]{1,0:T(8,128)(2,1)}, u32[]{:S(2)}, u32[]{:S(2)}) %collective-permute-start.43) | collective-permute-done | bytes 1048608 | tf_op jit(solution)/shard_map/ppermute | solution.py:451
  1282.5 22.5 %collective-permute-done.42.refs_6_ = bf16[512,1024]{1,0:T(8,128)(2,1)} collective-permute-done((bf16[512,1024]{1,0:T(8,128)(2,1)S(1)}, bf16[512,1024]{1,0:T(8,128)(2,1)}, u32[]{:S(2)}, u32[]{:S(2)}) %collective-permute-start.42) | collective-permute-done | bytes 1048608 | tf_op jit(solution)/shard_map/ppermute | solution.py:451
  1304.9 43.1 %collective-permute-done.41.refs_5_ = bf16[512,1024]{1,0:T(8,128)(2,1)} collective-permute-done((bf16[512,1024]{1,0:T(8,128)(2,1)S(1)}, bf16[512,1024]{1,0:T(8,128)(2,1)}, u32[]{:S(2)}, u32[]{:S(2)}) %collective-permute-start.41) | collective-permute-done | bytes 1048608 | tf_op jit(solution)/shard_map/ppermute | solution.py:451
  1363.9 27.3 %collective-permute-done.44 = bf16[2560,256]{1,0:T(8,128)(2,1)} collective-permute-done((bf16[2560,256]{1,0:T(8,128)(2,1)}, bf16[2560,256]{1,0:T(8,128)(2,1)}, u32[]{:S(2)}, u32[]{:S(2)}) %collective-permute-start.44) | collective-permute-done | bytes 1310752 | tf_op jit(solution)/shard_map/ppermute | solution.py:620
  1407.5 46.2 %collective-permute-done.49.refs_3_ = bf16[512,1024]{1,0:T(8,128)(2,1)S(1)} collective-permute-done((bf16[512,1024]{1,0:T(8,128)(2,1)}, bf16[512,1024]{1,0:T(8,128)(2,1)S(1)}, u32[]{:S(2)}, u32[]{:S(2)}) %collective-permute-start.49) | collective-permute-done | bytes 1048608 | tf_op jit(solution)/shard_map/ppermute | solution.py:451
  1453.7 20.6 %collective-permute-done.48.refs_2_ = bf16[512,1024]{1,0:T(8,128)(2,1)} collective-permute-done((bf16[512,1024]{1,0:T(8,128)(2,1)S(1)}, bf16[512,1024]{1,0:T(8,128)(2,1)}, u32[]{:S(2)}, u32[]{:S(2)}) %collective-permute-start.48) | collective-permute-done | bytes 1048608 | tf_op jit(solution)/shard_map/ppermute | solution.py:451
  1544.6 36.4 %collective-permute-done.52.refs_4_ = bf16[512,1024]{1,0:T(8,128)(2,1)S(1)} collective-permute-done((bf16[512,1024]{1,0:T(8,128)(2,1)S(1)}, bf16[512,1024]{1,0:T(8,128)(2,1)S(1)}, u32[]{:S(2)}, u32[]{:S(2)}) %collective-permute-start.52) | collective-permute-done | bytes 1048608 | tf_op jit(solution)/shard_map/ppermute | solution.py:451
  1582.0 15.4 all-gather.27.cloned.1.call-done
  1607.6 11.9 collective-permute-done.53
  1638.3 21.4 %tree_backward.1 = (f32[2560,256]{1,0:T(8,128)}, f32[2560,256]{1,0:T(8,128)}, bf16[2560,256]{1,0:T(8,128)(2,1)S(1)}) custom-call(s32[1,20]{1,0:T(1,128)S(1)} %copy-done.18, bf16[2560,256]{1,0:T(8,128)(2,1)S(1)} %get-tuple-element.284.qr_ref, bf16[2560,256]{1,0:T(8,128)(2,1)S(1)} %copy-done.3, bf16[2560,256]{1,0:T(8,128)(2,1)} %get-tuple-element.286.vl_ref, ...), custom_call_target="tpu_custom_call" | custom-call | tf_op jit(solution)/shard_map/tree_backward/pallas_call | solution.py:333
  1663.9 14.4 collective-permute-start.57
  1730.3 12.6 convolution_convert_fusion.9
  1762.7 15.3 collective-permute-done.71
  1801.8 12.6 collective-permute-done.73
  (569 shorter events, 603.0 us)
Async XLA Ops:
  7.2 69.7 %all-gather.17.cloned.1.call-start = ((), (), s32[]{:S(2)}) async-start(), calls=%async_computation.5 | async-start | bytes 3932160 | tf_op jit(solution)/shard_map/all_gather | solution.py:657
  13.8 120.2 %all-gather.19.cloned.1.call-start = ((), (), s32[]{:S(2)}) async-start(), calls=%async_computation.6 | async-start | bytes 1310720 | tf_op jit(solution)/shard_map/all_gather | solution.py:660
  76.9 191.4 %reduce-scatter.6.cloned.1.call-start = ((), (), s32[]{:S(2)}) async-start(), calls=%async_computation.7 | async-start | bytes 11796480 | tf_op jit(solution)/shard_map/reduce_scatter | solution.py:682
  76.9 64.4 %collective-permute-start.8 = (bf16[2560,256]{1,0:T(8,128)(2,1)}, bf16[2560,256]{1,0:T(8,128)(2,1)}, u32[]{:S(2)}, u32[]{:S(2)}) collective-permute-start(bf16[2560,256]{1,0:T(8,128)(2,1)} %param.31), channel_id=1, source_target_pairs={{0,8},{8,16},{16,24},{1,9},{9,17},{17,25},{2,10},{10,18},{18,26},{... | collective-permute-start | bytes 3932168 | tf_op jit(solution)/shard_map/ppermute | solution.py:588
  79.6 61.8 %collective-permute-start.9 = (bf16[2560,256]{1,0:T(8,128)(2,1)}, bf16[2560,256]{1,0:T(8,128)(2,1)}, u32[]{:S(2)}, u32[]{:S(2)}) collective-permute-start(bf16[2560,256]{1,0:T(8,128)(2,1)} %param.31), channel_id=1, source_target_pairs={{8,0},{16,8},{24,16},{9,1},{17,9},{25,17},{10,2},{18,10},{26,18},{... | collective-permute-start | bytes 3932168 | tf_op jit(solution)/shard_map/ppermute | solution.py:589
  141.4 270.4 %all-gather.21.cloned.1.call-start = ((), (), s32[]{:S(2)}) async-start(), calls=%async_computation.8 | async-start | bytes 6553600 | tf_op jit(solution)/shard_map/all_gather | solution.py:695
  142.2 54.5 %collective-permute-start.17 = (s32[8,2560]{1,0:T(8,128)S(1)}, s32[8,2560]{1,0:T(8,128)S(1)}, u32[]{:S(2)}, u32[]{:S(2)}) collective-permute-start(s32[8,2560]{1,0:T(8,128)S(1)} %bitcast.128), channel_id=1, source_target_pairs={{0,24},{8,0},{16,8},{24,16},{1,25},{9,1},{17,9},{25,17},{2,26},{10... | collective-permute-start | bytes 245768 | tf_op jit(solution)/shard_map/ppermute | solution.py:451
  146.5 44.7 %collective-permute-start.16 = (s32[8,2560]{1,0:T(8,128)S(1)}, s32[8,2560]{1,0:T(8,128)S(1)}, u32[]{:S(2)}, u32[]{:S(2)}) collective-permute-start(s32[8,2560]{1,0:T(8,128)S(1)} %bitcast.129), channel_id=1, source_target_pairs={{0,16},{8,24},{16,0},{24,8},{1,17},{9,25},{17,1},{25,9},{2,18},{10... | collective-permute-start | bytes 245768 | tf_op jit(solution)/shard_map/ppermute | solution.py:451
  155.0 41.8 %collective-permute-start.20 = (f32[8,2560]{1,0:T(8,128)S(1)}, f32[8,2560]{1,0:T(8,128)S(1)}, u32[]{:S(2)}, u32[]{:S(2)}) collective-permute-start(f32[8,2560]{1,0:T(8,128)S(1)} %bitcast.134), channel_id=1, source_target_pairs={{0,24},{8,0},{16,8},{24,16},{1,25},{9,1},{17,9},{25,17},{2,26},{10... | collective-permute-start | bytes 245768 | tf_op jit(solution)/shard_map/ppermute | solution.py:451
  190.5 77.8 %collective-permute-start.12 = (bf16[512,2048]{1,0:T(8,128)(2,1)S(1)}, bf16[512,2048]{1,0:T(8,128)(2,1)}, u32[]{:S(2)}, u32[]{:S(2)}) collective-permute-start(bf16[512,2048]{1,0:T(8,128)(2,1)S(1)} %constant_dynamic-slice_fusion.37), channel_id=1, source_target_pairs={{0,8},{8,16},{16,24},{24,0},{1,9},{9,17},{17,25},{25,1},{2,10},{10... | collective-permute-start | bytes 6291464 | tf_op jit(solution)/shard_map/ppermute | solution.py:451
  192.4 70.9 %collective-permute-start.13 = (bf16[2560,256]{1,0:T(8,128)(2,1)S(1)}, bf16[2560,256]{1,0:T(8,128)(2,1)S(1)}, u32[]{:S(2)}, u32[]{:S(2)}) collective-permute-start(bf16[2560,256]{1,0:T(8,128)(2,1)S(1)} %collective-permute-done.10), channel_id=1, source_target_pairs={{0,8},{8,16},{16,24},{1,9},{9,17},{17,25},{2,10},{10,18},{18,26},{... | collective-permute-start | bytes 3932168 | tf_op jit(solution)/shard_map/ppermute | solution.py:588
  195.5 71.7 %collective-permute-start.14 = (bf16[2560,256]{1,0:T(8,128)(2,1)S(1)}, bf16[2560,256]{1,0:T(8,128)(2,1)S(1)}, u32[]{:S(2)}, u32[]{:S(2)}) collective-permute-start(bf16[2560,256]{1,0:T(8,128)(2,1)S(1)} %collective-permute-done.11), channel_id=1, source_target_pairs={{8,0},{16,8},{24,16},{9,1},{17,9},{25,17},{10,2},{18,10},{26,18},{... | collective-permute-start | bytes 3932168 | tf_op jit(solution)/shard_map/ppermute | solution.py:589
  271.7 345.5 %all-gather.23.cloned.1.call-start = ((), (), s32[]{:S(2)}) async-start(), calls=%async_computation.9 | async-start | bytes 47185920 | tf_op jit(solution)/shard_map/all_gather | solution.py:713
  288.2 107.3 %collective-permute-start.21 = (bf16[512,1024]{1,0:T(8,128)(2,1)S(1)}, bf16[512,1024]{1,0:T(8,128)(2,1)S(1)}, u32[]{:S(2)}, u32[]{:S(2)}) collective-permute-start(bf16[512,1024]{1,0:T(8,128)(2,1)S(1)} %constant_dynamic-slice_fusion.36), channel_id=1, source_target_pairs={{0,16},{8,24},{16,0},{24,8},{1,17},{9,25},{17,1},{25,9},{2,18},{10... | collective-permute-start | bytes 3145736 | tf_op jit(solution)/shard_map/ppermute | solution.py:451
  411.8 418.8 %all-gather.25.cloned.1.call-start = ((), (), s32[]{:S(2)}) async-start(), calls=%async_computation.10 | async-start | bytes 47185920 | tf_op jit(solution)/shard_map/all_gather | solution.py:722
  413.1 46.5 %collective-permute-start.22 = (bf16[512,1024]{1,0:T(8,128)(2,1)S(1)}, bf16[512,1024]{1,0:T(8,128)(2,1)}, u32[]{:S(2)}, u32[]{:S(2)}) collective-permute-start(bf16[512,1024]{1,0:T(8,128)(2,1)S(1)} %constant_dynamic-slice_fusion.35), channel_id=1, source_target_pairs={{0,16},{8,24},{16,0},{24,8},{1,17},{9,25},{17,1},{25,9},{2,18},{10... | collective-permute-start | bytes 3145736 | tf_op jit(solution)/shard_map/ppermute | solution.py:451
  461.5 47.6 %collective-permute-start.23 = (bf16[512,2048]{1,0:T(8,128)(2,1)S(1)}, bf16[512,2048]{1,0:T(8,128)(2,1)S(1)}, u32[]{:S(2)}, u32[]{:S(2)}) collective-permute-start(bf16[512,2048]{1,0:T(8,128)(2,1)S(1)} %constant_dynamic-slice_fusion.34), channel_id=1, source_target_pairs={{0,24},{8,0},{16,8},{24,16},{1,25},{9,1},{17,9},{25,17},{2,26},{10... | collective-permute-start | bytes 6291464 | tf_op jit(solution)/shard_map/ppermute | solution.py:451
  511.7 48.8 %collective-permute-start.24 = (bf16[512,2048]{1,0:T(8,128)(2,1)S(1)}, bf16[512,2048]{1,0:T(8,128)(2,1)}, u32[]{:S(2)}, u32[]{:S(2)}) collective-permute-start(bf16[512,2048]{1,0:T(8,128)(2,1)S(1)} %constant_dynamic-slice_fusion.33), channel_id=1, source_target_pairs={{0,8},{8,16},{16,24},{24,0},{1,9},{9,17},{17,25},{25,1},{2,10},{10... | collective-permute-start | bytes 6291464 | tf_op jit(solution)/shard_map/ppermute | solution.py:451
  561.8 45.1 %collective-permute-start.25 = (bf16[512,1024]{1,0:T(8,128)(2,1)S(1)}, bf16[512,1024]{1,0:T(8,128)(2,1)S(1)}, u32[]{:S(2)}, u32[]{:S(2)}) collective-permute-start(bf16[512,1024]{1,0:T(8,128)(2,1)S(1)} %constant_dynamic-slice_fusion.32), channel_id=1, source_target_pairs={{0,16},{8,24},{16,0},{24,8},{1,17},{9,25},{17,1},{25,9},{2,18},{10... | collective-permute-start | bytes 3145736 | tf_op jit(solution)/shard_map/ppermute | solution.py:451
  617.3 738.0 %reduce-scatter.8.cloned.1.call-start = ((), (), s32[]{:S(2)}) async-start(), calls=%async_computation.11 | async-start | bytes 47185920 | tf_op jit(solution)/shard_map/reduce_scatter | solution.py:780
  618.6 54.0 %collective-permute-start.26 = (bf16[512,1024]{1,0:T(8,128)(2,1)S(1)}, bf16[512,1024]{1,0:T(8,128)(2,1)S(1)}, u32[]{:S(2)}, u32[]{:S(2)}) collective-permute-start(bf16[512,1024]{1,0:T(8,128)(2,1)S(1)} %constant_dynamic-slice_fusion.31), channel_id=1, source_target_pairs={{0,16},{8,24},{16,0},{24,8},{1,17},{9,25},{17,1},{25,9},{2,18},{10... | collective-permute-start | bytes 3145736 | tf_op jit(solution)/shard_map/ppermute | solution.py:451
  674.7 47.9 %collective-permute-start.27 = (bf16[512,2048]{1,0:T(8,128)(2,1)S(1)}, bf16[512,2048]{1,0:T(8,128)(2,1)S(1)}, u32[]{:S(2)}, u32[]{:S(2)}) collective-permute-start(bf16[512,2048]{1,0:T(8,128)(2,1)S(1)} %constant_dynamic-slice_fusion.30), channel_id=1, source_target_pairs={{0,24},{8,0},{16,8},{24,16},{1,25},{9,1},{17,9},{25,17},{2,26},{10... | collective-permute-start | bytes 6291464 | tf_op jit(solution)/shard_map/ppermute | solution.py:451
  732.5 49.2 %collective-permute-start.28 = (bf16[512,2048]{1,0:T(8,128)(2,1)S(1)}, bf16[512,2048]{1,0:T(8,128)(2,1)S(1)}, u32[]{:S(2)}, u32[]{:S(2)}) collective-permute-start(bf16[512,2048]{1,0:T(8,128)(2,1)S(1)} %constant_dynamic-slice_fusion.29), channel_id=1, source_target_pairs={{0,8},{8,16},{16,24},{24,0},{1,9},{9,17},{17,25},{25,1},{2,10},{10... | collective-permute-start | bytes 6291464 | tf_op jit(solution)/shard_map/ppermute | solution.py:451
  784.4 46.2 %collective-permute-start.29 = (bf16[512,1024]{1,0:T(8,128)(2,1)S(1)}, bf16[512,1024]{1,0:T(8,128)(2,1)S(1)}, u32[]{:S(2)}, u32[]{:S(2)}) collective-permute-start(bf16[512,1024]{1,0:T(8,128)(2,1)S(1)} %constant_dynamic-slice_fusion.28), channel_id=1, source_target_pairs={{0,16},{8,24},{16,0},{24,8},{1,17},{9,25},{17,1},{25,9},{2,18},{10... | collective-permute-start | bytes 3145736 | tf_op jit(solution)/shard_map/ppermute | solution.py:451
  831.9 49.0 %collective-permute-start.30 = (bf16[512,1024]{1,0:T(8,128)(2,1)S(1)}, bf16[512,1024]{1,0:T(8,128)(2,1)S(1)}, u32[]{:S(2)}, u32[]{:S(2)}) collective-permute-start(bf16[512,1024]{1,0:T(8,128)(2,1)S(1)} %constant_dynamic-slice_fusion.27), channel_id=1, source_target_pairs={{0,16},{8,24},{16,0},{24,8},{1,17},{9,25},{17,1},{25,9},{2,18},{10... | collective-permute-start | bytes 3145736 | tf_op jit(solution)/shard_map/ppermute | solution.py:451
  882.9 48.3 %collective-permute-start.31 = (bf16[512,2048]{1,0:T(8,128)(2,1)S(1)}, bf16[512,2048]{1,0:T(8,128)(2,1)S(1)}, u32[]{:S(2)}, u32[]{:S(2)}) collective-permute-start(bf16[512,2048]{1,0:T(8,128)(2,1)S(1)} %constant_dynamic-slice_fusion.26), channel_id=1, source_target_pairs={{0,24},{8,0},{16,8},{24,16},{1,25},{9,1},{17,9},{25,17},{2,26},{10... | collective-permute-start | bytes 6291464 | tf_op jit(solution)/shard_map/ppermute | solution.py:451
  931.2 51.1 %collective-permute-start.32 = (bf16[512,1024]{1,0:T(8,128)(2,1)S(1)}, bf16[512,1024]{1,0:T(8,128)(2,1)S(1)}, u32[]{:S(2)}, u32[]{:S(2)}) collective-permute-start(bf16[512,1024]{1,0:T(8,128)(2,1)S(1)} %constant_dynamic-slice_fusion.25), channel_id=1, source_target_pairs={{0,16},{8,24},{16,0},{24,8},{1,17},{9,25},{17,1},{25,9},{2,18},{10... | collective-permute-start | bytes 3145736 | tf_op jit(solution)/shard_map/ppermute | solution.py:451
  984.3 46.1 %collective-permute-start.33 = (bf16[512,1024]{1,0:T(8,128)(2,1)S(1)}, bf16[512,1024]{1,0:T(8,128)(2,1)S(1)}, u32[]{:S(2)}, u32[]{:S(2)}) collective-permute-start(bf16[512,1024]{1,0:T(8,128)(2,1)S(1)} %constant_dynamic-slice_fusion.24), channel_id=1, source_target_pairs={{0,8},{8,16},{16,24},{24,0},{1,9},{9,17},{17,25},{25,1},{2,10},{10... | collective-permute-start | bytes 3145736 | tf_op jit(solution)/shard_map/ppermute | solution.py:451
  1031.6 79.3 %collective-permute-start.35 = (bf16[512,1024]{1,0:T(8,128)(2,1)}, bf16[512,1024]{1,0:T(8,128)(2,1)}, u32[]{:S(2)}, u32[]{:S(2)}) collective-permute-start(bf16[512,1024]{1,0:T(8,128)(2,1)} %constant_dynamic-slice_fusion.22), channel_id=1, source_target_pairs={{0,16},{8,24},{16,0},{24,8},{1,17},{9,25},{17,1},{25,9},{2,18},{10... | collective-permute-start | bytes 3145736 | tf_op jit(solution)/shard_map/ppermute | solution.py:451
  1111.0 418.3 %reduce-scatter.10.cloned.1.call-start = ((), (), s32[]{:S(2)}) async-start(), calls=%async_computation.12 | async-start | bytes 23592960 | tf_op jit(solution)/shard_map/reduce_scatter | solution.py:797
  1114.3 49.0 %collective-permute-start.37 = (bf16[512,1024]{1,0:T(8,128)(2,1)S(1)}, bf16[512,1024]{1,0:T(8,128)(2,1)S(1)}, u32[]{:S(2)}, u32[]{:S(2)}) collective-permute-start(bf16[512,1024]{1,0:T(8,128)(2,1)S(1)} %constant_dynamic-slice_fusion.20), channel_id=1, source_target_pairs={{0,24},{8,0},{16,8},{24,16},{1,25},{9,1},{17,9},{25,17},{2,26},{10... | collective-permute-start | bytes 3145736 | tf_op jit(solution)/shard_map/ppermute | solution.py:451
  1118.2 45.0 %collective-permute-start.36 = (bf16[512,1024]{1,0:T(8,128)(2,1)S(1)}, bf16[512,1024]{1,0:T(8,128)(2,1)S(1)}, u32[]{:S(2)}, u32[]{:S(2)}) collective-permute-start(bf16[512,1024]{1,0:T(8,128)(2,1)S(1)} %constant_dynamic-slice_fusion.21), channel_id=1, source_target_pairs={{0,24},{8,0},{16,8},{24,16},{1,25},{9,1},{17,9},{25,17},{2,26},{10... | collective-permute-start | bytes 3145736 | tf_op jit(solution)/shard_map/ppermute | solution.py:451
  1163.3 88.6 %collective-permute-start.40 = (bf16[512,1024]{1,0:T(8,128)(2,1)S(1)}, bf16[512,1024]{1,0:T(8,128)(2,1)S(1)}, u32[]{:S(2)}, u32[]{:S(2)}) collective-permute-start(bf16[512,1024]{1,0:T(8,128)(2,1)S(1)} %constant_dynamic-slice_fusion.17), channel_id=1, source_target_pairs={{0,16},{8,24},{16,0},{24,8},{1,17},{9,25},{17,1},{25,9},{2,18},{10... | collective-permute-start | bytes 3145736 | tf_op jit(solution)/shard_map/ppermute | solution.py:451
  1164.5 87.4 %collective-permute-start.39 = (bf16[512,1024]{1,0:T(8,128)(2,1)}, bf16[512,1024]{1,0:T(8,128)(2,1)}, u32[]{:S(2)}, u32[]{:S(2)}) collective-permute-start(bf16[512,1024]{1,0:T(8,128)(2,1)} %constant_dynamic-slice_fusion.18), channel_id=1, source_target_pairs={{0,8},{8,16},{16,24},{24,0},{1,9},{9,17},{17,25},{25,1},{2,10},{10... | collective-permute-start | bytes 3145736 | tf_op jit(solution)/shard_map/ppermute | solution.py:451
  1166.5 85.4 %collective-permute-start.38 = (bf16[512,1024]{1,0:T(8,128)(2,1)}, bf16[512,1024]{1,0:T(8,128)(2,1)}, u32[]{:S(2)}, u32[]{:S(2)}) collective-permute-start(bf16[512,1024]{1,0:T(8,128)(2,1)} %constant_dynamic-slice_fusion.19), channel_id=1, source_target_pairs={{0,8},{8,16},{16,24},{24,0},{1,9},{9,17},{17,25},{25,1},{2,10},{10... | collective-permute-start | bytes 3145736 | tf_op jit(solution)/shard_map/ppermute | solution.py:451
  1256.3 48.6 %collective-permute-start.42 = (bf16[512,1024]{1,0:T(8,128)(2,1)S(1)}, bf16[512,1024]{1,0:T(8,128)(2,1)}, u32[]{:S(2)}, u32[]{:S(2)}) collective-permute-start(bf16[512,1024]{1,0:T(8,128)(2,1)S(1)} %constant_dynamic-slice_fusion.15), channel_id=1, source_target_pairs={{0,24},{8,0},{16,8},{24,16},{1,25},{9,1},{17,9},{25,17},{2,26},{10... | collective-permute-start | bytes 3145736 | tf_op jit(solution)/shard_map/ppermute | solution.py:451
  1258.8 89.2 %collective-permute-start.41 = (bf16[512,1024]{1,0:T(8,128)(2,1)S(1)}, bf16[512,1024]{1,0:T(8,128)(2,1)}, u32[]{:S(2)}, u32[]{:S(2)}) collective-permute-start(bf16[512,1024]{1,0:T(8,128)(2,1)S(1)} %constant_dynamic-slice_fusion.16), channel_id=1, source_target_pairs={{0,16},{8,24},{16,0},{24,8},{1,17},{9,25},{17,1},{25,9},{2,18},{10... | collective-permute-start | bytes 3145736 | tf_op jit(solution)/shard_map/ppermute | solution.py:451
  1355.3 242.1 %all-gather.27.cloned.1.call-start = ((), (), s32[]{:S(2)}) async-start(), calls=%async_computation.13 | async-start | bytes 11796480 | tf_op jit(solution)/shard_map/all_gather | solution.py:814
  1395.4 78.9 %collective-permute-start.47 = (bf16[2560,256]{1,0:T(8,128)(2,1)}, bf16[2560,256]{1,0:T(8,128)(2,1)}, u32[]{:S(2)}, u32[]{:S(2)}) collective-permute-start(bf16[2560,256]{1,0:T(8,128)(2,1)} %get-tuple-element.346), channel_id=1, source_target_pairs={{24,16},{16,8},{25,17},{17,9},{26,18},{18,10},{27,19},{19,11},{28,... | collective-permute-start | bytes 3932168 | tf_op jit(solution)/shard_map/ppermute | solution.py:621
  1397.2 77.1 %collective-permute-start.46 = (bf16[2560,256]{1,0:T(8,128)(2,1)}, bf16[2560,256]{1,0:T(8,128)(2,1)}, u32[]{:S(2)}, u32[]{:S(2)}) collective-permute-start(bf16[2560,256]{1,0:T(8,128)(2,1)} %get-tuple-element.347), channel_id=1, source_target_pairs={{0,8},{8,16},{1,9},{9,17},{2,10},{10,18},{3,11},{11,19},{4,12},{12... | collective-permute-start | bytes 3932168 | tf_op jit(solution)/shard_map/ppermute | solution.py:620
  1405.8 47.9 %collective-permute-start.49 = (bf16[512,1024]{1,0:T(8,128)(2,1)}, bf16[512,1024]{1,0:T(8,128)(2,1)S(1)}, u32[]{:S(2)}, u32[]{:S(2)}) collective-permute-start(bf16[512,1024]{1,0:T(8,128)(2,1)} %constant_dynamic-slice_fusion.10), channel_id=1, source_target_pairs={{0,8},{8,16},{16,24},{24,0},{1,9},{9,17},{17,25},{25,1},{2,10},{10... | collective-permute-start | bytes 3145736 | tf_op jit(solution)/shard_map/ppermute | solution.py:451
  1407.4 66.9 %collective-permute-start.48 = (bf16[512,1024]{1,0:T(8,128)(2,1)S(1)}, bf16[512,1024]{1,0:T(8,128)(2,1)}, u32[]{:S(2)}, u32[]{:S(2)}) collective-permute-start(bf16[512,1024]{1,0:T(8,128)(2,1)S(1)} %constant_dynamic-slice_fusion.11), channel_id=1, source_target_pairs={{0,8},{8,16},{16,24},{24,0},{1,9},{9,17},{17,25},{25,1},{2,10},{10... | collective-permute-start | bytes 3145736 | tf_op jit(solution)/shard_map/ppermute | solution.py:451
  1529.3 219.9 %reduce-scatter.12.cloned.1.call-start = ((), (), s32[]{:S(2)}) async-start(), calls=%async_computation.14 | async-start | bytes 23592960 | tf_op jit(solution)/shard_map/reduce_scatter | solution.py:816
  1530.7 50.3 %collective-permute-start.52 = (bf16[512,1024]{1,0:T(8,128)(2,1)S(1)}, bf16[512,1024]{1,0:T(8,128)(2,1)S(1)}, u32[]{:S(2)}, u32[]{:S(2)}) collective-permute-start(bf16[512,1024]{1,0:T(8,128)(2,1)S(1)} %constant_dynamic-slice_fusion.9), channel_id=1, source_target_pairs={{0,16},{8,24},{16,0},{24,8},{1,17},{9,25},{17,1},{25,9},{2,18},{10... | collective-permute-start | bytes 3145736 | tf_op jit(solution)/shard_map/ppermute | solution.py:451
  1597.4 257.4 %reduce-scatter.14.cloned.1.call-start = ((), (), s32[]{:S(2)}) async-start(), calls=%async_computation.15 | async-start | bytes 11796480 | tf_op jit(solution)/shard_map/reduce_scatter | solution.py:853
  1607.3 87.9 %collective-permute-start.59 = (bf16[512,1024]{1,0:T(8,128)(2,1)}, bf16[512,1024]{1,0:T(8,128)(2,1)}, u32[]{:S(2)}, u32[]{:S(2)}) collective-permute-start(bf16[512,1024]{1,0:T(8,128)(2,1)} %constant_dynamic-slice_fusion.6), channel_id=1, source_target_pairs={{0,16},{8,24},{16,0},{24,8},{1,17},{9,25},{17,1},{25,9},{2,18},{10... | collective-permute-start | bytes 3145736 | tf_op jit(solution)/shard_map/ppermute | solution.py:451
  1697.5 51.7 %collective-permute-start.61 = (bf16[512,1024]{1,0:T(8,128)(2,1)}, bf16[512,1024]{1,0:T(8,128)(2,1)}, u32[]{:S(2)}, u32[]{:S(2)}) collective-permute-start(bf16[512,1024]{1,0:T(8,128)(2,1)} %constant_dynamic-slice_fusion.4), channel_id=1, source_target_pairs={{0,24},{8,0},{16,8},{24,16},{1,25},{9,1},{17,9},{25,17},{2,26},{10... | collective-permute-start | bytes 3145736 | tf_op jit(solution)/shard_map/ppermute | solution.py:451
  1702.3 46.9 %collective-permute-start.60 = (bf16[512,1024]{1,0:T(8,128)(2,1)}, bf16[512,1024]{1,0:T(8,128)(2,1)}, u32[]{:S(2)}, u32[]{:S(2)}) collective-permute-start(bf16[512,1024]{1,0:T(8,128)(2,1)} %constant_dynamic-slice_fusion.5), channel_id=1, source_target_pairs={{0,24},{8,0},{16,8},{24,16},{1,25},{9,1},{17,9},{25,17},{2,26},{10... | collective-permute-start | bytes 3145736 | tf_op jit(solution)/shard_map/ppermute | solution.py:451
  (138 other events, 2811.1 us)
Sparse Core Ops, SparseCore 0:
  13.9 62.8 all-gather.16
  78.4 40.6 all-gather.18
  141.5 82.4 reduce-scatter.5
  271.8 139.8 all-gather.20
  413.5 203.7 all-gather.22
  619.0 205.4 all-gather.24
  1111.1 244.1 reduce-scatter.7
  1359.3 136.1 reduce-scatter.9
  1529.4 67.9 all-gather.26
  1601.3 136.6 reduce-scatter.11
  1749.3 79.1 reduce-scatter.13
